TPU v7x, 32 devices: a whole 2x2x4 slice. The times are simulated.
32 devices in a mesh: dp: 8 (over z, y), seq: 4 (over x, core).
Axes of the slice: x: 2, y: 2, z: 4, core: 2. Of those that a mesh axis runs over, the one named last changes fastest.
Arguments:
- tokens: bfloat16 [16, 1024, 1024], P('dp', 'seq'), may hold values from -6 to 6
- bins: int32 [16], P('dp'), may hold values from 0 to 127
- plan: float32 [128], replicated, may hold values from 1 to 300
- w_qkv: bfloat16 [1024, 3072], P('dp', 'seq'), may hold values from -0.1875 to 0.1875
- w_out: bfloat16 [1024, 1024], P('seq', 'dp'), may hold values from -1.5 to 1.5
- w_up: bfloat16 [1024, 4096], P('dp', 'seq'), may hold values from -0.1875 to 0.1875
- w_down: bfloat16 [4096, 1024], P('seq', 'dp'), may hold values from -0.09375 to 0.09375
- w_time: bfloat16 [256, 2048], P(('dp', 'seq')), may hold values from -0.1875 to 0.1875
- cotangent: bfloat16 [16, 1024, 1024], P('dp', 'seq'), may hold values from -6 to 6
Outputs:
- output: bfloat16 [16, 1024, 1024], P('dp', 'seq')
- grad_tokens: bfloat16 [16, 1024, 1024], P('dp', 'seq')
- grad_qkv: float32 [1024, 3072], P('dp', 'seq')
- grad_out: float32 [1024, 1024], P('seq', 'dp')
- grad_up: float32 [1024, 4096], P('dp', 'seq')
- grad_down: float32 [4096, 1024], P('seq', 'dp')
- grad_time: float32 [256, 2048], P(('dp', 'seq'))
All inputs are finite; a program needn't handle non-finite values.
Results may differ from a plain program's by a relative error of at most 0.02.
Values may be sent and summed in bfloat16 or wider, within the bound.
A program may use at most 192 MiB of HBM per device.

v0:
```python
import math

import jax
import jax.numpy as jnp
from jax import lax
from jax.sharding import PartitionSpec as P

D = 1024
HD = 64
TF = 256
LEN = 1024


EPSILON = 1e-05
HIGHEST = lax.Precision.HIGHEST
ROOT_HALF = 0.7071067811865476
DENSITY = 0.3989422804014327


def time_features(plan, bins):
    table = jnp.arange(plan.shape[0], dtype=jnp.int32)
    picked = jnp.where(bins[:, None] == table[None, :], plan[None, :], 0.0)
    sigma = jnp.sum(picked, axis=1)
    level = 0.25 * jnp.log(sigma)
    count = TF // 2
    freqs = jnp.exp(jnp.arange(count, dtype=jnp.float32) * (math.log(1000.0) / count))
    angles = level[:, None] * freqs[None, :]
    return jnp.concatenate([jnp.sin(angles), jnp.cos(angles)], axis=1)


def normalize(field):
    centered = field - jnp.mean(field, axis=-1, keepdims=True)
    spread = jnp.mean(centered * centered, axis=-1, keepdims=True)
    inverse = lax.rsqrt(spread + EPSILON)
    return (centered * inverse, inverse)


def norm_backward(grad_scaled, normed, inverse, scale):
    grad_normed = grad_scaled * scale
    grad_scale = jnp.sum(grad_scaled * normed, axis=1)
    inner = jnp.mean(grad_normed * normed, axis=-1, keepdims=True)
    grad_field = inverse * (
        grad_normed - jnp.mean(grad_normed, axis=-1, keepdims=True) - normed * inner
    )
    return (grad_field, grad_scale)


def rotate(field, cosine, sine):
    half = HD // 2
    first = field[..., :half]
    second = field[..., half:]
    return jnp.concatenate(
        [first * cosine - second * sine, second * cosine + first * sine], axis=-1
    )


def rotary_tables(places):
    half = HD // 2
    inverse = jnp.exp(jnp.arange(half, dtype=jnp.float32) * (-math.log(10000.0) / half))
    angle = places[:, None] * inverse[None, :]
    return (jnp.cos(angle)[:, None, None, :], jnp.sin(angle)[:, None, None, :])


def pack_heads(h_one, qkv_weight, cosine, sine):
    seqs, rows, width = h_one.shape
    raw = jnp.einsum("std,de->ste", h_one, qkv_weight, preferred_element_type=jnp.float32)
    local_heads = qkv_weight.shape[1] // (3 * HD)
    raw = raw.reshape(seqs, rows, local_heads, 3, HD)
    turned = rotate(raw[:, :, :, 0:2], cosine, sine)
    packed = jnp.concatenate([turned, raw[:, :, :, 2:3]], axis=3).astype(jnp.bfloat16)
    return packed.reshape(seqs, rows, local_heads * 3 * HD)


def unpack_grads(grad_packed, cosine, sine):
    seqs, rows, width = grad_packed.shape
    local_heads = width // (3 * HD)
    grad_fields = grad_packed.reshape(seqs, rows, local_heads, 3, HD).astype(jnp.float32)
    unturned = rotate(grad_fields[:, :, :, 0:2], cosine, -sine)
    grad_raw = jnp.concatenate([unturned, grad_fields[:, :, :, 2:3]], axis=3).astype(jnp.bfloat16)
    return grad_raw.reshape(seqs, rows, width)


def gelu_slope(upper):
    return 0.5 * (1.0 + lax.erf(upper * ROOT_HALF)) + upper * DENSITY * jnp.exp(
        -0.5 * upper * upper
    )


def attend_sequence(fields):
    local_heads = fields.shape[1]
    block = min(512, LEN)
    count = LEN // block
    keys = fields[:, :, 1]
    values = fields[:, :, 2]
    query_blocks = fields[:, :, 0].reshape(count, block, local_heads, HD)

    def attend_one_block(query_blk):
        scores = jnp.einsum(
            "qhd,khd->hqk", query_blk, keys, preferred_element_type=jnp.float32
        ) * HD ** (-0.5)
        top = jnp.max(scores, axis=-1, keepdims=True)
        expo = jnp.exp(scores - top)
        totals = jnp.sum(expo, axis=-1, keepdims=True)
        probs = (expo / totals).astype(jnp.bfloat16)
        result = jnp.einsum("hqk,khd->qhd", probs, values, preferred_element_type=jnp.float32)
        return (result.astype(jnp.bfloat16), (top + jnp.log(totals))[:, :, 0])

    results, logsums = lax.map(attend_one_block, query_blocks)
    logsums = jnp.transpose(logsums, (1, 0, 2)).reshape(local_heads, LEN)
    return (results.reshape(LEN, local_heads, HD), logsums)


def attend_all(packed_heads):
    items = packed_heads.shape[0]
    local_heads = packed_heads.shape[2] // (3 * HD)
    fields = packed_heads.reshape(items, LEN, local_heads, 3, HD)
    results, logsums = lax.map(attend_sequence, fields)
    return (results.reshape(items, LEN, local_heads * HD), logsums)


def back_sequence(pieces):
    fields, logsums, grad_heads = pieces
    local_heads = fields.shape[1]
    block = min(512, LEN)
    count = LEN // block
    keys = fields[:, :, 1]
    values = fields[:, :, 2]
    query_blocks = fields[:, :, 0].reshape(count, block, local_heads, HD)
    grad_blocks = grad_heads.reshape(count, block, local_heads, HD)
    sum_blocks = jnp.transpose(logsums.reshape(local_heads, count, block), (1, 0, 2))

    def back_one_block(carry, piece):
        key_acc, value_acc = carry
        query_blk, grad_blk, sum_blk = piece
        scores = jnp.einsum(
            "qhd,khd->hqk", query_blk, keys, preferred_element_type=jnp.float32
        ) * HD ** (-0.5)
        probs = jnp.exp(scores - sum_blk[:, :, None])
        grad_probs = jnp.einsum(
            "qhd,khd->hqk", grad_blk, values, preferred_element_type=jnp.float32
        )
        inner = jnp.sum(probs * grad_probs, axis=-1, keepdims=True)
        grad_scores = (probs * (grad_probs - inner)).astype(jnp.bfloat16)
        grad_query = jnp.einsum(
            "hqk,khd->qhd", grad_scores, keys, preferred_element_type=jnp.float32
        ) * HD ** (-0.5)
        key_acc = key_acc + jnp.einsum(
            "hqk,qhd->khd", grad_scores, query_blk, preferred_element_type=jnp.float32
        ) * HD ** (-0.5)
        value_acc = value_acc + jnp.einsum(
            "hqk,qhd->khd", probs.astype(jnp.bfloat16), grad_blk, preferred_element_type=jnp.float32
        )
        return ((key_acc, value_acc), grad_query)

    empty = jnp.zeros((LEN, local_heads, HD), jnp.float32)
    (grad_keys, grad_values), grad_queries = lax.scan(
        back_one_block, (empty, empty), (query_blocks, grad_blocks, sum_blocks)
    )
    grad_queries = grad_queries.reshape(LEN, local_heads, HD)
    return jnp.stack([grad_queries, grad_keys, grad_values], axis=2).astype(jnp.bfloat16)


def back_all(packed_heads, logsums, grad_heads):
    items = packed_heads.shape[0]
    local_heads = packed_heads.shape[2] // (3 * HD)
    fields = packed_heads.reshape(items, LEN, local_heads, 3, HD)
    grads = grad_heads.reshape(items, LEN, local_heads, HD)
    result = lax.map(back_sequence, (fields, logsums, grads))
    return result.reshape(items, LEN, local_heads * 3 * HD)


def data_layer(
    tokens, cotangent, w_qkv, w_up, w_out, w_down, scale_one, scale_two, norm_one, inverse_one
):
    seqs, local_len, width = tokens.shape
    wide = (
        lax.all_gather(w_qkv, "seq", axis=1, tiled=True),
        lax.all_gather(w_up, "seq", axis=1, tiled=True),
        lax.all_gather(w_out, "seq", axis=0, tiled=True),
        lax.all_gather(w_down, "seq", axis=0, tiled=True),
    )
    full_qkv, full_up, full_out, full_down = (
        lax.all_gather(wide[0], "dp", axis=0, tiled=True),
        lax.all_gather(wide[1], "dp", axis=0, tiled=True),
        lax.all_gather(wide[2], "dp", axis=1, tiled=True),
        lax.all_gather(wide[3], "dp", axis=1, tiled=True),
    )
    field = tokens.astype(jnp.float32)
    h_one = (norm_one * scale_one).astype(jnp.bfloat16)
    places = (lax.axis_index("seq") * local_len + jnp.arange(local_len, dtype=jnp.int32)).astype(
        jnp.float32
    )
    cosine, sine = rotary_tables(places)
    packed = pack_heads(h_one, full_qkv, cosine, sine)
    packed_heads = lax.all_to_all(packed, "seq", split_axis=2, concat_axis=1, tiled=True)
    results, logsums = attend_all(packed_heads)
    back_tokens = lax.all_to_all(results, "seq", split_axis=1, concat_axis=2, tiled=True)
    middle = field + jnp.einsum(
        "std,de->ste", back_tokens, full_out, preferred_element_type=jnp.float32
    )
    norm_two, inverse_two = normalize(middle)
    h_two = (norm_two * scale_two).astype(jnp.bfloat16)
    upper = jnp.einsum("std,df->stf", h_two, full_up, preferred_element_type=jnp.float32)
    active = jax.nn.gelu(upper, approximate=False).astype(jnp.bfloat16)
    output = (
        middle + jnp.einsum("stf,fd->std", active, full_down, preferred_element_type=jnp.float32)
    ).astype(jnp.bfloat16)
    grad_down = jnp.einsum("stf,std->fd", active, cotangent, preferred_element_type=jnp.float32)
    grad_active = jnp.einsum(
        "std,fd->stf", cotangent, full_down, preferred_element_type=jnp.float32
    )
    grad_upper = (grad_active * gelu_slope(upper)).astype(jnp.bfloat16)
    grad_up = jnp.einsum("std,stf->df", h_two, grad_upper, preferred_element_type=jnp.float32)
    grad_htwo = jnp.einsum("stf,df->std", grad_upper, full_up, preferred_element_type=jnp.float32)
    grad_middle, grad_scale_two = norm_backward(grad_htwo, norm_two, inverse_two, scale_two)
    grad_middle = grad_middle + cotangent.astype(jnp.float32)
    grad_branch = grad_middle.astype(jnp.bfloat16)
    grad_out = jnp.einsum(
        "std,ste->de", back_tokens, grad_branch, preferred_element_type=jnp.float32
    )
    grad_attended = jnp.einsum(
        "ste,de->std", grad_branch, full_out, preferred_element_type=jnp.float32
    ).astype(jnp.bfloat16)
    grad_heads = lax.all_to_all(grad_attended, "seq", split_axis=2, concat_axis=1, tiled=True)
    grad_packed_heads = back_all(packed_heads, logsums, grad_heads)
    grad_packed = lax.all_to_all(grad_packed_heads, "seq", split_axis=1, concat_axis=2, tiled=True)
    grad_raw = unpack_grads(grad_packed, cosine, sine)
    grad_qkv = jnp.einsum("std,ste->de", h_one, grad_raw, preferred_element_type=jnp.float32)
    grad_hone = jnp.einsum("ste,de->std", grad_raw, full_qkv, preferred_element_type=jnp.float32)
    grad_field, grad_scale_one = norm_backward(grad_hone, norm_one, inverse_one, scale_one)
    grad_tokens = (grad_middle + grad_field).astype(jnp.bfloat16)
    partial_sums = (
        lax.psum_scatter(
            grad_qkv.astype(jnp.bfloat16), "dp", scatter_dimension=0, tiled=True
        ).astype(jnp.float32),
        lax.psum_scatter(
            grad_up.astype(jnp.bfloat16), "dp", scatter_dimension=0, tiled=True
        ).astype(jnp.float32),
        lax.psum_scatter(
            grad_out.astype(jnp.bfloat16), "dp", scatter_dimension=1, tiled=True
        ).astype(jnp.float32),
        lax.psum_scatter(
            grad_down.astype(jnp.bfloat16), "dp", scatter_dimension=1, tiled=True
        ).astype(jnp.float32),
    )
    sums = (
        lax.psum_scatter(
            partial_sums[0].astype(jnp.bfloat16), "seq", scatter_dimension=1, tiled=True
        ).astype(jnp.float32),
        lax.psum_scatter(
            partial_sums[1].astype(jnp.bfloat16), "seq", scatter_dimension=1, tiled=True
        ).astype(jnp.float32),
        lax.psum_scatter(
            partial_sums[2].astype(jnp.bfloat16), "seq", scatter_dimension=0, tiled=True
        ).astype(jnp.float32),
        lax.psum_scatter(
            partial_sums[3].astype(jnp.bfloat16), "seq", scatter_dimension=0, tiled=True
        ).astype(jnp.float32),
    )
    return (output, grad_tokens, grad_scale_one, grad_scale_two, sums)


def shards(tokens, bins, plan, w_qkv, w_out, w_up, w_down, w_time, cotangent):
    feats = time_features(plan, bins).astype(jnp.bfloat16)
    full_time = lax.all_gather(w_time, ("dp", "seq"), axis=0, tiled=True)
    modul = jnp.dot(feats, full_time, preferred_element_type=jnp.float32)
    scale_one = 1.0 + modul[:, None, :D]
    scale_two = 1.0 + modul[:, None, D:]
    norm_one, inverse_one = normalize(tokens.astype(jnp.float32))
    output, grad_tokens, grad_scale_one, grad_scale_two, sums = data_layer(
        tokens, cotangent, w_qkv, w_up, w_out, w_down, scale_one, scale_two, norm_one, inverse_one
    )
    grad_scales = jnp.concatenate([grad_scale_one, grad_scale_two], axis=1)
    grad_time = jnp.dot(feats.astype(jnp.float32).T, grad_scales, precision=HIGHEST)
    time_sum = lax.psum_scatter(grad_time, ("dp", "seq"), scatter_dimension=0, tiled=True)
    return (output, grad_tokens, sums[0], sums[2], sums[1], sums[3], time_sum)


def solution(mesh):
    return jax.shard_map(
        shards,
        mesh=mesh,
        in_specs=(
            P("dp", "seq", None),
            P("dp"),
            P(),
            P("dp", "seq"),
            P("seq", "dp"),
            P("dp", "seq"),
            P("seq", "dp"),
            P(("dp", "seq"), None),
            P("dp", "seq", None),
        ),
        out_specs=(
            P("dp", "seq", None),
            P("dp", "seq", None),
            P("dp", "seq"),
            P("seq", "dp"),
            P("dp", "seq"),
            P("seq", "dp"),
            P(("dp", "seq"), None),
        ),
        check_vma=False,
    )
```

profile of v0, /device:TPU:0, one launch (start us, length us, event | category | flops | bytes accessed | tf_op | source)
XLA Modules:
  0.0 1374.7 jit_solution(13455809357310904896)
XLA Ops:
  8.7 11.7 all_gather.28
  21.1 8.3 all_gather.30
  35.4 51.6 %all-gather.8.cloned.1.call-done = bf16[256,2048]{1,0:T(8,128)(2,1)} async-done(((bf16[8,2048]{1,0:T(8,128)(2,1)}), bf16[256,2048]{1,0:T(8,128)(2,1)}) %all-gather.8.cloned.1.call-update) | async-done | bytes 1048592 | tf_op jit(solution)/shard_map/all_gather | solution.py:265
  89.1 98.1 %all-gather.10.cloned.1.call-done = bf16[1024,3072]{1,0:T(8,128)(2,1)} async-done(((bf16[128,3072]{1,0:T(8,128)(2,1)}), bf16[1024,3072]{1,0:T(8,128)(2,1)}) %all-gather.10.cloned.1.call-update) | async-done | bytes 6291472 | tf_op jit(solution)/shard_map/all_gather | solution.py:183
  194.4 20.6 %copy.77 = bf16[2,256,3072]{1,0,2:T(2,128)(2,1)} copy(bf16[2,256,3072]{1,2,0:T(8,128)(2,1)S(1)} %bitcast.227) | data formatting | bytes 6291456 | tf_op jit(solution)/shard_map/convert_element_type | solution.py:70
  219.5 36.1 %all-to-all-done = bf16[2,256,3072]{1,0,2:T(2,128)(2,1)S(1)} async-done(((bf16[2,256,3072]{1,0,2:T(2,128)(2,1)}), bf16[2,256,3072]{1,0,2:T(2,128)(2,1)S(1)}, u32[]{:S(2)}, u32[]{:S(2)}) %all-to-all-start) | async-done | bytes 3145760 | tf_op jit(solution)/shard_map/all_to_all | solution.py:195
  266.5 30.3 %while.50 = (s32[]{:T(128)}, bf16[2,1024,4,64]{1,3,2,0:T(8,128)(2,1)}, f32[2,4,1024]{2,1,0:T(4,128)S(1)}, bf16[2,1024,4,3,64]{1,4,2,3,0:T(8,128)(2,1)}, s32[]{:T(128)}, /*index=5*/s32[]{:T(128)}, s32[]{:T(128)}) while((s32[]{:T(128)}, bf16[2,1024,4,64]{1,3,2,0:T(8,128)(2,1)}, f32[2,4,1024]{2,1,0:T(4,128)S(1)}, ...), condition=%wide.region_8.9_spmd, body=%wide.region_3.8_spmd.sunk | while | flops 555874304 | bytes 38371584 | solution.py:117
  268.7 10.8 while.53
  283.9 10.8 while.53
  299.5 17.1 %all_to_all.57 = bf16[2,1024,256]{2,0,1:T(2,128)(2,1)S(1)} all-to-all(bf16[2,1024,256]{2,0,1:T(2,128)(2,1)S(1)} %copy.81), channel_id=1, replica_groups=mesh['dp'=8,'seq'=4] {'seq'}, dimensions={1} | all-to-all | bytes 2097152 | tf_op jit(solution)/shard_map/all_to_all | solution.py:197
  321.5 60.0 %all-gather.16.cloned.1.call-done = bf16[1024,4096]{1,0:T(8,128)(2,1)} async-done(((bf16[128,4096]{1,0:T(8,128)(2,1)}), bf16[1024,4096]{1,0:T(8,128)(2,1)}) %all-gather.16.cloned.1.call-update) | async-done | bytes 8388624 | tf_op jit(solution)/shard_map/all_gather | solution.py:184
  381.5 14.4 %fusion.87 = (u8[256,4096]{1,0:T(8,128)(4,1)}, u8[256,4096]{1,0:T(8,128)(4,1)}, f32[2,256,4096]{2,1,0:T(8,128)}) fusion(bf16[1024,4096]{1,0:T(8,128)(2,1)} %all-gather.16.cloned.1.call-done, f32[2,256,1024]{2,1,0:T(8,128)S(1)} %get-tuple-element.324, f32[2,1024]{1,0:T(2,128)S(1)} %copy-done.24, f32[2,256]{1,0:T(2,128)S(1)} %add_rsqrt_fusion, ...), kind=kOutput, calls=%fused_computation.139 | convolution fusion | flops 4322230272 | bytes 20983808 | tf_op jit(solution)/shard_map/std,df->stf/dot_general | solution.py:203
  395.9 111.2 %all-gather.20.cloned.1.call-done = bf16[4096,1024]{1,0:T(8,128)(2,1)} async-done(((bf16[4096,128]{1,0:T(8,128)(2,1)}), bf16[4096,1024]{1,0:T(8,128)(2,1)}) %all-gather.20.cloned.1.call-update) | async-done | bytes 8388624 | tf_op jit(solution)/shard_map/all_gather | solution.py:186
  507.1 10.7 fusion.47
  549.7 94.8 %while.52 = (s32[]{:T(128)}, bf16[2,1024,4,3,64]{1,4,3,2,0:T(8,128)(2,1)}, bf16[2,1024,4,3,64]{1,4,2,3,0:T(8,128)(2,1)}, bf16[2,1024,4,64]{1,3,2,0:T(8,128)(2,1)...) while((s32[]{:T(128)}, bf16[2,1024,4,3,64]{1,4,3,2,0:T(8,128)(2,1)}, ...), condition=%wide.region_17.18_spmd, body=%wide.region_13.17_spmd.sunk | while | flops 1370880000 | bytes 180445744 | solution.py:168
  558.1 35.7 %while.54 = (s32[]{:T(128)}, f32[1024,4,64]{0,2,1:T(8,128)S(1)}, f32[1024,4,64]{0,2,1:T(8,128)S(1)}, bf16[2,512,4,64]{1,3,2,0:T(8,128)(2,1)}, bf16[2,512,4,64]{1...) while((s32[]{:T(128)}, f32[1024,4,64]{0,2,1:T(8,128)S(1)}, ...), condition=%wide.region_16.16_spmd.clone, body=%wide.region_14.15_spmd.clone.sunk | while | flops 1368782848 | bytes 160489808 | solution.py:156
  605.6 35.5 %while.54 = (s32[]{:T(128)}, f32[1024,4,64]{0,2,1:T(8,128)S(1)}, f32[1024,4,64]{0,2,1:T(8,128)S(1)}, bf16[2,512,4,64]{1,3,2,0:T(8,128)(2,1)}, bf16[2,512,4,64]{1...) while((s32[]{:T(128)}, f32[1024,4,64]{0,2,1:T(8,128)S(1)}, ...), condition=%wide.region_16.16_spmd.clone, body=%wide.region_14.15_spmd.clone.sunk | while | flops 1368782848 | bytes 160489808 | solution.py:156
  644.6 7.6 copy.88
  652.2 39.6 %all_to_all.58 = bf16[2,1024,768]{2,0,1:T(2,128)(2,1)S(1)} all-to-all(bf16[2,1024,768]{2,0,1:T(2,128)(2,1)S(1)} %copy.88), channel_id=1, replica_groups=mesh['dp'=8,'seq'=4] {'seq'}, dimensions={1} | all-to-all | bytes 6291456 | tf_op jit(solution)/shard_map/all_to_all | solution.py:226
  708.4 9.2 bitcast_convert_fusion.1
  717.7 20.4 %fusion.42 = bf16[2,256,4096]{2,1,0:T(8,128)(2,1)S(1)} fusion(f32[2,256,4096]{2,1,0:T(8,128)} %get-tuple-element.325, u8[256,4096]{1,0:T(8,128)(4,1)} %get-tuple-element.245, u8[256,4096]{1,0:T(8,128)(4,1)} %get-tuple-element.244), kind=kLoop, calls=%fused_computation.66 | loop fusion | flops 146800640 | bytes 14680064 | tf_op jit(solution)/shard_map/convert_element_type | solution.py:204
  740.2 6.8 bitcast_convert_fusion
  746.9 11.6 copy.106
  760.5 61.7 %reduce-scatter.14.cloned.1.call-done = bf16[128,3072]{1,0:T(8,128)(2,1)} async-done(((bf16[1024,3072]{1,0:T(8,128)(2,1)}), bf16[128,3072]{1,0:T(8,128)(2,1)}) %reduce-scatter.14.cloned.1.call-update) | async-done | bytes 786448 | tf_op jit(solution)/shard_map/reduce_scatter | solution.py:233
  822.3 151.6 %reduce-scatter.20.cloned.1.call-done = bf16[128,4096]{1,0:T(8,128)(2,1)} async-done(((bf16[1024,4096]{1,0:T(8,128)(2,1)}), bf16[128,4096]{1,0:T(8,128)(2,1)}) %reduce-scatter.20.cloned.1.call-update) | async-done | bytes 1048592 | tf_op jit(solution)/shard_map/reduce_scatter | solution.py:236
  974.0 152.0 %reduce-scatter.30.cloned.1.call-done = bf16[128,4096]{1,0:T(8,128)(2,1)} async-done(((bf16[1024,4096]{1,0:T(8,128)(2,1)}), bf16[128,4096]{1,0:T(8,128)(2,1)}) %reduce-scatter.30.cloned.1.call-update) | async-done | bytes 1048592
  1128.7 9.0 fusion.80
  1140.1 10.3 add_convert_fusion.1
  1153.7 20.3 %reduce-scatter.16.cloned.1.call-done = bf16[128,768]{1,0:T(8,128)(2,1)} async-done(((bf16[128,3072]{1,0:T(8,128)(2,1)}), bf16[128,768]{1,0:T(8,128)(2,1)}) %reduce-scatter.16.cloned.1.call-update) | async-done | bytes 196624 | tf_op jit(solution)/shard_map/reduce_scatter | solution.py:247
  1175.7 25.6 %reduce-scatter.22.cloned.1.call-done = bf16[128,1024]{1,0:T(8,128)(2,1)} async-done(((bf16[128,4096]{1,0:T(8,128)(2,1)}), bf16[128,1024]{1,0:T(8,128)(2,1)}) %reduce-scatter.22.cloned.1.call-update) | async-done | bytes 262160 | tf_op jit(solution)/shard_map/reduce_scatter | solution.py:250
  1203.1 25.7 %reduce-scatter.24.cloned.1.call-done = bf16[1024,128]{1,0:T(8,128)(2,1)} async-done(((bf16[4096,128]{1,0:T(8,128)(2,1)}), bf16[1024,128]{1,0:T(8,128)(2,1)}) %reduce-scatter.24.cloned.1.call-update) | async-done | bytes 262160 | tf_op jit(solution)/shard_map/reduce_scatter | solution.py:256
  1230.5 137.2 %reduce-scatter.26.cloned.1.call-done = f32[8,2048]{1,0:T(8,128)} async-done(((f32[256,2048]{1,0:T(8,128)}), f32[8,2048]{1,0:T(8,128)}) %reduce-scatter.26.cloned.1.call-update) | async-done | bytes 65552 | tf_op jit(solution)/shard_map/reduce_scatter | solution.py:275
  (310 shorter events, 230.3 us)
Async XLA Ops:
  7.2 180.0 %copy-start.6 = (bf16[2,256,1024]{2,1,0:T(8,128)(2,1)S(1)}, bf16[2,256,1024]{2,1,0:T(8,128)(2,1)}, u32[]{:S(2)}) copy-start(bf16[2,256,1024]{2,1,0:T(8,128)(2,1)} %param.17) | copy-start | bytes 3145732
  7.2 23.3 %all-gather.14.cloned.1.call-start = ((), (), s32[]{:S(2)}) async-start(), calls=%async_computation.16 | async-start | bytes 1310720 | tf_op jit(solution)/shard_map/all_gather | solution.py:178
  7.9 79.1 %all-gather.8.cloned.1.call-start = ((), (), s32[]{:S(2)}) async-start(), calls=%async_computation.13 | async-start | bytes 1081344 | tf_op jit(solution)/shard_map/all_gather | solution.py:265
  8.7 178.5 %all-gather.10.cloned.1.call-start = ((), (), s32[]{:S(2)}) async-start(), calls=%async_computation.14 | async-start | bytes 7077888 | tf_op jit(solution)/shard_map/all_gather | solution.py:183
  20.5 198.5 %all-gather.18.cloned.1.call-start = ((), (), s32[]{:S(2)}) async-start(), calls=%async_computation.18 | async-start | bytes 1310720 | tf_op jit(solution)/shard_map/all_gather | solution.py:180
  21.0 296.8 %all-gather.12.cloned.1.call-start = ((), (), s32[]{:S(2)}) async-start(), calls=%async_computation.15 | async-start | bytes 2359296 | tf_op jit(solution)/shard_map/all_gather | solution.py:185
  29.4 352.0 %all-gather.16.cloned.1.call-start = ((), (), s32[]{:S(2)}) async-start(), calls=%async_computation.17 | async-start | bytes 9437184 | tf_op jit(solution)/shard_map/all_gather | solution.py:184
  32.8 160.3 %copy-start.26 = (f32[2,256]{1,0:T(2,128)}, f32[2,256]{1,0:T(2,128)S(1)}, u32[]{:S(2)}) copy-start(f32[2,256]{1,0:T(2,128)S(1)} %broadcast_multiply_fusion.5) | copy-start | bytes 6148
  34.6 52.4 %copy-start.35 = (bf16[2,128]{1,0:T(2,128)(2,1)}, bf16[2,128]{1,0:T(2,128)(2,1)S(1)}, u32[]{:S(2)}) copy-start(bf16[2,128]{1,0:T(2,128)(2,1)S(1)} %get-tuple-element.321) | copy-start | bytes 1540
  34.6 52.4 %copy-start.37 = (bf16[2,128]{1,0:T(2,128)(2,1)}, bf16[2,128]{1,0:T(2,128)(2,1)S(1)}, u32[]{:S(2)}) copy-start(bf16[2,128]{1,0:T(2,128)(2,1)S(1)} %get-tuple-element.322) | copy-start | bytes 1540
  34.6 158.5 %copy-start.31 = (f32[2,256]{1,0:T(2,128)}, f32[2,256]{1,0:T(2,128)S(1)}, u32[]{:S(2)}) copy-start(f32[2,256]{1,0:T(2,128)S(1)} %add_rsqrt_fusion.1) | copy-start | bytes 6148
  35.4 157.9 %copy-start.19 = (f32[256,32]{0,1:T(8,128)}, f32[256,32]{0,1:T(8,128)S(1)}, u32[]{:S(2)}) copy-start(f32[256,32]{0,1:T(8,128)S(1)} %get-tuple-element.320) | copy-start | bytes 98308
  89.1 104.1 %copy-start.22 = (f32[2,1024]{1,0:T(2,128)}, f32[2,1024]{1,0:T(2,128)S(1)}, u32[]{:S(2)}) copy-start(f32[2,1024]{1,0:T(2,128)S(1)} %get-tuple-element.317) | copy-start | bytes 24580
  215.0 40.6 %all-to-all-start = ((bf16[2,256,3072]{1,0,2:T(2,128)(2,1)}), bf16[2,256,3072]{1,0,2:T(2,128)(2,1)S(1)}, u32[]{:S(2)}, u32[]{:S(2)}) async-start(bf16[2,256,3072]{1,0,2:T(2,128)(2,1)} %copy.77), calls=%async_computation | async-start | bytes 6291456 | tf_op jit(solution)/shard_map/all_to_all | solution.py:195
  218.7 288.4 %all-gather.20.cloned.1.call-start = ((), (), s32[]{:S(2)}) async-start(), calls=%async_computation.19 | async-start | bytes 9437184 | tf_op jit(solution)/shard_map/all_gather | solution.py:186
  296.8 21.0 %copy-start.7 = (bf16[2,256,1024]{2,1,0:T(8,128)(2,1)S(1)}, bf16[2,256,1024]{2,1,0:T(8,128)(2,1)}, u32[]{:S(2)}) copy-start(bf16[2,256,1024]{2,1,0:T(8,128)(2,1)} %param.17) | copy-start | bytes 3145732
  316.7 64.8 %copy-start.24 = (f32[2,1024]{1,0:T(2,128)S(1)}, f32[2,1024]{1,0:T(2,128)}, u32[]{:S(2)}) copy-start(f32[2,1024]{1,0:T(2,128)} %get-tuple-element.316) | copy-start | bytes 24580
  321.1 196.8 %copy-start.11 = (f32[2,256,1024]{2,1,0:T(8,128)}, f32[2,256,1024]{2,1,0:T(8,128)S(1)}, u32[]{:S(2)}) copy-start(f32[2,256,1024]{2,1,0:T(8,128)S(1)} %get-tuple-element.324) | copy-start | bytes 6291460
  321.1 202.2 %copy-start.28 = (f32[2,256]{1,0:T(2,128)}, f32[2,256]{1,0:T(2,128)S(1)}, u32[]{:S(2)}) copy-start(f32[2,256]{1,0:T(2,128)S(1)} %broadcast_multiply_fusion.4) | copy-start | bytes 6148
  321.5 201.9 %copy-start.33 = (f32[2,256]{1,0:T(2,128)}, f32[2,256]{1,0:T(2,128)S(1)}, u32[]{:S(2)}) copy-start(f32[2,256]{1,0:T(2,128)S(1)} %add_rsqrt_fusion) | copy-start | bytes 6148
  381.5 125.6 %copy-start.16 = (bf16[2,256,1024]{2,1,0:T(8,128)(2,1)S(1)}, bf16[2,256,1024]{2,1,0:T(8,128)(2,1)}, u32[]{:S(2)}) copy-start(bf16[2,256,1024]{2,1,0:T(8,128)(2,1)} %param.25) | copy-start | bytes 3145732
  529.3 18.0 %all-to-all-start.2 = ((bf16[2,256,1024]{1,0,2:T(2,128)(2,1)}), bf16[2,256,1024]{1,0,2:T(2,128)(2,1)S(1)}, u32[]{:S(2)}, u32[]{:S(2)}) async-start(bf16[2,256,1024]{1,0,2:T(2,128)(2,1)} %copy.84), calls=%async_computation.2 | async-start | bytes 2097152 | tf_op jit(solution)/shard_map/all_to_all | solution.py:224
  532.8 225.9 %reduce-scatter.28.cloned.1.call-start = ((), (), s32[]{:S(2)}) async-start(), calls=%async_computation.27 | async-start | bytes 2359296
  540.6 281.6 %reduce-scatter.14.cloned.1.call-start = ((), (), s32[]{:S(2)}) async-start(), calls=%async_computation.20 | async-start | bytes 7077888 | tf_op jit(solution)/shard_map/reduce_scatter | solution.py:233
  706.9 267.1 %reduce-scatter.20.cloned.1.call-start = ((), (), s32[]{:S(2)}) async-start(), calls=%async_computation.23 | async-start | bytes 9437184 | tf_op jit(solution)/shard_map/reduce_scatter | solution.py:236
  717.7 408.4 %reduce-scatter.30.cloned.1.call-start = ((), (), s32[]{:S(2)}) async-start(), calls=%async_computation.28 | async-start | bytes 9437184
  717.7 22.4 %copy-start.18 = (bf16[2,256,1024]{2,1,0:T(8,128)(2,1)S(1)}, bf16[2,256,1024]{2,1,0:T(8,128)(2,1)}, u32[]{:S(2)}) copy-start(bf16[2,256,1024]{2,1,0:T(8,128)(2,1)} %param.25) | copy-start | bytes 3145732
  758.6 393.6 %reduce-scatter.18.cloned.1.call-start = ((), (), s32[]{:S(2)}) async-start(), calls=%async_computation.22 | async-start | bytes 327680 | tf_op jit(solution)/shard_map/reduce_scatter | solution.py:253
  760.5 413.5 %reduce-scatter.16.cloned.1.call-start = ((), (), s32[]{:S(2)}) async-start(), calls=%async_computation.21 | async-start | bytes 983040 | tf_op jit(solution)/shard_map/reduce_scatter | solution.py:247
  822.3 379.0 %reduce-scatter.22.cloned.1.call-start = ((), (), s32[]{:S(2)}) async-start(), calls=%async_computation.24 | async-start | bytes 1310720 | tf_op jit(solution)/shard_map/reduce_scatter | solution.py:250
  974.0 254.8 %reduce-scatter.24.cloned.1.call-start = ((), (), s32[]{:S(2)}) async-start(), calls=%async_computation.25 | async-start | bytes 1310720 | tf_op jit(solution)/shard_map/reduce_scatter | solution.py:256
  1128.6 239.1 %reduce-scatter.26.cloned.1.call-start = ((), (), s32[]{:S(2)}) async-start(), calls=%async_computation.26 | async-start | bytes 2162688 | tf_op jit(solution)/shard_map/reduce_scatter | solution.py:275
  (46 other events, 176.8 us)
Sparse Core Ops, SparseCore 0:
  9.6 20.8 all-gather.13
  33.3 53.6 all-gather.7
  89.2 97.9 all-gather.9
  188.6 14.8 all-gather.17
  205.4 50.8 all-gather.11
  258.3 123.1 all-gather.15
  383.5 123.5 all-gather.19
  540.7 66.6 reduce-scatter.27
  707.0 115.2 reduce-scatter.13
  825.7 148.1 reduce-scatter.19
  978.0 147.9 reduce-scatter.29
  1128.9 19.0 reduce-scatter.17
  1150.7 23.2 reduce-scatter.15
  1176.4 24.8 reduce-scatter.21
  1203.8 24.8 reduce-scatter.23
  1231.4 136.2 reduce-scatter.25
where the time goes:
time: 1380 us; the launch traced here: 1370 us
  waiting for transfers between devices  941 us (68%)
  matrix products  152 us (11%)
  local copies, waits for them, and re-layouts  118 us (9%)
  blocking collectives  76.8 us (6%)
  other arithmetic  63.7 us (5%)
  between operations  15 us (1%)
    unnamed x18, waiting for transfers between devices  155 us
    reduce_scatter x1, waiting for transfers between devices, data_layer(): lax.psum_scatter(grad_up.astype(jnp.bfloat16), 'dp', scatter_dimension=0,...  152 us
    reduce_scatter x1, waiting for transfers between devices, shards(): lax.psum_scatter(grad_time, ('dp', 'seq'), scatter_dimension=0, tiled=True)  137 us
    all_gather x1, waiting for transfers between devices, data_layer(): lax.all_gather(wide[3], 'dp', axis=1, tiled=True)  111 us
    all_gather x1, waiting for transfers between devices, data_layer(): lax.all_gather(wide[0], 'dp', axis=0, tiled=True)  98.1 us
    reduce_scatter x1, waiting for transfers between devices, data_layer(): lax.psum_scatter(grad_qkv.astype(jnp.bfloat16), 'dp', scatter_dimension=0...  61.7 us
    all_gather x1, waiting for transfers between devices, data_layer(): lax.all_gather(wide[1], 'dp', axis=0, tiled=True)  60 us
    all_gather x1, waiting for transfers between devices, shards(): full_time = lax.all_gather(w_time, ('dp', 'seq'), axis=0, tiled=True)  51.6 us
  transfers between devices with their start and end apart: 18, of which 14 were waited for; matrix products, arithmetic and copies ran while one was open for 21% of the time, Pallas kernels for 0%

commit v1 on v0

--- a/solution.py
+++ b/solution.py
@@ -1,8 +1,11 @@
+import functools
 import math
 
 import jax
 import jax.numpy as jnp
 from jax import lax
+from jax.experimental import pallas as pl
+from jax.experimental.pallas import tpu as pltpu
 from jax.sharding import PartitionSpec as P
 
 D = 1024
@@ -276,9 +279,984 @@
     return (output, grad_tokens, sums[0], sums[2], sums[1], sums[3], time_sum)
 
 
+BF = jnp.bfloat16
+F32 = jnp.float32
+MESHID = pl.DeviceIdType.MESH
+VMEM_LIMIT = 60 * 1024 * 1024
+
+
+def mm(a, b):
+    return lax.dot_general(a, b, (((1,), (0,)), ((), ())), preferred_element_type=F32)
+
+
+def mm_nt(a, b):
+    return lax.dot_general(a, b, (((1,), (1,)), ((), ())), preferred_element_type=F32)
+
+
+def mm_tn(a, b):
+    return lax.dot_general(a, b, (((0,), (0,)), ((), ())), preferred_element_type=F32)
+
+
+def peers():
+    g = lax.axis_index("dp")
+    s = lax.axis_index("seq")
+    core = lax.rem(s, 2)
+    return g, s, core, s + 1 - 2 * core, lax.rem(s + 2, 4), 3 - s
+
+
+def remote(src, dst, ss, rs, i, dev):
+    return pltpu.make_async_remote_copy(
+        src_ref=src,
+        dst_ref=dst,
+        send_sem=ss.at[i],
+        recv_sem=rs.at[i],
+        device_id=dev,
+        device_id_type=MESHID,
+    )
+
+
+def greet(devices):
+    barrier = pltpu.get_barrier_semaphore()
+    for dev in devices:
+        pl.semaphore_signal(barrier, inc=1, device_id=dev, device_id_type=MESHID)
+    pl.semaphore_wait(barrier, len(devices))
+
+
+def moments(field):
+    centered = field - jnp.mean(field, axis=-1, keepdims=True)
+    spread = jnp.mean(centered * centered, axis=-1, keepdims=True)
+    inverse = lax.rsqrt(spread + EPSILON)
+    return centered * inverse, inverse
+
+
+def ring_place(g):
+    z, y = g // 2, lax.rem(g, 2)
+    return z + y * (7 - 2 * z)
+
+
+def ring_index(p):
+    p = lax.rem(p + 16, 8)
+    return 2 * p + (p // 4) * (15 - 4 * p)
+
+
+WAYS = (1, -1)
+
+
+class Gather:
+    def __init__(self, own, view, ss, rs, first):
+        self.own, self.view, self.ss, self.rs, self.first = own, view, ss, rs, first
+
+    def hop(self, k, way):
+        g, s = lax.axis_index("dp"), lax.axis_index("seq")
+        p = ring_place(g)
+        j = ring_index(p - way * (k - 1))
+        half = None if k < 4 else (0 if way > 0 else 1)
+        dst = self.view(j, half)
+        src = self.own if k == 1 else dst
+        i = self.first + 2 * (k - 1) + (way < 0)
+        return remote(src, dst, self.ss, self.rs, i, (ring_index(p + way), s))
+
+    def start(self):
+        for way in WAYS:
+            self.hop(1, way).start()
+
+    def forward(self, k):
+        for way in WAYS:
+            self.hop(k - 1, way).wait_recv()
+            self.hop(k, way).start()
+
+    def arrive(self):
+        for way in WAYS:
+            self.hop(4, way).wait_recv()
+
+    def drain(self):
+        for k in (1, 2, 3, 4):
+            for way in WAYS:
+                self.hop(k, way).wait_send()
+
+
+class Scatter:
+    def __init__(self, view, halves, wholes, ss, rs, first):
+        self.view, self.halves, self.wholes = view, halves, wholes
+        self.ss, self.rs, self.first = ss, rs, first
+
+    def hop(self, k, way):
+        g, s = lax.axis_index("dp"), lax.axis_index("seq")
+        p = ring_place(g)
+        side = 0 if way > 0 else 1
+        j = ring_index(p + way * (5 - k))
+        src = self.view(j, side if k == 1 else None)
+        dst = self.halves.at[side] if k == 1 else self.wholes.at[3 * side + k - 2]
+        i = self.first + 2 * (k - 1) + side
+        return remote(src, dst, self.ss, self.rs, i, (ring_index(p + way), s))
+
+    def start(self):
+        for way in WAYS:
+            self.hop(1, way).start()
+
+    def forward(self, k):
+        p = ring_place(lax.axis_index("dp"))
+        for way in WAYS:
+            side = 0 if way > 0 else 1
+            self.hop(k - 1, way).wait_recv()
+            got = self.halves.at[side] if k == 2 else self.wholes.at[3 * side + k - 3]
+            mine = self.view(ring_index(p + way * (5 - k)), side if k == 2 else None)
+            mine[...] = (mine[...].astype(F32) + got[...].astype(F32)).astype(BF)
+            self.hop(k, way).start()
+
+    def result(self):
+        for way in WAYS:
+            self.hop(4, way).wait_recv()
+        mine = self.view(lax.axis_index("dp"), None)
+        return mine[...].astype(F32) + (self.wholes[2].astype(F32) + self.wholes[5].astype(F32))
+
+    def drain(self):
+        for k in (1, 2, 3, 4):
+            for way in WAYS:
+                self.hop(k, way).wait_send()
+
+
+def rows_of(ref, half, size):
+    return ref if half is None else ref.at[half * (size // 2) : (half + 1) * (size // 2)]
+
+
+def k1_body(
+    tok, wt, fs, w_qkv, w_out, w_up, w_down, cs, sn, cot,
+    tok_all, modul, wq, out_all, up_all, down_all, h_out, qkv, lse, own, attn_all, cot_all,
+    tokv, wtime, pbuf, ls, ss, rs, gs, gr, fs_, fr_,
+):
+    g, s, core, s1, s2, s3 = peers()
+    p = ring_place(g)
+    greet([(g, s1), (g, s2), (g, s3), (ring_index(p + 1), s), (ring_index(p - 1), s)])
+    nb, tl = tok.shape[0], tok.shape[1]
+    rows = 4 * tl
+    blk = 256
+    nq = rows // blk
+    heads = own.shape[2] // HD
+    nr, nc = w_out.shape[0], w_out.shape[1]
+
+    def lanes(j, size):
+        return pl.ds(pl.multiple_of(j * size, size), size)
+
+    def view_out(other):
+        def view(j, half):
+            lo, size = (0, nr) if half is None else (half * (nr // 2), nr // 2)
+            return out_all.at[pl.ds(pl.multiple_of(other * nr + lo, size), size), lanes(j, nc)]
+
+        return view
+
+    def view_down(j, half):
+        size = w_down.shape[0]
+        lo, n = (0, size) if half is None else (half * (size // 2), size // 2)
+        return down_all.at[lo : lo + n, lanes(j, w_down.shape[1])]
+
+    def view_rows(ref, size):
+        def view(j, half):
+            lo, n = (0, size) if half is None else (half * (size // 2), size // 2)
+            return ref.at[pl.ds(pl.multiple_of(j * size + lo, n), n)]
+
+        return view
+
+    def view_time(j, half):
+        return wtime.at[j] if half is None else wtime.at[j, :, half * D : (half + 1) * D]
+
+    here = view_out(s)(g, None)
+    time_ring = Gather(wt, view_time, gs, gr, 0)
+    qkv_ring = Gather(w_qkv, view_rows(wq, w_qkv.shape[0]), gs, gr, 8)
+    up_ring = Gather(w_up, view_rows(up_all, w_up.shape[0]), gs, gr, 16)
+    down_ring = Gather(w_down, view_down, gs, gr, 24)
+    out_ring = Gather(w_out, view_out(s), gs, gr, 32)
+    far_ring = Gather(view_out(s2)(g, None), view_out(s2), gs, gr, 40)
+
+    time_ring.start()
+    qkv_ring.start()
+    pair_out = remote(w_out, here, ss, rs, 0, (g, s2))
+    pair_out.start()
+    far, near, passed = [], [], []
+    for b in range(nb):
+        cp = remote(tok.at[b], tokv.at[b, s], ss, rs, 1 + b, (g, s2))
+        cp.start()
+        far.append(cp)
+    for b in range(nb):
+        cp = remote(tok.at[b], tokv.at[b, s], ss, rs, 3 + b, (g, s1))
+        cp.start()
+        near.append(cp)
+    local = [
+        pltpu.make_async_copy(tok, tokv.at[:, s], ls.at[0]),
+        pltpu.make_async_copy(w_qkv, view_rows(wq, w_qkv.shape[0])(g, None), ls.at[1]),
+        pltpu.make_async_copy(w_up, view_rows(up_all, w_up.shape[0])(g, None), ls.at[2]),
+        pltpu.make_async_copy(w_down, view_down(g, None), ls.at[3]),
+        pltpu.make_async_copy(w_out, here, ls.at[4]),
+        pltpu.make_async_copy(cot, cot_all.at[:, s], ls.at[5]),
+    ]
+    for cp in local:
+        cp.start()
+    wtime[g] = wt[...]
+    for k in (2, 3, 4):
+        time_ring.forward(k)
+        qkv_ring.forward(k)
+    up_ring.start()
+    time_ring.arrive()
+    weights = wtime[...].astype(F32)
+    parts = [
+        jnp.sum(jnp.sum(weights * fs[b], axis=0), axis=0, keepdims=True) for b in range(nb)
+    ]
+    pbuf[0] = jnp.concatenate(parts, axis=0)
+    small = []
+    for e, other in ((1, s1), (2, s2), (3, s3)):
+        cp = remote(pbuf.at[0], pbuf.at[e], ss, rs, 4 + e, (g, other))
+        cp.start()
+        small.append(cp)
+    down_ring.start()
+    out_ring.start()
+    pair_out.wait_recv()
+    far_ring.start()
+    for b in range(nb):
+        far[b].wait_recv()
+        cp = remote(tokv.at[b, s2], tokv.at[b, s2], ss, rs, 8 + b, (g, s1))
+        cp.start()
+        passed.append(cp)
+        if b == 0:
+            for c in small:
+                c.wait_recv()
+            modul[...] = (pbuf[0] + pbuf[1]) + (pbuf[2] + pbuf[3])
+            qkv_ring.arrive()
+            local[0].wait()
+            local[1].wait()
+    cot_far, cot_near, cot_pass = [], [], []
+    for b in range(nb):
+        cp = remote(cot.at[b], cot_all.at[b, s], ss, rs, 10 + b, (g, s2))
+        cp.start()
+        cot_far.append(cp)
+    for b in range(nb):
+        cp = remote(cot.at[b], cot_all.at[b, s], ss, rs, 12 + b, (g, s1))
+        cp.start()
+        cot_near.append(cp)
+    for cp in near + passed:
+        cp.wait_recv()
+    keep_tok = pltpu.make_async_copy(tokv, tok_all, ls.at[6])
+    keep_tok.start()
+
+    def attn_copy(kind, it):
+        b, q = it // nq, lax.rem(it, nq)
+        r = pl.ds(pl.multiple_of(q * blk, blk), blk)
+        if kind == 2:
+            ref = attn_all.at[b, s2, r]
+            return remote(ref, ref, fs_.at[2], fr_.at[2], it, (g, s1))
+        return remote(
+            own.at[b, r], attn_all.at[b, s, r], fs_.at[kind], fr_.at[kind], it, (g, (s2, s1)[kind])
+        )
+
+    lane = lax.broadcasted_iota(jnp.int32, (1, 2 * 128), 1)
+
+    def project(b):
+        scale = 1.0 + modul[pl.ds(b, 1), :D]
+
+        def one(i, _):
+            r = pl.ds(pl.multiple_of(i * blk, blk), blk)
+            normed, _inv = moments(tokv[b, i].astype(F32))
+            h = (normed * scale).astype(BF)
+            h_out[b, r] = h
+            raw = mm(h, wq[...])
+            c, n = cs[r], sn[r]
+            qa, qb = raw[:, :128] * 0.125, raw[:, 128:256] * 0.125
+            ka, kb = raw[:, 256:384], raw[:, 384:512]
+            qkv[b, 0, r] = jnp.concatenate([qa * c - qb * n, qb * c + qa * n], axis=1).astype(BF)
+            qkv[b, 1, r] = jnp.concatenate([ka * c - kb * n, kb * c + ka * n], axis=1).astype(BF)
+            qkv[b, 2, r] = raw[:, 512:].astype(BF)
+            return 0
+
+        lax.fori_loop(0, nq, one, 0)
+
+    def step(it, _):
+        b, q = it // nq, lax.rem(it, nq)
+
+        @pl.when(q == 0)
+        def _():
+            project(b)
+
+        for when, ring, k in (
+            (1, up_ring, 2), (2, down_ring, 2), (2, out_ring, 2), (3, far_ring, 2),
+            (4, up_ring, 3), (5, down_ring, 3), (5, out_ring, 3), (6, far_ring, 3),
+            (7, up_ring, 4),
+        ):
+
+            @pl.when(it == when)
+            def _(ring=ring, k=k):
+                ring.forward(k)
+
+        r = pl.ds(pl.multiple_of(q * blk, blk), blk)
+        query = qkv[b, 0, r]
+        keys, values = qkv[b, 1], qkv[b, 2]
+        out = jnp.zeros((blk, heads * HD), F32)
+        stats = jnp.zeros((blk, 128), F32)
+        for h in range(heads):
+            mask = lax.rem(lane, 128) // 32 == h
+            scores = mm_nt(jnp.where(mask, query, jnp.zeros_like(query)), keys)
+            top = jnp.max(scores, axis=1, keepdims=True)
+            expo = jnp.exp(scores - top)
+            total = jnp.sum(expo, axis=1, keepdims=True)
+            res = mm(expo.astype(BF), values) * (1.0 / total)
+            out = jnp.where(lane // HD == h, res, out)
+            stats = jnp.where(lane[:, :128] == h, top + jnp.log(total), stats)
+        own[b, r] = out.astype(BF)
+        lse[b, :, r] = stats.T[:8]
+        attn_copy(0, it).start()
+        attn_copy(1, it).start()
+        return 0
+
+    lax.fori_loop(0, nb * nq, step, 0)
+    keep = pltpu.make_async_copy(own, attn_all.at[:, s], ls.at[7])
+    keep.start()
+    for ring in (down_ring, out_ring, far_ring):
+        ring.forward(4)
+    for b in range(nb):
+        cot_far[b].wait_recv()
+        cp = remote(cot_all.at[b, s2], cot_all.at[b, s2], ss, rs, 14 + b, (g, s1))
+        cp.start()
+        cot_pass.append(cp)
+
+    def forward(it, _):
+        attn_copy(0, it).wait_recv()
+        attn_copy(2, it).start()
+        return 0
+
+    lax.fori_loop(0, nb * nq, forward, 0)
+    for ring in (up_ring, down_ring, out_ring, far_ring):
+        ring.arrive()
+    local[4].wait()
+    cross = []
+    for e, other in ((0, s), (1, s2)):
+        ref = out_all.at[pl.ds(pl.multiple_of(other * nr, nr), nr)]
+        cp = remote(ref, ref, ss, rs, 16 + e, (g, s1))
+        cp.start()
+        cross.append(cp)
+
+    def finish(it, _):
+        attn_copy(0, it).wait_send()
+        attn_copy(1, it).wait()
+        attn_copy(2, it).wait()
+        return 0
+
+    lax.fori_loop(0, nb * nq, finish, 0)
+    for cp in cot_near + cot_pass + cross:
+        cp.wait()
+    for cp in cot_far + far + near + passed + small + [pair_out]:
+        cp.wait_send()
+    for ring in (time_ring, qkv_ring, up_ring, down_ring, out_ring, far_ring):
+        ring.drain()
+    for i in (2, 3, 5):
+        local[i].wait()
+    keep_tok.wait()
+    keep.wait()
+
+
+def run_k1(nd, tokens, w_time, fs, w_qkv, w_out, w_up, w_down, cs, sn, cot):
+    nb, tl, width = tokens.shape
+    rows = 4 * tl
+    cols = w_qkv.shape[1] // 3
+    hidden = w_up.shape[1]
+    vm = pl.BlockSpec(memory_space=pltpu.VMEM)
+    hb = pl.BlockSpec(memory_space=pl.ANY)
+    steps = nb * (rows // 256)
+    sds = jax.ShapeDtypeStruct
+    dma = pltpu.SemaphoreType.DMA
+    return pl.pallas_call(
+        k1_body,
+        out_shape=(
+            sds((nb, 4, tl, width), BF),
+            sds((nb, 2 * width), F32),
+            sds((width, 3 * cols), BF),
+            sds((width, width), BF),
+            sds((width, hidden), BF),
+            sds((hidden, width), BF),
+            sds((nb, rows, width), BF),
+            sds((nb, 3, rows, cols), BF),
+            sds((nb, 8, rows), F32),
+            sds((nb, rows, cols), BF),
+            sds((nb, 4, rows, cols), BF),
+            sds((nb, 4, tl, width), BF),
+        ),
+        in_specs=[hb, vm, vm, hb, hb, hb, hb, vm, vm, hb],
+        out_specs=(hb, vm, vm, hb, hb, hb, vm, vm, vm, vm, hb, hb),
+        scratch_shapes=[
+            pltpu.VMEM((nb, 4, tl, width), BF),
+            pltpu.VMEM((nd,) + w_time.shape, BF),
+            pltpu.VMEM((4, nb, 2 * width), F32),
+            dma((8,)),
+            dma((18,)),
+            dma((18,)),
+            dma((48,)),
+            dma((48,)),
+            dma((3, steps)),
+            dma((3, steps)),
+        ],
+        compiler_params=pltpu.CompilerParams(
+            collective_id=0, has_side_effects=True, vmem_limit_bytes=VMEM_LIMIT
+        ),
+        name="attention_forward",
+    )(tokens, w_time, fs, w_qkv, w_out, w_up, w_down, cs, sn, cot)
+
+
+def k2_body(
+    tok, attn, cot, modul, w_out, w_up, w_down,
+    grad_down, grad_up, grad_out, d_mid, base, osend, d_heads, dsc,
+    act, htwo, dup, mids, pa, pb_, ra, rb, xs, xr, dat, stage,
+    ls, ss, rs, gs,
+):
+    g, s, core, s1, s2, s3 = peers()
+    chip = s // 2
+    greet([(g, s1), (g, s2), (g, s3)])
+    nb, tl = tok.shape[0], tok.shape[2]
+
+    def block(b, owner, slot):
+        scale = 1.0 + modul[pl.ds(b, 1), D:]
+        r = pl.ds(pl.multiple_of(owner * tl, tl), tl)
+        a = jnp.concatenate([attn[b, j, r] for j in range(4)], axis=1)
+        mid = tok[b, owner].astype(F32) + mm(a, w_out[...])
+        normed, _inv = moments(mid)
+        h = (normed * scale).astype(BF)
+        upper = mm(h, w_up[...])
+        phi = 0.5 * (1.0 + lax.erf(upper * ROOT_HALF))
+        active = (upper * phi).astype(BF)
+        slope = phi + upper * (DENSITY * jnp.exp(-0.5 * upper * upper))
+        d_act = mm_nt(cot[b, owner], w_down[...])
+        d_up = (d_act * slope).astype(BF)
+        i = b * 4 + owner
+        act[i] = active
+        htwo[i] = h
+        dup[i] = d_up
+        return mid, mm_nt(d_up, w_up[...]), mm(active, w_down[...])
+
+    def pair_copies(jp):
+        return (
+            remote(pa.at[jp], ra.at[jp], ss, rs, jp, (g, s1)),
+            remote(pb_.at[jp], rb.at[jp], ss, rs, 4 + jp, (g, s1)),
+        )
+
+    def far_copy(b):
+        return remote(xs.at[b], xr.at[b], ss, rs, 8 + b, (g, s2))
+
+    def pair(jp, _):
+        phase, b = jp // nb, lax.rem(jp, nb)
+        where = chip + (1 - phase) * (1 - 2 * chip)
+        _mid, dh, out = block(b, 2 * where + 1 - core, jp)
+        pa[jp] = dh.astype(BF)
+        pb_[jp] = out.astype(BF)
+        ca, cb = pair_copies(jp)
+        ca.start()
+        cb.start()
+        mid, dh, out = block(b, 2 * where + core, jp)
+        ca.wait_recv()
+        cb.wait_recv()
+        dh = dh + ra[jp].astype(F32)
+        out = out + rb[jp].astype(F32)
+
+        @pl.when(phase == 0)
+        def _():
+            xs[b] = dh.astype(BF)
+            osend[b] = out.astype(BF)
+            far_copy(b).start()
+
+        @pl.when(phase == 1)
+        def _():
+            d_mid[b] = dh
+            mids[b] = mid
+            base[b] = out + mid
+
+        return 0
+
+    lax.fori_loop(0, 2 * nb, pair, 0)
+
+    def tail(b, _):
+        scale = 1.0 + modul[pl.ds(b, 1), D:]
+        far_copy(b).wait_recv()
+        dh = d_mid[b] + xr[b].astype(F32)
+        normed, inverse = moments(mids[b])
+        dsc[pl.ds(b, 1)] = jnp.sum(dh * normed, axis=0, keepdims=True)
+        dn = dh * scale
+        inner = jnp.mean(dn * normed, axis=-1, keepdims=True)
+        dm = cot[b, s].astype(F32) + inverse * (
+            dn - jnp.mean(dn, axis=-1, keepdims=True) - normed * inner
+        )
+        d_mid[b] = dm
+        branch = dm.astype(BF)
+        xs2 = mm_nt(branch, w_out[...]).astype(BF)
+        for j in range(4):
+            dat[j, b] = xs2[:, j * 256 : (j + 1) * 256]
+        return 0
+
+    lax.fori_loop(0, nb, tail, 0)
+    copies = []
+    for e, other in ((2, s2), (3, s3), (1, s1)):
+        cp = remote(dat.at[other], d_heads.at[s], ss, rs, 9 + e, (g, other))
+        cp.start()
+        copies.append(cp)
+    keep = pltpu.make_async_copy(dat.at[s], d_heads.at[s], ls)
+    keep.start()
+
+    own_rows = pl.ds(pl.multiple_of(s * tl, tl), tl)
+    branch = d_mid[...].astype(BF).reshape(nb * tl, D)
+    for j in range(4):
+        a = jnp.concatenate([attn[b, j, own_rows] for b in range(nb)], axis=0)
+        stage[j] = mm_tn(a, branch).astype(BF)
+        pltpu.make_async_copy(stage.at[j], grad_out.at[j], gs.at[j]).start()
+
+    def out_copy(which, i):
+        r = pl.ds(pl.multiple_of(i * 256, 256), 256)
+        k = 2 * lax.rem(i, 2) + which
+        return pltpu.make_async_copy(stage.at[k], (grad_down, grad_up)[which].at[r], gs.at[k])
+
+    def grads(i, _):
+        r = pl.ds(pl.multiple_of(i * 256, 256), 256)
+        left = act[:, :, r].reshape(4 * nb * tl, 256)
+        res = mm_tn(left, cot[...].reshape(4 * nb * tl, D)).astype(BF)
+        out_copy(0, i).wait()
+        stage[2 * lax.rem(i, 2)] = res
+        out_copy(0, i).start()
+        left = htwo[:, :, r].reshape(4 * nb * tl, 256)
+        res = mm_tn(left, dup[...].reshape(4 * nb * tl, dup.shape[2])).astype(BF)
+        out_copy(1, i).wait()
+        stage[2 * lax.rem(i, 2) + 1] = res
+        out_copy(1, i).start()
+        return 0
+
+    lax.fori_loop(0, D // 256, grads, 0)
+    for i in range(D // 256 - 2, D // 256):
+        out_copy(0, i).wait()
+        out_copy(1, i).wait()
+
+    def done(jp, _):
+        ca, cb = pair_copies(jp)
+        ca.wait_send()
+        cb.wait_send()
+        return 0
+
+    lax.fori_loop(0, 2 * nb, done, 0)
+    for b in range(nb):
+        far_copy(b).wait_send()
+    for cp in copies:
+        cp.wait()
+    keep.wait()
+
+
+def run_k2(tok_all, attn_all, cot_all, modul, w_out, w_up, w_down):
+    nb, _, tl, width = tok_all.shape
+    hidden = w_up.shape[1]
+    cols = attn_all.shape[3]
+    vm = pl.BlockSpec(memory_space=pltpu.VMEM)
+    hb = pl.BlockSpec(memory_space=pl.ANY)
+    sds = jax.ShapeDtypeStruct
+    return pl.pallas_call(
+        k2_body,
+        out_shape=(
+            sds((hidden, width), BF),
+            sds((width, hidden), BF),
+            sds((4, cols, width), BF),
+            sds((nb, tl, width), F32),
+            sds((nb, tl, width), F32),
+            sds((nb, tl, width), BF),
+            sds((4, nb, tl, cols), BF),
+            sds((nb, width), F32),
+        ),
+        in_specs=[vm] * 7,
+        out_specs=(hb, hb, hb, vm, vm, vm, hb, vm),
+        scratch_shapes=[
+            pltpu.VMEM((4 * nb, tl, hidden), BF),
+            pltpu.VMEM((4 * nb, tl, width), BF),
+            pltpu.VMEM((4 * nb, tl, hidden), BF),
+            pltpu.VMEM((nb, tl, width), F32),
+            pltpu.VMEM((2 * nb, tl, width), BF),
+            pltpu.VMEM((2 * nb, tl, width), BF),
+            pltpu.VMEM((2 * nb, tl, width), BF),
+            pltpu.VMEM((2 * nb, tl, width), BF),
+            pltpu.VMEM((nb, tl, width), BF),
+            pltpu.VMEM((nb, tl, width), BF),
+            pltpu.VMEM((4, nb, tl, cols), BF),
+            pltpu.VMEM((4, 256, width), BF),
+            pltpu.SemaphoreType.DMA,
+            pltpu.SemaphoreType.DMA((13,)),
+            pltpu.SemaphoreType.DMA((13,)),
+            pltpu.SemaphoreType.DMA((4,)),
+        ],
+        compiler_params=pltpu.CompilerParams(
+            collective_id=1, has_side_effects=True, vmem_limit_bytes=VMEM_LIMIT
+        ),
+        name="feed_forward",
+    )(tok_all, attn_all, cot_all, modul, w_out, w_up, w_down)
+
+
+def k3_body(
+    qkv, lse, own, d_heads, w, h_one, tok, modul, cs, sn, d_mid, base, osend,
+    g_down, g_up, g_out, dsc_two, feats,
+    output, grad_tok, s_qkv, s_out, s_up, s_down, s_time,
+    orecv, dqt, draw, pa, ra, xs, xr, sumh, dhb,
+    vd, vu, vo, vq, oa, ob, ox, osum, down_h, down_w, up_h, up_w, out_h, out_w, qkv_h, qkv_w,
+    dpart, dall,
+    ls, ss, rs, gs, gr,
+):
+    g, s, core, s1, s2, s3 = peers()
+    chip = s // 2
+    p = ring_place(g)
+    nd = dall.shape[0]
+    others = [(lax.rem(g + d, nd), s) for d in range(1, nd)]
+    loads = [
+        pltpu.make_async_copy(g_down, vd, ls.at[0]),
+        pltpu.make_async_copy(g_up, vu, ls.at[1]),
+        pltpu.make_async_copy(g_out, oa, ls.at[2]),
+    ]
+    for cp in loads:
+        cp.start()
+    greet([(g, s1), (g, s2), (g, s3)] + others)
+    nb, tl = tok.shape[0], tok.shape[1]
+    rows, cols = own.shape[1], own.shape[2]
+    heads = cols // HD
+    blk = 256
+    nk = rows // blk
+    pc = D // nd
+
+    def lanes(j, size):
+        return pl.ds(pl.multiple_of(j * size, size), size)
+
+    def view_cols(ref, size):
+        def view(j, half):
+            lo, n = (0, size) if half is None else (half * (size // 2), size // 2)
+            return ref.at[lo : lo + n, lanes(j, pc)]
+
+        return view
+
+    def view_rows(ref):
+        def view(j, half):
+            lo, n = (0, pc) if half is None else (half * (pc // 2), pc // 2)
+            return ref.at[pl.ds(pl.multiple_of(j * pc + lo, n), n)]
+
+        return view
+
+    down_ring = Scatter(view_cols(vd, vd.shape[0]), down_h, down_w, gs, gr, 0)
+    up_ring = Scatter(view_rows(vu), up_h, up_w, gs, gr, 8)
+    out_ring = Scatter(view_cols(vo, vo.shape[0]), out_h, out_w, gs, gr, 16)
+    qkv_ring = Scatter(view_rows(vq), qkv_h, qkv_w, gs, gr, 24)
+    loads[0].wait()
+    down_ring.start()
+    back = []
+    for b in range(nb):
+        cp = remote(osend.at[b], orecv.at[b], ss, rs, b, (g, s2))
+        cp.start()
+        back.append(cp)
+    loads[2].wait()
+    cross = []
+    for phase in range(2):
+        where = chip if phase else 1 - chip
+        cp = remote(oa.at[2 * where + 1 - core], ob.at[phase], ss, rs, 8 + phase, (g, s1))
+        cp.start()
+        cross.append(cp)
+    loads[1].wait()
+    up_ring.start()
+    over = remote(osum, ox, ss, rs, 10, (g, s2))
+
+    def out_pair():
+        for cp in cross:
+            cp.wait_recv()
+        osum[...] = (oa[2 * (1 - chip) + core].astype(F32) + ob[0].astype(F32)).astype(BF)
+        over.start()
+
+    def out_own():
+        over.wait_recv()
+        vo[...] = (
+            (oa[s].astype(F32) + ob[1].astype(F32)) + ox[...].astype(F32)
+        ).astype(BF)
+        out_ring.start()
+
+    lane = lax.broadcasted_iota(jnp.int32, (1, cols), 1)
+    pick = (
+        lax.broadcasted_iota(jnp.int32, (8, cols), 1) // HD
+        == lax.broadcasted_iota(jnp.int32, (8, cols), 0)
+    ).astype(F32)
+
+    def near_copy(b, phase):
+        i = 2 * b + phase
+        return remote(pa.at[i], ra.at[i], ss, rs, 2 + i, (g, s1))
+
+    def far_copy(b):
+        return remote(xs.at[b], xr.at[b], ss, rs, 6 + b, (g, s2))
+
+    def sequence(b, _):
+        for j in range(4):
+            dhb[j * tl : (j + 1) * tl] = d_heads[j, b]
+        query = qkv[b, 0]
+        d_out = dhb[...]
+        prod = d_out.astype(F32) * own[b].astype(F32)
+        delta = lax.dot_general(
+            pick, prod, (((1,), (1,)), ((), ())), precision=HIGHEST, preferred_element_type=F32
+        )
+        dqt[...] = jnp.zeros_like(dqt)
+
+        def keys_block(i, _):
+            it = b * nk + i
+            for when, act in (
+                (1, out_pair),
+                (1, lambda: down_ring.forward(2)),
+                (2, lambda: up_ring.forward(2)),
+                (3, lambda: down_ring.forward(3)),
+                (4, lambda: up_ring.forward(3)),
+                (5, lambda: down_ring.forward(4)),
+                (6, lambda: up_ring.forward(4)),
+                (7, out_own),
+            ):
+
+                @pl.when(it == when)
+                def _(act=act):
+                    act()
+
+            r = pl.ds(pl.multiple_of(i * blk, blk), blk)
+            keys, values = qkv[b, 1, r], qkv[b, 2, r]
+            dk = jnp.zeros((blk, cols), F32)
+            dv = jnp.zeros((blk, cols), F32)
+            for h in range(heads):
+                mask = lax.rem(lane, 128) // 32 == h
+                mask_v = lane // HD == h
+                km = jnp.where(mask, keys, jnp.zeros_like(keys))
+                vmask = jnp.where(mask_v, values, jnp.zeros_like(values))
+                probs = jnp.exp(mm_nt(km, query) - lse[b, h : h + 1])
+                d_probs = mm_nt(vmask, d_out)
+                ds = (probs * (d_probs - delta[h : h + 1])).astype(BF)
+                dv = jnp.where(mask_v, mm(probs.astype(BF), d_out), dv)
+                dk = jnp.where(mask, mm(ds, query), dk)
+                dqt[...] += mm_tn(km, ds)
+            c, n = cs[r], sn[r]
+            da, db = dk[:, :128], dk[:, 128:]
+            draw[b, r, 256:512] = jnp.concatenate([da * c + db * n, db * c - da * n], axis=1).astype(BF)
+            draw[b, r, 512:768] = dv.astype(BF)
+            return 0
+
+        lax.fori_loop(0, nk, keys_block, 0)
+        dq = dqt[...].T * 0.125
+        da, db = dq[:, :128], dq[:, 128:]
+        c, n = cs[...], sn[...]
+        draw[b, :, 0:256] = jnp.concatenate([da * c + db * n, db * c - da * n], axis=1).astype(BF)
+
+        def part(owner):
+            r = pl.ds(pl.multiple_of(owner * tl, tl), tl)
+            return mm_nt(draw[b, r], w[...])
+
+        for phase in range(2):
+            where = chip if phase else 1 - chip
+            pa[2 * b + phase] = part(2 * where + 1 - core).astype(BF)
+            near_copy(b, phase).start()
+            kept = part(2 * where + core)
+            near_copy(b, phase).wait_recv()
+            kept = kept + ra[2 * b + phase].astype(F32)
+            if phase == 0:
+                xs[b] = kept.astype(BF)
+                far_copy(b).start()
+            else:
+                sumh[b] = kept
+        return 0
+
+    lax.fori_loop(0, nb, sequence, 0)
+
+    def grads(i, _):
+        r = pl.ds(pl.multiple_of(i * 256, 256), 256)
+        left = h_one[:, :, r].reshape(nb * rows, 256)
+        vq[r] = mm_tn(left, draw[...].reshape(nb * rows, 3 * cols)).astype(BF)
+        return 0
+
+    lax.fori_loop(0, D // 256, grads, 0)
+    qkv_ring.start()
+    out_ring.forward(2)
+    s_down[...] = down_ring.result()
+    s_up[...] = up_ring.result()
+    out_ring.forward(3)
+    qkv_ring.forward(2)
+    for b in range(nb):
+        back[b].wait_recv()
+        output[b] = (base[b] + orecv[b].astype(F32)).astype(BF)
+    out_ring.forward(4)
+    qkv_ring.forward(3)
+
+    def tail(b, _):
+        scale = 1.0 + modul[pl.ds(b, 1), :D]
+        far_copy(b).wait_recv()
+        dh = sumh[b] + xr[b].astype(F32)
+        normed, inverse = moments(tok[b].astype(F32))
+        dpart[0, pl.ds(b, 1), :D] = jnp.sum(dh * normed, axis=0, keepdims=True)
+        dn = dh * scale
+        inner = jnp.mean(dn * normed, axis=-1, keepdims=True)
+        grad_tok[b] = (
+            d_mid[b]
+            + inverse * (dn - jnp.mean(dn, axis=-1, keepdims=True) - normed * inner)
+        ).astype(BF)
+        return 0
+
+    lax.fori_loop(0, nb, tail, 0)
+    dpart[0, :, D:] = dsc_two[...]
+    small = []
+    for e, other in ((1, s1), (2, s2), (3, s3)):
+        cp = remote(dpart.at[0], dpart.at[e], ss, rs, 10 + e, (g, other))
+        cp.start()
+        small.append(cp)
+    qkv_ring.forward(4)
+    for cp in small:
+        cp.wait_recv()
+    dall[0, :, : 2 * D] = (dpart[0] + dpart[1]) + (dpart[2] + dpart[3])
+    dall[0, :, 2 * D :] = feats[...]
+    wide = []
+    for d in range(1, nd):
+        cp = remote(dall.at[0], dall.at[d], ss, rs, 13 + d, others[d - 1])
+        cp.start()
+        wide.append(cp)
+    s_out[...] = out_ring.result()
+    s_qkv[...] = qkv_ring.result()
+    for cp in wide:
+        cp.wait_recv()
+    depth = s_time.shape[0]
+    place = (4 * g + s) * depth
+    hit = (
+        lax.broadcasted_iota(jnp.int32, (depth, TF), 1)
+        == lax.broadcasted_iota(jnp.int32, (depth, TF), 0) + place
+    )
+    total = jnp.zeros((depth, 2 * D), F32)
+    for d in range(nd):
+        for b in range(nb):
+            row = dall[d, b : b + 1]
+            column = jnp.sum(jnp.where(hit, row[:, 2 * D :], 0.0), axis=1, keepdims=True)
+            total = total + column * row[:, : 2 * D]
+    s_time[...] = total
+    for b in range(nb):
+        back[b].wait_send()
+        far_copy(b).wait_send()
+        for phase in range(2):
+            near_copy(b, phase).wait_send()
+    for cp in cross + small + wide + [over]:
+        cp.wait_send()
+    for ring in (down_ring, up_ring, out_ring, qkv_ring):
+        ring.drain()
+
+
+def run_k3(
+    nd, qkv, lse, own, d_heads, w, h_one, tokens, modul, cs, sn, d_mid, base, osend,
+    g_down, g_up, g_out, dsc_two, feats,
+):
+    nb, tl, width = tokens.shape
+    rows, cols = own.shape[1], own.shape[2]
+    hidden = g_up.shape[1]
+    pc = width // nd
+    vm = pl.BlockSpec(memory_space=pltpu.VMEM)
+    hb = pl.BlockSpec(memory_space=pl.ANY)
+    sds = jax.ShapeDtypeStruct
+    v = pltpu.VMEM
+    dma = pltpu.SemaphoreType.DMA
+    return pl.pallas_call(
+        k3_body,
+        out_shape=(
+            sds((nb, tl, width), BF),
+            sds((nb, tl, width), BF),
+            sds((pc, 3 * cols), F32),
+            sds((cols, pc), F32),
+            sds((pc, hidden), F32),
+            sds((hidden, pc), F32),
+            sds((TF // (4 * nd), 2 * width), F32),
+        ),
+        in_specs=[vm] * 12 + [hb, hb, hb, hb, vm, vm],
+        out_specs=(vm,) * 7,
+        scratch_shapes=[
+            v((nb, tl, width), BF),
+            v((cols, rows), F32),
+            v((nb, rows, 3 * cols), BF),
+            v((2 * nb, tl, width), BF),
+            v((2 * nb, tl, width), BF),
+            v((nb, tl, width), BF),
+            v((nb, tl, width), BF),
+            v((nb, tl, width), F32),
+            v((rows, cols), BF),
+            v((hidden, width), BF),
+            v((width, hidden), BF),
+            v((cols, width), BF),
+            v((width, 3 * cols), BF),
+            v((4, cols, width), BF),
+            v((2, cols, width), BF),
+            v((cols, width), BF),
+            v((cols, width), BF),
+            v((2, hidden // 2, pc), BF),
+            v((6, hidden, pc), BF),
+            v((2, pc // 2, hidden), BF),
+            v((6, pc, hidden), BF),
+            v((2, cols // 2, pc), BF),
+            v((6, cols, pc), BF),
+            v((2, pc // 2, 3 * cols), BF),
+            v((6, pc, 3 * cols), BF),
+            v((4, nb, 2 * width), F32),
+            v((nd, nb, 2 * width + TF), F32),
+            dma((3,)),
+            dma((21,)),
+            dma((21,)),
+            dma((32,)),
+            dma((32,)),
+        ],
+        compiler_params=pltpu.CompilerParams(
+            collective_id=2, has_side_effects=True, vmem_limit_bytes=VMEM_LIMIT
+        ),
+        name="attention_backward",
+    )(
+        qkv, lse, own, d_heads, w, h_one, tokens, modul, cs, sn, d_mid, base, osend,
+        g_down, g_up, g_out, dsc_two, feats,
+    )
+
+
+def order_columns(w):
+    rows = w.shape[0]
+    heads = w.shape[1] // (3 * HD)
+    w = w.reshape(rows, heads, 3, HD)
+    turned = w[:, :, 0:2].reshape(rows, heads, 2, 2, HD // 2)
+    turned = jnp.transpose(turned, (0, 2, 3, 1, 4)).reshape(rows, 2 * heads * HD)
+    return jnp.concatenate([turned, w[:, :, 2].reshape(rows, heads * HD)], axis=1)
+
+
+def restore_columns(w):
+    rows = w.shape[0]
+    heads = w.shape[1] // (3 * HD)
+    turned = w[:, : 2 * heads * HD].reshape(rows, 2, 2, heads, HD // 2)
+    turned = jnp.transpose(turned, (0, 3, 1, 2, 4)).reshape(rows, heads, 2, HD)
+    values = w[:, 2 * heads * HD :].reshape(rows, heads, 1, HD)
+    return jnp.concatenate([turned, values], axis=2).reshape(rows, heads * 3 * HD)
+
+
+def fast_shards(nd, tokens, bins, plan, w_qkv, w_out, w_up, w_down, w_time, cotangent):
+    s = lax.axis_index("seq")
+    nb, tl, width = tokens.shape
+    rows = 4 * tl
+    feats = time_features(plan, bins).astype(BF).astype(F32)
+    depth = w_time.shape[0]
+    table = feats.reshape(nb, nd, 4, depth)
+    fs = lax.dynamic_index_in_dim(table, s, axis=2, keepdims=False)[:, :, :, None]
+    half = HD // 2
+    inverse = jnp.exp(jnp.arange(half, dtype=F32) * (-math.log(10000.0) / half))
+    angle = jnp.arange(rows, dtype=F32)[:, None] * inverse[None, :]
+    cs = jnp.tile(jnp.cos(angle), (1, 128 // half))
+    sn = jnp.tile(jnp.sin(angle), (1, 128 // half))
+    (
+        tok_all, modul, full_qkv, full_out, full_up, full_down,
+        h_one, qkv, lse, own, attn_all, cot_all,
+    ) = run_k1(
+        nd, tokens, w_time, fs, order_columns(w_qkv), w_out, w_up, w_down, cs, sn, cotangent
+    )
+    grad_down, grad_up, grad_out, d_mid, base, osend, d_heads, dsc_two = run_k2(
+        tok_all, attn_all, cot_all, modul, full_out, full_up, full_down
+    )
+    output, grad_tokens, sum_qkv, sum_out, sum_up, sum_down, grad_time = run_k3(
+        nd, qkv, lse, own, d_heads, full_qkv, h_one, tokens, modul, cs, sn, d_mid, base, osend,
+        grad_down, grad_up, grad_out, dsc_two, feats,
+    )
+    return (
+        output, grad_tokens, restore_columns(sum_qkv), sum_out, sum_up, sum_down, grad_time
+    )
+
+
 def solution(mesh):
+    nd, ns = mesh.shape["dp"], mesh.shape["seq"]
+    fast = nd == 8 and ns == 4
     return jax.shard_map(
-        shards,
+        functools.partial(fast_shards, nd) if fast else shards,
         mesh=mesh,
         in_specs=(
             P("dp", "seq", None),

time: 1380 us -> 246 us (0.18)
  waiting for transfers between devices: 941 us -> 0 us
  Pallas kernels: 0 us -> 230 us
  matrix products: 152 us -> 0 us
  local copies, waits for them, and re-layouts: 118 us -> 11.3 us
  blocking collectives: 76.8 us -> 0 us
  other arithmetic: 63.7 us -> 3.12 us
  between operations: 15 us -> 0.82 us
    reduce_scatter x7 -> x0, waiting for transfers between devices: 422 us -> none  [the longest x1 152 us: data_layer(): lax.psum_scatter(grad_up.astype(jnp.bfloat16), 'dp', scatter_dimension=0,...]
    all_gather x7 -> x0, waiting for transfers between devices: 322 us -> none  [the longest x1 111 us: data_layer(): lax.all_gather(wide[3], 'dp', axis=1, tiled=True)]
    pallas_call x0 -> x3, Pallas kernels: none -> 230 us  [the longest x1 87.1 us: run_k3(): pl.pallas_call(k3_body, out_shape=(sds((nb, tl, width), BF), sds((nb, tl,...]
    unnamed x18 -> x0, waiting for transfers between devices: 155 us -> none
    dot_general x42 -> x0, matrix products: 152 us -> none  [the longest x1 14.4 us: data_layer(): jnp.einsum('std,df->stf', h_two, full_up, preferred_element_type=jnp.floa...]
    all_to_all x2 -> x0, blocking collectives: 56.8 us -> none  [the longest x1 39.6 us: data_layer(): lax.all_to_all(grad_packed_heads, 'seq', split_axis=1, concat_axis=2, til...]
    all_to_all x2 -> x0, waiting for transfers between devices: 42.7 us -> none  [the longest x1 36.1 us: data_layer(): lax.all_to_all(packed, 'seq', split_axis=2, concat_axis=1, tiled=True)]
    convert_element_type x12 -> x1, other arithmetic: 43.1 us -> 0.59 us  [fast_shards(): feats = time_features(plan, bins).astype(BF).astype(F32)]
  transfers between devices with their start and end apart: 18 -> 0, of which waited for: 14 -> 0; matrix products, arithmetic and copies ran while one was open for 21% -> 0% of each run, Pallas kernels for 0% -> 0%
where the time goes in v1:
time: 246 us; the launch traced here: 245 us
  Pallas kernels  230 us (93%)
  local copies, waits for them, and re-layouts  11.3 us (5%)
  other arithmetic  3.12 us (1%)
    pallas_call x1, Pallas kernels, run_k3(): pl.pallas_call(k3_body, out_shape=(sds((nb, tl, width), BF), sds((nb, tl,...  87.1 us
    pallas_call x1, Pallas kernels, run_k1(): pl.pallas_call(k1_body, out_shape=(sds((nb, 4, tl, width), BF), sds((nb,...  86.7 us
    pallas_call x1, Pallas kernels, run_k2(): pl.pallas_call(k2_body, out_shape=(sds((hidden, width), BF), sds((width,...  56.3 us
    unnamed x22, local copies, waits for them, and re-layouts  5.91 us

profile of v1, /device:TPU:0, one launch (start us, length us, event | category | flops | bytes accessed | tf_op | source)
XLA Modules:
  0.0 245.4 jit_solution(1239592333490011480)
XLA Ops:
  0.6 0.0 copy-start.4
  0.6 0.9 fusion.7
  1.6 0.2 fusion.3
  1.8 0.8 copy.37.fs
  2.6 0.5 fusion
  3.2 1.0 copy.38.cs
  4.3 1.0 copy.39.sn
  5.3 0.0 copy-done.4
  5.3 0.2 copy.33
  5.5 0.1 copy.35
  5.6 0.1 copy.36
  5.7 0.7 pad_maximum_fusion.1.w_qkv
  6.4 86.7 %attention_forward.1 = (bf16[2,4,256,1024]{3,2,1,0:T(8,128)(2,1)}, f32[2,2048]{1,0:T(2,128)}, bf16[1024,768]{1,0:T(8,128)(2,1)}, bf16[1024,1024]{1,0:T(8,128)(2,...) custom-call(bf16[2,256,1024]{2,1,0:T(8,128)(2,1)} %tok.3, ...), custom_call_target="tpu_custom_call" | custom-call | tf_op jit(solution)/shard_map/attention_forward/pallas_call | solution.py:664
  93.1 56.3 %feed_forward.1 = (bf16[1024,1024]{1,0:T(8,128)(2,1)}, bf16[1024,1024]{1,0:T(8,128)(2,1)}, bf16[4,256,1024]{2,1,0:T(8,128)(2,1)}, f32[2,256,1024]{2,1,0:T(8,128)...) custom-call(bf16[2,4,256,1024]{3,2,1,0:T(8,128)(2,1)} %get-tuple-ele, ...), custom_call_target="tpu_custom_call" | custom-call | tf_op jit(solution)/shard_map/feed_forward/pallas_call | solution.py:850
  149.4 0.1 fusion.5
  149.6 0.6 maximum_convert_fusion.feats
  150.1 87.1 %attention_backward.1 = (bf16[2,256,1024]{2,1,0:T(8,128)(2,1)}, bf16[2,256,1024]{2,1,0:T(8,128)(2,1)}, f32[128,768]{1,0:T(8,128)}, f32[256,128]{1,0:T(8,128)}, f...) custom-call(bf16[2,3,1024,256]{3,2,1,0:T(8,128)(2,1)} %get-tuple-element.34.qkv, ...), custom_call_target="tpu_custom_call" | custom-call | tf_op jit(solution)/shard_map/attention_backward/pallas_call | solution.py:1149
  237.2 0.0 copy-start.1
  237.2 1.1 slice.14
  238.3 0.1 copy.42
  238.5 0.0 copy-start
  238.5 1.0 slice.15
  239.5 0.1 copy.44
  239.6 0.9 copy.46
  240.5 0.0 copy-done.1
  240.5 1.0 copy.53
  241.5 1.0 copy.54
  242.5 0.7 copy.55
  243.1 0.0 copy-done.3
  243.1 0.8 copy.56
  243.9 0.8 copy.57
  244.7 0.6 copy.58
  (20 shorter events, 0.2 us)
Async XLA Ops:
  0.6 4.6 %copy-start.4 = (bf16[128,768]{1,0:T(8,128)(2,1)S(1)}, bf16[128,768]{1,0:T(8,128)(2,1)}, u32[]{:S(2)}) copy-start(bf16[128,768]{1,0:T(8,128)(2,1)} %param.12) | copy-start | bytes 589828
  237.2 3.3 %copy-start.1 = (bf16[2,256,1024]{2,1,0:T(8,128)(2,1)S(1)}, bf16[2,256,1024]{2,1,0:T(8,128)(2,1)}, u32[]{:S(2)}) copy-start(bf16[2,256,1024]{2,1,0:T(8,128)(2,1)} %get-tuple-element.88) | copy-start | bytes 3145732
  238.5 3.0 %copy-start = (bf16[2,256,1024]{2,1,0:T(8,128)(2,1)S(1)}, bf16[2,256,1024]{2,1,0:T(8,128)(2,1)}, u32[]{:S(2)}) copy-start(bf16[2,256,1024]{2,1,0:T(8,128)(2,1)} %get-tuple-element.89) | copy-start | bytes 3145732
  240.5 2.0 copy-start.5
  240.5 2.6 %copy-start.3 = (f32[128,1024]{1,0:T(8,128)S(1)}, f32[128,1024]{1,0:T(8,128)}, u32[]{:S(2)}) copy-start(f32[128,1024]{1,0:T(8,128)} %get-tuple-element.92) | copy-start | bytes 1572868
  241.5 2.4 copy-start.2
  241.5 3.2 %copy-start.6 = (f32[8,2048]{1,0:T(8,128)S(1)}, f32[8,2048]{1,0:T(8,128)}, u32[]{:S(2)}) copy-start(f32[8,2048]{1,0:T(8,128)} %get-tuple-element.94) | copy-start | bytes 196612

commit v2 on v1

--- a/solution.py
+++ b/solution.py
@@ -282,6 +282,7 @@
 BF = jnp.bfloat16
 F32 = jnp.float32
 MESHID = pl.DeviceIdType.MESH
+QUERY_SCALE = HD**-0.5 / math.log(2.0)
 VMEM_LIMIT = 60 * 1024 * 1024
 
 
@@ -422,17 +423,18 @@
 
 def k1_body(
     tok, wt, fs, w_qkv, w_out, w_up, w_down, cs, sn, cot,
-    tok_all, modul, wq, out_all, up_all, down_all, h_out, qkv, lse, own, attn_all, cot_all,
-    tokv, wtime, pbuf, ls, ss, rs, gs, gr, fs_, fr_,
+    modul, wq_out, out_all, up_all, down_all, n_out, qkv_out, lse, attn_heads, attn_rows, cot_all,
+    act_out, slope_out, htwo_out, mid_out,
+    tokv, wtime, pbuf, vt, cotv, wq, nv, qkv, attn, outv, upv, act, slope, htwo, mids, csv, snv,
+    ks, ls, ss, rs, gs, gr, fs_, fr_, os_,
 ):
     g, s, core, s1, s2, s3 = peers()
     p = ring_place(g)
-    greet([(g, s1), (g, s2), (g, s3), (ring_index(p + 1), s), (ring_index(p - 1), s)])
     nb, tl = tok.shape[0], tok.shape[1]
     rows = 4 * tl
     blk = 256
     nq = rows // blk
-    heads = own.shape[2] // HD
+    heads = attn.shape[3] // HD
     nr, nc = w_out.shape[0], w_out.shape[1]
 
     def lanes(j, size):
@@ -441,7 +443,7 @@
     def view_out(other):
         def view(j, half):
             lo, size = (0, nr) if half is None else (half * (nr // 2), nr // 2)
-            return out_all.at[pl.ds(pl.multiple_of(other * nr + lo, size), size), lanes(j, nc)]
+            return outv.at[pl.ds(pl.multiple_of(other * nr + lo, size), size), lanes(j, nc)]
 
         return view
 
@@ -460,41 +462,73 @@
     def view_time(j, half):
         return wtime.at[j] if half is None else wtime.at[j, :, half * D : (half + 1) * D]
 
+    def view_qkv(side):
+        size = w_qkv.shape[0]
+
+        def view(j, half):
+            lo, n = (0, size // 2) if half is None else (half * (size // 4), size // 4)
+            at = pl.multiple_of(j * size + side * (size // 2) + lo, n)
+            return wq.at[pl.ds(at, n)]
+
+        return view
+
     here = view_out(s)(g, None)
     time_ring = Gather(wt, view_time, gs, gr, 0)
-    qkv_ring = Gather(w_qkv, view_rows(wq, w_qkv.shape[0]), gs, gr, 8)
-    up_ring = Gather(w_up, view_rows(up_all, w_up.shape[0]), gs, gr, 16)
+    part = w_qkv.shape[0] // 2
+    qkv_rings = [
+        Gather(w_qkv.at[i * part : (i + 1) * part], view_qkv(i), gs, gr, 8 + 40 * i)
+        for i in range(2)
+    ]
+    up_ring = Gather(w_up, view_rows(upv, w_up.shape[0]), gs, gr, 16)
     down_ring = Gather(w_down, view_down, gs, gr, 24)
     out_ring = Gather(w_out, view_out(s), gs, gr, 32)
     far_ring = Gather(view_out(s2)(g, None), view_out(s2), gs, gr, 40)
 
+    local = [
+        pltpu.make_async_copy(tok, tokv.at[:, s], ls.at[0]),
+        pltpu.make_async_copy(w_qkv, view_rows(wq, w_qkv.shape[0])(g, None), ls.at[1]),
+        pltpu.make_async_copy(w_up, view_rows(upv, w_up.shape[0])(g, None), ls.at[2]),
+        pltpu.make_async_copy(w_down, view_down(g, None), ls.at[3]),
+        pltpu.make_async_copy(w_out, here, ls.at[4]),
+        pltpu.make_async_copy(cot, cotv, ls.at[5]),
+        pltpu.make_async_copy(cs, csv, ls.at[6]),
+        pltpu.make_async_copy(sn, snv, ls.at[7]),
+    ]
+    greet([(g, s1), (g, s2), (g, s3), (ring_index(p + 1), s), (ring_index(p - 1), s)])
     time_ring.start()
-    qkv_ring.start()
+    for ring in qkv_rings:
+        ring.start()
+    out_ring.start()
     pair_out = remote(w_out, here, ss, rs, 0, (g, s2))
     pair_out.start()
-    far, near, passed = [], [], []
-    for b in range(nb):
-        cp = remote(tok.at[b], tokv.at[b, s], ss, rs, 1 + b, (g, s2))
-        cp.start()
-        far.append(cp)
+    far = [remote(tok.at[b], tokv.at[b, s], ss, rs, 1 + b, (g, s2)) for b in range(nb)]
+    near = []
+    far[0].start()
     for b in range(nb):
         cp = remote(tok.at[b], tokv.at[b, s], ss, rs, 3 + b, (g, s1))
         cp.start()
         near.append(cp)
-    local = [
-        pltpu.make_async_copy(tok, tokv.at[:, s], ls.at[0]),
-        pltpu.make_async_copy(w_qkv, view_rows(wq, w_qkv.shape[0])(g, None), ls.at[1]),
-        pltpu.make_async_copy(w_up, view_rows(up_all, w_up.shape[0])(g, None), ls.at[2]),
-        pltpu.make_async_copy(w_down, view_down(g, None), ls.at[3]),
-        pltpu.make_async_copy(w_out, here, ls.at[4]),
-        pltpu.make_async_copy(cot, cot_all.at[:, s], ls.at[5]),
-    ]
     for cp in local:
         cp.start()
     wtime[g] = wt[...]
+    half_rows = tl // 2
+
+    def cot_piece(k):
+        r = slice((k % 2) * half_rows, (k % 2 + 1) * half_rows)
+        return remote(
+            cotv.at[k // 2, r], cot_all.at[k // 2, s, r], ss, rs, 18 + k, (g, s2)
+        )
+
+    local[5].wait()
+    cot_far = [cot_piece(k) for k in range(2 * nb)]
+    cot_far[0].start()
     for k in (2, 3, 4):
         time_ring.forward(k)
-        qkv_ring.forward(k)
+        for ring in qkv_rings:
+            ring.forward(k)
+        out_ring.forward(k)
+    pair_out.wait_recv()
+    far_ring.start()
     up_ring.start()
     time_ring.arrive()
     weights = wtime[...].astype(F32)
@@ -507,47 +541,42 @@
         cp = remote(pbuf.at[0], pbuf.at[e], ss, rs, 4 + e, (g, other))
         cp.start()
         small.append(cp)
-    down_ring.start()
-    out_ring.start()
-    pair_out.wait_recv()
-    far_ring.start()
-    for b in range(nb):
-        far[b].wait_recv()
-        cp = remote(tokv.at[b, s2], tokv.at[b, s2], ss, rs, 8 + b, (g, s1))
-        cp.start()
-        passed.append(cp)
-        if b == 0:
-            for c in small:
-                c.wait_recv()
-            modul[...] = (pbuf[0] + pbuf[1]) + (pbuf[2] + pbuf[3])
-            qkv_ring.arrive()
-            local[0].wait()
-            local[1].wait()
-    cot_far, cot_near, cot_pass = [], [], []
-    for b in range(nb):
-        cp = remote(cot.at[b], cot_all.at[b, s], ss, rs, 10 + b, (g, s2))
-        cp.start()
-        cot_far.append(cp)
-    for b in range(nb):
-        cp = remote(cot.at[b], cot_all.at[b, s], ss, rs, 12 + b, (g, s1))
-        cp.start()
-        cot_near.append(cp)
-    for cp in near + passed:
-        cp.wait_recv()
-    keep_tok = pltpu.make_async_copy(tokv, tok_all, ls.at[6])
-    keep_tok.start()
+    far[1].start()
+    cot_far[1].start()
+    passed = [
+        remote(tokv.at[b, s2], tokv.at[b, s2], ss, rs, 8 + b, (g, s1)) for b in range(nb)
+    ]
+    cot_near = [remote(cotv.at[b], cot_all.at[b, s], ss, rs, 12 + b, (g, s1)) for b in range(nb)]
+    cot_pass = [
+        remote(cot_all.at[b, s2], cot_all.at[b, s2], ss, rs, 14 + b, (g, s1)) for b in range(nb)
+    ]
+    far[0].wait_recv()
+    passed[0].start()
+    for c in small:
+        c.wait_recv()
+    modul[...] = (pbuf[0] + pbuf[1]) + (pbuf[2] + pbuf[3])
+    for ring in qkv_rings:
+        ring.arrive()
+    for i in (0, 1, 6, 7):
+        local[i].wait()
+    keep_w = pltpu.make_async_copy(wq, wq_out, ls.at[8])
+    keep_w.start()
+    keep_cot = pltpu.make_async_copy(cotv, cot_all.at[:, s], ls.at[9])
+    keep_cot.start()
 
     def attn_copy(kind, it):
         b, q = it // nq, lax.rem(it, nq)
         r = pl.ds(pl.multiple_of(q * blk, blk), blk)
-        if kind == 2:
-            ref = attn_all.at[b, s2, r]
-            return remote(ref, ref, fs_.at[2], fr_.at[2], it, (g, s1))
-        return remote(
-            own.at[b, r], attn_all.at[b, s, r], fs_.at[kind], fr_.at[kind], it, (g, (s2, s1)[kind])
+        ref = attn.at[b, s2 if kind == 2 else s, r]
+        return remote(ref, ref, fs_.at[kind], fr_.at[kind], it, (g, s2 if kind == 0 else s1))
+
+    lane = lax.broadcasted_iota(jnp.int32, (1, 2 * 128), 1)
+
+    def keep_fields(b):
+        return (
+            pltpu.make_async_copy(nv.at[b], n_out.at[b], ks.at[0, b]),
+            pltpu.make_async_copy(qkv.at[b], qkv_out.at[b], ks.at[1, b]),
         )
-
-    lane = lax.broadcasted_iota(jnp.int32, (1, 2 * 128), 1)
 
     def project(b):
         scale = 1.0 + modul[pl.ds(b, 1), :D]
@@ -555,11 +584,10 @@
         def one(i, _):
             r = pl.ds(pl.multiple_of(i * blk, blk), blk)
             normed, _inv = moments(tokv[b, i].astype(F32))
-            h = (normed * scale).astype(BF)
-            h_out[b, r] = h
-            raw = mm(h, wq[...])
-            c, n = cs[r], sn[r]
-            qa, qb = raw[:, :128] * 0.125, raw[:, 128:256] * 0.125
+            nv[b, r] = normed.astype(BF)
+            raw = mm((normed * scale).astype(BF), wq[...])
+            c, n = csv[r], snv[r]
+            qa, qb = raw[:, :128] * QUERY_SCALE, raw[:, 128:256] * QUERY_SCALE
             ka, kb = raw[:, 256:384], raw[:, 384:512]
             qkv[b, 0, r] = jnp.concatenate([qa * c - qb * n, qb * c + qa * n], axis=1).astype(BF)
             qkv[b, 1, r] = jnp.concatenate([ka * c - kb * n, kb * c + ka * n], axis=1).astype(BF)
@@ -568,87 +596,181 @@
 
         lax.fori_loop(0, nq, one, 0)
 
+    def pass_attn(lo, hi):
+        def forward(it, _):
+            attn_copy(0, it).wait_recv()
+            attn_copy(2, it).start()
+            return 0
+
+        lax.fori_loop(lo, hi, forward, 0)
+
+    def arrive_attn(lo, hi):
+        def forward(it, _):
+            attn_copy(1, it).wait_recv()
+            attn_copy(2, it).wait_recv()
+            return 0
+
+        lax.fori_loop(lo, hi, forward, 0)
+
+    def tokens_of(b):
+        near[b].wait_recv()
+        passed[b].wait_recv()
+
+    def second_tokens():
+        far[1].wait_recv()
+        passed[1].start()
+
     def step(it, _):
         b, q = it // nq, lax.rem(it, nq)
+        for i in range(nb):
+
+            @pl.when(it == i * nq)
+            def _(i=i):
+                tokens_of(i)
 
         @pl.when(q == 0)
         def _():
             project(b)
-
-        for when, ring, k in (
-            (1, up_ring, 2), (2, down_ring, 2), (2, out_ring, 2), (3, far_ring, 2),
-            (4, up_ring, 3), (5, down_ring, 3), (5, out_ring, 3), (6, far_ring, 3),
-            (7, up_ring, 4),
+            vt[...] = qkv[b, 2].T
+            for cp in keep_fields(b):
+                cp.start()
+
+        for when, action in (
+            (1, lambda: up_ring.forward(2)),
+            (1, lambda: far_ring.forward(2)),
+            (2, second_tokens),
+            (3, lambda: up_ring.forward(3)),
+            (3, lambda: far_ring.forward(3)),
+            (4, lambda: up_ring.forward(4)),
+            (4, down_ring.start),
+            (5, lambda: far_ring.forward(4)),
+            (6, lambda: pass_attn(0, nq)),
         ):
 
             @pl.when(it == when)
-            def _(ring=ring, k=k):
-                ring.forward(k)
+            def _(action=action):
+                action()
 
         r = pl.ds(pl.multiple_of(q * blk, blk), blk)
-        query = qkv[b, 0, r]
-        keys, values = qkv[b, 1], qkv[b, 2]
-        out = jnp.zeros((blk, heads * HD), F32)
-        stats = jnp.zeros((blk, 128), F32)
+        query, keys = qkv[b, 0, r], qkv[b, 1]
+        outs, stats = [], []
         for h in range(heads):
             mask = lax.rem(lane, 128) // 32 == h
-            scores = mm_nt(jnp.where(mask, query, jnp.zeros_like(query)), keys)
-            top = jnp.max(scores, axis=1, keepdims=True)
-            expo = jnp.exp(scores - top)
-            total = jnp.sum(expo, axis=1, keepdims=True)
-            res = mm(expo.astype(BF), values) * (1.0 / total)
-            out = jnp.where(lane // HD == h, res, out)
-            stats = jnp.where(lane[:, :128] == h, top + jnp.log(total), stats)
-        own[b, r] = out.astype(BF)
-        lse[b, :, r] = stats.T[:8]
+            scores = mm_nt(keys, jnp.where(mask, query, jnp.zeros_like(query)))
+            top = jnp.max(scores, axis=0, keepdims=True)
+            expo = jnp.exp2(scores - top)
+            total = jnp.sum(expo, axis=0, keepdims=True)
+            outs.append(mm(vt[h * HD : (h + 1) * HD], expo.astype(BF)) * (1.0 / total))
+            stats.append(top + jnp.log2(total))
+        attn[b, s, r] = jnp.concatenate(outs, axis=0).T.astype(BF)
+        lse[b, :, r] = jnp.concatenate(stats + [jnp.zeros((8 - heads, blk), F32)], axis=0)
         attn_copy(0, it).start()
         attn_copy(1, it).start()
         return 0
 
     lax.fori_loop(0, nb * nq, step, 0)
-    keep = pltpu.make_async_copy(own, attn_all.at[:, s], ls.at[7])
+    for cp in cot_far[2:] + cot_near:
+        cp.start()
+    keep = pltpu.make_async_copy(attn.at[:, s], attn_heads, ls.at[10])
     keep.start()
-    for ring in (down_ring, out_ring, far_ring):
-        ring.forward(4)
-    for b in range(nb):
-        cot_far[b].wait_recv()
-        cp = remote(cot_all.at[b, s2], cot_all.at[b, s2], ss, rs, 14 + b, (g, s1))
-        cp.start()
-        cot_pass.append(cp)
-
-    def forward(it, _):
-        attn_copy(0, it).wait_recv()
-        attn_copy(2, it).start()
-        return 0
-
-    lax.fori_loop(0, nb * nq, forward, 0)
-    for ring in (up_ring, down_ring, out_ring, far_ring):
-        ring.arrive()
+    out_ring.arrive()
+    far_ring.arrive()
     local[4].wait()
     cross = []
     for e, other in ((0, s), (1, s2)):
-        ref = out_all.at[pl.ds(pl.multiple_of(other * nr, nr), nr)]
+        ref = outv.at[pl.ds(pl.multiple_of(other * nr, nr), nr)]
         cp = remote(ref, ref, ss, rs, 16 + e, (g, s1))
         cp.start()
         cross.append(cp)
+    up_ring.arrive()
+    local[2].wait()
+    for cp in cross:
+        cp.wait_recv()
+    arrive_attn(0, nq)
+    keep_out = pltpu.make_async_copy(outv, out_all, ls.at[11])
+    keep_out.start()
+    keep_up = pltpu.make_async_copy(upv, up_all, ls.at[12])
+    keep_up.start()
+
+    def keep_block(i):
+        return (
+            pltpu.make_async_copy(act.at[i], act_out.at[i], os_.at[0, i]),
+            pltpu.make_async_copy(slope.at[i], slope_out.at[i], os_.at[1, i]),
+            pltpu.make_async_copy(htwo.at[i], htwo_out.at[i], os_.at[2, i]),
+        )
+
+    def feed(i, _):
+        b, owner = i // 4, lax.rem(i, 4)
+        for when, action in (
+            (1, lambda: down_ring.forward(2)),
+            (3, lambda: pass_attn(nq, 2 * nq)),
+            (3, lambda: down_ring.forward(3)),
+            (4, lambda: arrive_attn(nq, 2 * nq)),
+            (6, lambda: down_ring.forward(4)),
+        ):
+
+            @pl.when(i == when)
+            def _(action=action):
+                action()
+
+        scale = 1.0 + modul[pl.ds(b, 1), D:]
+        r = pl.ds(pl.multiple_of(owner * tl, tl), tl)
+        joined = jnp.concatenate([attn[b, j, r] for j in range(4)], axis=1)
+        mid = tokv[b, owner].astype(F32) + mm(joined, outv[...])
+        normed, _inv = moments(mid)
+        h = (normed * scale).astype(BF)
+        upper = mm(h, upv[...])
+        phi = 0.5 * (1.0 + lax.erf(upper * ROOT_HALF))
+        act[i] = (upper * phi).astype(BF)
+        slope[i] = (phi + upper * (DENSITY * jnp.exp(-0.5 * upper * upper))).astype(BF)
+        htwo[i] = h
+
+        @pl.when(owner == s)
+        def _():
+            mids[b] = mid
+
+        for cp in keep_block(i):
+            cp.start()
+        return 0
+
+    lax.fori_loop(0, 4 * nb, feed, 0)
+    keep_mid = pltpu.make_async_copy(mids, mid_out, ls.at[13])
+    keep_mid.start()
+    own_rows = pl.ds(pl.multiple_of(s * tl, tl), tl)
+    keep_rows = pltpu.make_async_copy(attn.at[:, :, own_rows], attn_rows, ls.at[14])
+    keep_rows.start()
+    for b in range(nb):
+        cot_far[2 * b].wait_recv()
+        cot_far[2 * b + 1].wait_recv()
+        cot_pass[b].start()
 
     def finish(it, _):
         attn_copy(0, it).wait_send()
-        attn_copy(1, it).wait()
-        attn_copy(2, it).wait()
+        attn_copy(1, it).wait_send()
+        attn_copy(2, it).wait_send()
         return 0
 
     lax.fori_loop(0, nb * nq, finish, 0)
-    for cp in cot_near + cot_pass + cross:
+
+    def kept(i, _):
+        for cp in keep_block(i):
+            cp.wait()
+        return 0
+
+    lax.fori_loop(0, 4 * nb, kept, 0)
+    down_ring.arrive()
+    for cp in cot_near + cot_pass:
         cp.wait()
-    for cp in cot_far + far + near + passed + small + [pair_out]:
+    for cp in cot_far + far + near + passed + small + cross + [pair_out]:
         cp.wait_send()
-    for ring in (time_ring, qkv_ring, up_ring, down_ring, out_ring, far_ring):
+    for ring in [time_ring, up_ring, down_ring, out_ring, far_ring] + qkv_rings:
         ring.drain()
-    for i in (2, 3, 5):
-        local[i].wait()
-    keep_tok.wait()
-    keep.wait()
+    local[3].wait()
+    for cp in (keep_cot, keep, keep_w, keep_out, keep_up, keep_mid, keep_rows):
+        cp.wait()
+    for b in range(nb):
+        for cp in keep_fields(b):
+            cp.wait()
 
 
 def run_k1(nd, tokens, w_time, fs, w_qkv, w_out, w_up, w_down, cs, sn, cot):
@@ -661,10 +783,10 @@
     steps = nb * (rows // 256)
     sds = jax.ShapeDtypeStruct
     dma = pltpu.SemaphoreType.DMA
+    v = pltpu.VMEM
     return pl.pallas_call(
         k1_body,
         out_shape=(
-            sds((nb, 4, tl, width), BF),
             sds((nb, 2 * width), F32),
             sds((width, 3 * cols), BF),
             sds((width, width), BF),
@@ -674,22 +796,42 @@
             sds((nb, 3, rows, cols), BF),
             sds((nb, 8, rows), F32),
             sds((nb, rows, cols), BF),
-            sds((nb, 4, rows, cols), BF),
+            sds((nb, 4, tl, cols), BF),
             sds((nb, 4, tl, width), BF),
+            sds((4 * nb, tl, hidden), BF),
+            sds((4 * nb, tl, hidden), BF),
+            sds((4 * nb, tl, width), BF),
+            sds((nb, tl, width), F32),
         ),
-        in_specs=[hb, vm, vm, hb, hb, hb, hb, vm, vm, hb],
-        out_specs=(hb, vm, vm, hb, hb, hb, vm, vm, vm, vm, hb, hb),
+        in_specs=[hb, vm, vm, hb, vm, vm, vm, hb, hb, hb],
+        out_specs=(vm, hb, hb, hb, hb, hb, hb, vm) + (hb,) * 7,
         scratch_shapes=[
-            pltpu.VMEM((nb, 4, tl, width), BF),
-            pltpu.VMEM((nd,) + w_time.shape, BF),
-            pltpu.VMEM((4, nb, 2 * width), F32),
-            dma((8,)),
-            dma((18,)),
-            dma((18,)),
-            dma((48,)),
-            dma((48,)),
+            v((nb, 4, tl, width), BF),
+            v((nd,) + w_time.shape, BF),
+            v((4, nb, 2 * width), F32),
+            v((cols, rows), BF),
+            v((nb, tl, width), BF),
+            v((width, 3 * cols), BF),
+            v((nb, rows, width), BF),
+            v((nb, 3, rows, cols), BF),
+            v((nb, 4, rows, cols), BF),
+            v((width, width), BF),
+            v((width, hidden), BF),
+            v((4 * nb, tl, hidden), BF),
+            v((4 * nb, tl, hidden), BF),
+            v((4 * nb, tl, width), BF),
+            v((nb, tl, width), F32),
+            v(cs.shape, F32),
+            v(sn.shape, F32),
+            dma((2, nb)),
+            dma((15,)),
+            dma((22,)),
+            dma((22,)),
+            dma((56,)),
+            dma((56,)),
             dma((3, steps)),
             dma((3, steps)),
+            dma((3, 4 * nb)),
         ],
         compiler_params=pltpu.CompilerParams(
             collective_id=0, has_side_effects=True, vmem_limit_bytes=VMEM_LIMIT
@@ -699,34 +841,65 @@
 
 
 def k2_body(
-    tok, attn, cot, modul, w_out, w_up, w_down,
-    grad_down, grad_up, grad_out, d_mid, base, osend, d_heads, dsc,
-    act, htwo, dup, mids, pa, pb_, ra, rb, xs, xr, dat, stage,
-    ls, ss, rs, gs,
+    act_h, slope_h, htwo_h, mid_h, attn_h, cot_h, modul, w_out_h, w_up_h, w_down_h,
+    grad_up, grad_out, d_mid_h, base_h, osend_h, d_heads, dsc, s_down,
+    act, dup, htwo, mids, attn, cot, w_out, w_up, w_down, d_mid, base, osend,
+    pa, pb_, ra, rb, xs, xr, dat, stage, gdv, down_h, down_w,
+    ls, ss, rs, os_, ins, keeps, bs, gs, gr,
 ):
     g, s, core, s1, s2, s3 = peers()
+    p = ring_place(g)
     chip = s // 2
-    greet([(g, s1), (g, s2), (g, s3)])
-    nb, tl = tok.shape[0], tok.shape[2]
-
-    def block(b, owner, slot):
-        scale = 1.0 + modul[pl.ds(b, 1), D:]
-        r = pl.ds(pl.multiple_of(owner * tl, tl), tl)
-        a = jnp.concatenate([attn[b, j, r] for j in range(4)], axis=1)
-        mid = tok[b, owner].astype(F32) + mm(a, w_out[...])
-        normed, _inv = moments(mid)
-        h = (normed * scale).astype(BF)
-        upper = mm(h, w_up[...])
-        phi = 0.5 * (1.0 + lax.erf(upper * ROOT_HALF))
-        active = (upper * phi).astype(BF)
-        slope = phi + upper * (DENSITY * jnp.exp(-0.5 * upper * upper))
+    nb, tl = cot.shape[0], cot.shape[2]
+
+    def pull(jp, which):
+        phase, b = jp // nb, lax.rem(jp, nb)
+        where = chip + (1 - phase) * (1 - 2 * chip)
+        owner = 2 * where + (1 - core if which == 0 else core)
+        i = b * 4 + owner
+        k = 2 * jp + which
+        return (
+            pltpu.make_async_copy(cot_h.at[b, owner], cot.at[b, owner], bs.at[0, k]),
+            pltpu.make_async_copy(slope_h.at[i], dup.at[i], bs.at[1, k]),
+            pltpu.make_async_copy(act_h.at[i], act.at[i], bs.at[2, k]),
+        )
+
+    loads = []
+    for i, (src, dst) in enumerate(
+        (
+            (w_down_h, w_down), (w_up_h, w_up),
+            (mid_h, mids), (w_out_h, w_out), (htwo_h, htwo), (attn_h, attn),
+        )
+    ):
+        loads.append(pltpu.make_async_copy(src, dst, ins.at[i]))
+    first = pull(0, 0)
+    loads[0].start()
+    for cp in first:
+        cp.start()
+    loads[1].start()
+    for jp in range(2 * nb):
+        for which in (0, 1):
+            if jp + which:
+                for cp in pull(jp, which):
+                    cp.start()
+    for cp in loads[2:]:
+        cp.start()
+    greet([(g, s1), (g, s2), (g, s3), (ring_index(p + 1), s), (ring_index(p - 1), s)])
+    hidden = act.shape[2]
+    pc = s_down.shape[1]
+
+    def view_down(j, half):
+        lo, n = (0, hidden) if half is None else (half * (hidden // 2), hidden // 2)
+        return gdv.at[lo : lo + n, pl.ds(pl.multiple_of(j * pc, pc), pc)]
+
+    down_ring = Scatter(view_down, down_h, down_w, gs, gr, 0)
+
+    def block(b, owner):
+        i = b * 4 + owner
         d_act = mm_nt(cot[b, owner], w_down[...])
-        d_up = (d_act * slope).astype(BF)
-        i = b * 4 + owner
-        act[i] = active
-        htwo[i] = h
+        d_up = (d_act * dup[i].astype(F32)).astype(BF)
         dup[i] = d_up
-        return mid, mm_nt(d_up, w_up[...]), mm(active, w_down[...])
+        return mm_nt(d_up, w_up[...]), mm(act[i], w_down[...])
 
     def pair_copies(jp):
         return (
@@ -737,18 +910,36 @@
     def far_copy(b):
         return remote(xs.at[b], xr.at[b], ss, rs, 8 + b, (g, s2))
 
-    def pair(jp, _):
+    def place(jp):
         phase, b = jp // nb, lax.rem(jp, nb)
-        where = chip + (1 - phase) * (1 - 2 * chip)
-        _mid, dh, out = block(b, 2 * where + 1 - core, jp)
+        return phase, b, chip + (1 - phase) * (1 - 2 * chip)
+
+    def give(jp, _):
+        phase, b, where = place(jp)
+
+        @pl.when(phase == 0)
+        def _():
+            for cp in pull(jp, 0):
+                cp.wait()
+
+        dh, out = block(b, 2 * where + 1 - core)
         pa[jp] = dh.astype(BF)
         pb_[jp] = out.astype(BF)
-        ca, cb = pair_copies(jp)
-        ca.start()
-        cb.start()
-        mid, dh, out = block(b, 2 * where + core, jp)
-        ca.wait_recv()
-        cb.wait_recv()
+        for cp in pair_copies(jp):
+            cp.start()
+        return 0
+
+    def take(jp, _):
+        phase, b, where = place(jp)
+
+        @pl.when(phase == 0)
+        def _():
+            for cp in pull(jp, 1):
+                cp.wait()
+
+        dh, out = block(b, 2 * where + core)
+        for cp in pair_copies(jp):
+            cp.wait_recv()
         dh = dh + ra[jp].astype(F32)
         out = out + rb[jp].astype(F32)
 
@@ -761,12 +952,29 @@
         @pl.when(phase == 1)
         def _():
             d_mid[b] = dh
-            mids[b] = mid
-            base[b] = out + mid
+            base[b] = out + mids[b]
 
         return 0
 
-    lax.fori_loop(0, 2 * nb, pair, 0)
+    def down_grads(i, _):
+        r = pl.ds(pl.multiple_of(i * 256, 256), 256)
+        left = act[:, :, r].reshape(4 * nb * tl, 256)
+        gdv[r] = mm_tn(left, cot[...].reshape(4 * nb * tl, D)).astype(BF)
+        return 0
+
+    def up_copy(i):
+        r = pl.ds(pl.multiple_of(i * 256, 256), 256)
+        return pltpu.make_async_copy(stage.at[i], grad_up.at[r], os_.at[i])
+
+    def up_grads(i, _):
+        r = pl.ds(pl.multiple_of(i * 256, 256), 256)
+        left = htwo[:, :, r].reshape(4 * nb * tl, 256)
+        stage[i] = mm_tn(left, dup[...].reshape(4 * nb * tl, hidden)).astype(BF)
+        up_copy(i).start()
+        return 0
+
+    def spread(e, other, b):
+        return remote(dat.at[other, b], d_heads.at[s, b], ss, rs, 10 + 2 * e + b, (g, other))
 
     def tail(b, _):
         scale = 1.0 + modul[pl.ds(b, 1), D:]
@@ -780,51 +988,48 @@
             dn - jnp.mean(dn, axis=-1, keepdims=True) - normed * inner
         )
         d_mid[b] = dm
-        branch = dm.astype(BF)
-        xs2 = mm_nt(branch, w_out[...]).astype(BF)
+        branch = mm_nt(dm.astype(BF), w_out[...]).astype(BF)
         for j in range(4):
-            dat[j, b] = xs2[:, j * 256 : (j + 1) * 256]
+            dat[j, b] = branch[:, j * 256 : (j + 1) * 256]
+        for e, other in ((0, s2), (1, s3), (2, s1)):
+            spread(e, other, b).start()
         return 0
 
-    lax.fori_loop(0, nb, tail, 0)
-    copies = []
-    for e, other in ((2, s2), (3, s3), (1, s1)):
-        cp = remote(dat.at[other], d_heads.at[s], ss, rs, 9 + e, (g, other))
+    for cp in loads[:2]:
+        cp.wait()
+    half = D // 512
+    lax.fori_loop(0, nb, give, 0)
+    lax.fori_loop(0, nb, take, 0)
+    for jp in range(nb, 2 * nb):
+        for which in (0, 1):
+            for cp in pull(jp, which):
+                cp.wait()
+    lax.fori_loop(0, hidden // 256, down_grads, 0)
+    down_ring.start()
+    for cp in loads[2:]:
+        cp.wait()
+    lax.fori_loop(nb, 2 * nb, give, 0)
+    lax.fori_loop(nb, 2 * nb, take, 0)
+    down_ring.forward(2)
+    lax.fori_loop(0, nb - 1, tail, 0)
+    lax.fori_loop(0, half, up_grads, 0)
+    down_ring.forward(3)
+    lax.fori_loop(nb - 1, nb, tail, 0)
+    lax.fori_loop(half, 2 * half, up_grads, 0)
+    keep_all = []
+    for i, (src, dst) in enumerate(
+        ((d_mid, d_mid_h), (base, base_h), (osend, osend_h), (dat.at[s], d_heads.at[s]))
+    ):
+        cp = pltpu.make_async_copy(src, dst, keeps.at[i])
         cp.start()
-        copies.append(cp)
-    keep = pltpu.make_async_copy(dat.at[s], d_heads.at[s], ls)
-    keep.start()
-
-    own_rows = pl.ds(pl.multiple_of(s * tl, tl), tl)
+        keep_all.append(cp)
+    down_ring.forward(4)
     branch = d_mid[...].astype(BF).reshape(nb * tl, D)
     for j in range(4):
-        a = jnp.concatenate([attn[b, j, own_rows] for b in range(nb)], axis=0)
-        stage[j] = mm_tn(a, branch).astype(BF)
-        pltpu.make_async_copy(stage.at[j], grad_out.at[j], gs.at[j]).start()
-
-    def out_copy(which, i):
-        r = pl.ds(pl.multiple_of(i * 256, 256), 256)
-        k = 2 * lax.rem(i, 2) + which
-        return pltpu.make_async_copy(stage.at[k], (grad_down, grad_up)[which].at[r], gs.at[k])
-
-    def grads(i, _):
-        r = pl.ds(pl.multiple_of(i * 256, 256), 256)
-        left = act[:, :, r].reshape(4 * nb * tl, 256)
-        res = mm_tn(left, cot[...].reshape(4 * nb * tl, D)).astype(BF)
-        out_copy(0, i).wait()
-        stage[2 * lax.rem(i, 2)] = res
-        out_copy(0, i).start()
-        left = htwo[:, :, r].reshape(4 * nb * tl, 256)
-        res = mm_tn(left, dup[...].reshape(4 * nb * tl, dup.shape[2])).astype(BF)
-        out_copy(1, i).wait()
-        stage[2 * lax.rem(i, 2) + 1] = res
-        out_copy(1, i).start()
-        return 0
-
-    lax.fori_loop(0, D // 256, grads, 0)
-    for i in range(D // 256 - 2, D // 256):
-        out_copy(0, i).wait()
-        out_copy(1, i).wait()
+        left = jnp.concatenate([attn[b, j] for b in range(nb)], axis=0)
+        up_copy(j).wait()
+        stage[j] = mm_tn(left, branch).astype(BF)
+        pltpu.make_async_copy(stage.at[j], grad_out.at[j], os_.at[j]).start()
 
     def done(jp, _):
         ca, cb = pair_copies(jp)
@@ -833,24 +1038,31 @@
         return 0
 
     lax.fori_loop(0, 2 * nb, done, 0)
+    s_down[...] = down_ring.result()
+    down_ring.drain()
     for b in range(nb):
         far_copy(b).wait_send()
-    for cp in copies:
+        for e, other in ((0, s2), (1, s3), (2, s1)):
+            spread(e, other, b).wait()
+    for j in range(4):
+        pltpu.make_async_copy(stage.at[j], grad_out.at[j], os_.at[j]).wait()
+    for cp in keep_all:
         cp.wait()
-    keep.wait()
-
-
-def run_k2(tok_all, attn_all, cot_all, modul, w_out, w_up, w_down):
-    nb, _, tl, width = tok_all.shape
+
+
+def run_k2(nd, act, slope, htwo, mid, attn_rows, cot_all, modul, w_out, w_up, w_down):
+    nb, _, tl, width = cot_all.shape
     hidden = w_up.shape[1]
-    cols = attn_all.shape[3]
+    cols = attn_rows.shape[3]
+    pc = width // nd
     vm = pl.BlockSpec(memory_space=pltpu.VMEM)
     hb = pl.BlockSpec(memory_space=pl.ANY)
     sds = jax.ShapeDtypeStruct
+    v = pltpu.VMEM
+    dma = pltpu.SemaphoreType.DMA
     return pl.pallas_call(
         k2_body,
         out_shape=(
-            sds((hidden, width), BF),
             sds((width, hidden), BF),
             sds((4, cols, width), BF),
             sds((nb, tl, width), F32),
@@ -858,56 +1070,83 @@
             sds((nb, tl, width), BF),
             sds((4, nb, tl, cols), BF),
             sds((nb, width), F32),
+            sds((hidden, pc), F32),
         ),
-        in_specs=[vm] * 7,
-        out_specs=(hb, hb, hb, vm, vm, vm, hb, vm),
+        in_specs=[hb, hb, hb, hb, hb, hb, vm, hb, hb, hb],
+        out_specs=(hb, hb, hb, hb, hb, hb, vm, vm),
         scratch_shapes=[
-            pltpu.VMEM((4 * nb, tl, hidden), BF),
-            pltpu.VMEM((4 * nb, tl, width), BF),
-            pltpu.VMEM((4 * nb, tl, hidden), BF),
-            pltpu.VMEM((nb, tl, width), F32),
-            pltpu.VMEM((2 * nb, tl, width), BF),
-            pltpu.VMEM((2 * nb, tl, width), BF),
-            pltpu.VMEM((2 * nb, tl, width), BF),
-            pltpu.VMEM((2 * nb, tl, width), BF),
-            pltpu.VMEM((nb, tl, width), BF),
-            pltpu.VMEM((nb, tl, width), BF),
-            pltpu.VMEM((4, nb, tl, cols), BF),
-            pltpu.VMEM((4, 256, width), BF),
-            pltpu.SemaphoreType.DMA,
-            pltpu.SemaphoreType.DMA((13,)),
-            pltpu.SemaphoreType.DMA((13,)),
-            pltpu.SemaphoreType.DMA((4,)),
+            v(act.shape, BF),
+            v(slope.shape, BF),
+            v(htwo.shape, BF),
+            v(mid.shape, F32),
+            v(attn_rows.shape, BF),
+            v(cot_all.shape, BF),
+            v(w_out.shape, BF),
+            v(w_up.shape, BF),
+            v(w_down.shape, BF),
+            v((nb, tl, width), F32),
+            v((nb, tl, width), F32),
+            v((nb, tl, width), BF),
+            v((2 * nb, tl, width), BF),
+            v((2 * nb, tl, width), BF),
+            v((2 * nb, tl, width), BF),
+            v((2 * nb, tl, width), BF),
+            v((nb, tl, width), BF),
+            v((nb, tl, width), BF),
+            v((4, nb, tl, cols), BF),
+            v((4, 256, width), BF),
+            v((hidden, width), BF),
+            v((2, hidden // 2, pc), BF),
+            v((6, hidden, pc), BF),
+            dma,
+            dma((16,)),
+            dma((16,)),
+            dma((4,)),
+            dma((6,)),
+            dma((4,)),
+            dma((3, 4 * nb)),
+            dma((8,)),
+            dma((8,)),
         ],
         compiler_params=pltpu.CompilerParams(
             collective_id=1, has_side_effects=True, vmem_limit_bytes=VMEM_LIMIT
         ),
         name="feed_forward",
-    )(tok_all, attn_all, cot_all, modul, w_out, w_up, w_down)
+    )(act, slope, htwo, mid, attn_rows, cot_all, modul, w_out, w_up, w_down)
 
 
 def k3_body(
-    qkv, lse, own, d_heads, w, h_one, tok, modul, cs, sn, d_mid, base, osend,
-    g_down, g_up, g_out, dsc_two, feats,
-    output, grad_tok, s_qkv, s_out, s_up, s_down, s_time,
+    fields_h, lse, attn_h, d_heads_h, w_h, normed_h, tok_h, modul, cs_h, sn_h, d_mid_h, base_h, osend,
+    g_up, g_out, dsc_two, feats,
+    output, grad_tok, s_qkv, s_out, s_up, s_time,
     orecv, dqt, draw, pa, ra, xs, xr, sumh, dhb,
-    vd, vu, vo, vq, oa, ob, ox, osum, down_h, down_w, up_h, up_w, out_h, out_w, qkv_h, qkv_w,
-    dpart, dall,
-    ls, ss, rs, gs, gr,
+    vu, vo, vq, oa, ob, ox, osum, up_h, up_w, out_h, out_w, qkv_h, qkv_w,
+    dpart, tx, dall, qkv, own, d_heads, w, normed_one, tok, cs, sn, d_mid, base,
+    ins, ls, ss, rs, gs, gr,
 ):
     g, s, core, s1, s2, s3 = peers()
     chip = s // 2
     p = ring_place(g)
     nd = dall.shape[0]
-    others = [(lax.rem(g + d, nd), s) for d in range(1, nd)]
     loads = [
-        pltpu.make_async_copy(g_down, vd, ls.at[0]),
-        pltpu.make_async_copy(g_up, vu, ls.at[1]),
-        pltpu.make_async_copy(g_out, oa, ls.at[2]),
+        pltpu.make_async_copy(g_up, vu, ls.at[0]),
+        pltpu.make_async_copy(g_out, oa, ls.at[1]),
     ]
+    pulls = []
+    for i, (src, dst) in enumerate(
+        (
+            (fields_h, qkv), (attn_h, own), (d_heads_h, d_heads), (cs_h, cs), (sn_h, sn),
+            (w_h, w), (normed_h, normed_one), (tok_h, tok), (d_mid_h, d_mid), (base_h, base),
+        )
+    ):
+        pulls.append(pltpu.make_async_copy(src, dst, ins.at[i]))
+    for cp in pulls[:3]:
+        cp.start()
     for cp in loads:
         cp.start()
-    greet([(g, s1), (g, s2), (g, s3)] + others)
+    for cp in pulls[3:]:
+        cp.start()
+    greet([(g, s1), (g, s2), (ring_index(p + 1), s), (ring_index(p - 1), s)])
     nb, tl = tok.shape[0], tok.shape[1]
     rows, cols = own.shape[1], own.shape[2]
     heads = cols // HD
@@ -932,46 +1171,62 @@
 
         return view
 
-    down_ring = Scatter(view_cols(vd, vd.shape[0]), down_h, down_w, gs, gr, 0)
-    up_ring = Scatter(view_rows(vu), up_h, up_w, gs, gr, 8)
-    out_ring = Scatter(view_cols(vo, vo.shape[0]), out_h, out_w, gs, gr, 16)
-    qkv_ring = Scatter(view_rows(vq), qkv_h, qkv_w, gs, gr, 24)
+    up_ring = Scatter(view_rows(vu), up_h, up_w, gs, gr, 16)
+    def view_time(j, half):
+        wide = (2 * D + TF) // 2
+        ref = dall.at[j]
+        return ref if half is None else ref.at[:, half * wide : (half + 1) * wide]
+
+    out_rings = [
+        Scatter(view_cols(vo.at[i], vo.shape[1]), out_h.at[i], out_w.at[i], gs, gr, 8 * i)
+        for i in range(2)
+    ]
+    time_ring = Gather(dall.at[g], view_time, gs, gr, 32)
+    def view_qkv(side):
+        wide = vq.shape[1] // 2
+
+        def view(j, half):
+            lo, n = (0, pc) if half is None else (half * (pc // 2), pc // 2)
+            return vq.at[
+                pl.ds(pl.multiple_of(j * pc + lo, n), n), side * wide : (side + 1) * wide
+            ]
+
+        return view
+
+    qkv_rings = [
+        Scatter(view_qkv(i), qkv_h.at[i], qkv_w.at[i], gs, gr, 24 + 16 * i) for i in range(2)
+    ]
+
+    def qkv_forward(k):
+        for ring in qkv_rings:
+            ring.forward(k)
+
     loads[0].wait()
-    down_ring.start()
+    up_ring.start()
     back = []
     for b in range(nb):
         cp = remote(osend.at[b], orecv.at[b], ss, rs, b, (g, s2))
         cp.start()
         back.append(cp)
-    loads[2].wait()
+    loads[1].wait()
     cross = []
-    for phase in range(2):
-        where = chip if phase else 1 - chip
-        cp = remote(oa.at[2 * where + 1 - core], ob.at[phase], ss, rs, 8 + phase, (g, s1))
+    for i in range(2):
+        cp = remote(oa.at[2 * i + 1 - core], ob.at[i], ss, rs, 8 + i, (g, s1))
         cp.start()
         cross.append(cp)
-    loads[1].wait()
-    up_ring.start()
     over = remote(osum, ox, ss, rs, 10, (g, s2))
 
     def out_pair():
-        for cp in cross:
-            cp.wait_recv()
-        osum[...] = (oa[2 * (1 - chip) + core].astype(F32) + ob[0].astype(F32)).astype(BF)
-        over.start()
-
-    def out_own():
-        over.wait_recv()
-        vo[...] = (
-            (oa[s].astype(F32) + ob[1].astype(F32)) + ox[...].astype(F32)
-        ).astype(BF)
-        out_ring.start()
+        for i in range(2):
+            cross[i].wait_recv()
+            vo[i] = (oa[2 * i + core].astype(F32) + ob[i].astype(F32)).astype(BF)
+            out_rings[i].start()
+
+    def out_forward(k):
+        for ring in out_rings:
+            ring.forward(k)
 
     lane = lax.broadcasted_iota(jnp.int32, (1, cols), 1)
-    pick = (
-        lax.broadcasted_iota(jnp.int32, (8, cols), 1) // HD
-        == lax.broadcasted_iota(jnp.int32, (8, cols), 0)
-    ).astype(F32)
 
     def near_copy(b, phase):
         i = 2 * b + phase
@@ -979,6 +1234,29 @@
 
     def far_copy(b):
         return remote(xs.at[b], xr.at[b], ss, rs, 6 + b, (g, s2))
+
+    for cp in pulls[:5]:
+        cp.wait()
+    out_pair()
+
+    def grads(side):
+        wide = vq.shape[1] // 2
+        c = slice(side * wide, (side + 1) * wide)
+
+        def one(i, _):
+            r = pl.ds(pl.multiple_of(i * 256, 256), 256)
+            left = jnp.concatenate(
+                [
+                    (normed_one[b, :, r].astype(F32) * (1.0 + modul[b : b + 1, r])).astype(BF)
+                    for b in range(nb)
+                ],
+                axis=0,
+            )
+            vq[r, c] = mm_tn(left, draw[:, :, c].reshape(nb * rows, wide)).astype(BF)
+            return 0
+
+        lax.fori_loop(0, D // 256, one, 0)
+        qkv_rings[side].start()
 
     def sequence(b, _):
         for j in range(4):
@@ -986,22 +1264,22 @@
         query = qkv[b, 0]
         d_out = dhb[...]
         prod = d_out.astype(F32) * own[b].astype(F32)
-        delta = lax.dot_general(
-            pick, prod, (((1,), (1,)), ((), ())), precision=HIGHEST, preferred_element_type=F32
+        prod = prod.T
+        delta = jnp.concatenate(
+            [jnp.sum(prod[h * HD : (h + 1) * HD], axis=0, keepdims=True) for h in range(heads)],
+            axis=0,
         )
         dqt[...] = jnp.zeros_like(dqt)
 
         def keys_block(i, _):
             it = b * nk + i
             for when, act in (
-                (1, out_pair),
-                (1, lambda: down_ring.forward(2)),
-                (2, lambda: up_ring.forward(2)),
-                (3, lambda: down_ring.forward(3)),
-                (4, lambda: up_ring.forward(3)),
-                (5, lambda: down_ring.forward(4)),
-                (6, lambda: up_ring.forward(4)),
-                (7, out_own),
+                (1, lambda: up_ring.forward(2)),
+                (2, lambda: out_forward(2)),
+                (3, lambda: up_ring.forward(3)),
+                (4, lambda: out_forward(3)),
+                (5, lambda: up_ring.forward(4)),
+                (6, lambda: out_forward(4)),
             ):
 
                 @pl.when(it == when)
@@ -1017,13 +1295,13 @@
                 mask_v = lane // HD == h
                 km = jnp.where(mask, keys, jnp.zeros_like(keys))
                 vmask = jnp.where(mask_v, values, jnp.zeros_like(values))
-                probs = jnp.exp(mm_nt(km, query) - lse[b, h : h + 1])
+                probs = jnp.exp2(mm_nt(km, query) - lse[b, h : h + 1])
                 d_probs = mm_nt(vmask, d_out)
                 ds = (probs * (d_probs - delta[h : h + 1])).astype(BF)
                 dv = jnp.where(mask_v, mm(probs.astype(BF), d_out), dv)
                 dk = jnp.where(mask, mm(ds, query), dk)
                 dqt[...] += mm_tn(km, ds)
-            c, n = cs[r], sn[r]
+            c, n = cs[r] * math.log(2.0), sn[r] * math.log(2.0)
             da, db = dk[:, :128], dk[:, 128:]
             draw[b, r, 256:512] = jnp.concatenate([da * c + db * n, db * c - da * n], axis=1).astype(BF)
             draw[b, r, 512:768] = dv.astype(BF)
@@ -1035,14 +1313,31 @@
         c, n = cs[...], sn[...]
         draw[b, :, 0:256] = jnp.concatenate([da * c + db * n, db * c - da * n], axis=1).astype(BF)
 
+        @pl.when(b == 0)
+        def _():
+            for cp in pulls[5:]:
+                cp.wait()
+            dpart[0, :, :D] = jnp.zeros((nb, D), F32)
+
         def part(owner):
             r = pl.ds(pl.multiple_of(owner * tl, tl), tl)
-            return mm_nt(draw[b, r], w[...])
+            res = mm_nt(draw[b, r], w[...])
+            dpart[0, pl.ds(b, 1), :D] += jnp.sum(
+                res * normed_one[b, r].astype(F32), axis=0, keepdims=True
+            )
+            return res
+
+        @pl.when(b == nb - 1)
+        def _():
+            grads(0)
+            grads(1)
 
         for phase in range(2):
             where = chip if phase else 1 - chip
             pa[2 * b + phase] = part(2 * where + 1 - core).astype(BF)
             near_copy(b, phase).start()
+        for phase in range(2):
+            where = chip if phase else 1 - chip
             kept = part(2 * where + core)
             near_copy(b, phase).wait_recv()
             kept = kept + ra[2 * b + phase].astype(F32)
@@ -1054,33 +1349,30 @@
         return 0
 
     lax.fori_loop(0, nb, sequence, 0)
-
-    def grads(i, _):
-        r = pl.ds(pl.multiple_of(i * 256, 256), 256)
-        left = h_one[:, :, r].reshape(nb * rows, 256)
-        vq[r] = mm_tn(left, draw[...].reshape(nb * rows, 3 * cols)).astype(BF)
-        return 0
-
-    lax.fori_loop(0, D // 256, grads, 0)
-    qkv_ring.start()
-    out_ring.forward(2)
-    s_down[...] = down_ring.result()
-    s_up[...] = up_ring.result()
-    out_ring.forward(3)
-    qkv_ring.forward(2)
+    dpart[0, :, D:] = dsc_two[...]
+    small = [remote(dpart.at[0], dpart.at[1], ss, rs, 11, (g, s1))]
+    small[0].start()
+    first_out, second_out = out_rings[0].result(), out_rings[1].result()
+    osum[...] = jnp.where(chip == 0, second_out, first_out).astype(BF)
+    own_out = jnp.where(chip == 0, first_out, second_out)
+    over.start()
+    qkv_forward(2)
+    small[0].wait_recv()
+    dall[g, :, : 2 * D] = dpart[0] + dpart[1]
+    dall[g, :, 2 * D :] = feats[...]
+    time_ring.start()
     for b in range(nb):
         back[b].wait_recv()
         output[b] = (base[b] + orecv[b].astype(F32)).astype(BF)
-    out_ring.forward(4)
-    qkv_ring.forward(3)
+    s_up[...] = up_ring.result()
+    qkv_forward(3)
+    time_ring.forward(2)
 
     def tail(b, _):
         scale = 1.0 + modul[pl.ds(b, 1), :D]
         far_copy(b).wait_recv()
-        dh = sumh[b] + xr[b].astype(F32)
         normed, inverse = moments(tok[b].astype(F32))
-        dpart[0, pl.ds(b, 1), :D] = jnp.sum(dh * normed, axis=0, keepdims=True)
-        dn = dh * scale
+        dn = (sumh[b] + xr[b].astype(F32)) * scale
         inner = jnp.mean(dn * normed, axis=-1, keepdims=True)
         grad_tok[b] = (
             d_mid[b]
@@ -1088,57 +1380,52 @@
         ).astype(BF)
         return 0
 
-    lax.fori_loop(0, nb, tail, 0)
-    dpart[0, :, D:] = dsc_two[...]
-    small = []
-    for e, other in ((1, s1), (2, s2), (3, s3)):
-        cp = remote(dpart.at[0], dpart.at[e], ss, rs, 10 + e, (g, other))
-        cp.start()
-        small.append(cp)
-    qkv_ring.forward(4)
-    for cp in small:
-        cp.wait_recv()
-    dall[0, :, : 2 * D] = (dpart[0] + dpart[1]) + (dpart[2] + dpart[3])
-    dall[0, :, 2 * D :] = feats[...]
-    wide = []
-    for d in range(1, nd):
-        cp = remote(dall.at[0], dall.at[d], ss, rs, 13 + d, others[d - 1])
-        cp.start()
-        wide.append(cp)
-    s_out[...] = out_ring.result()
-    s_qkv[...] = qkv_ring.result()
-    for cp in wide:
-        cp.wait_recv()
+    lax.fori_loop(0, nb - 1, tail, 0)
+    qkv_forward(4)
+    time_ring.forward(3)
+    time_ring.forward(4)
+    lax.fori_loop(nb - 1, nb, tail, 0)
+    over.wait_recv()
+    s_out[...] = own_out + ox[...].astype(F32)
+    time_ring.arrive()
     depth = s_time.shape[0]
-    place = (4 * g + s) * depth
-    hit = (
-        lax.broadcasted_iota(jnp.int32, (depth, TF), 1)
-        == lax.broadcasted_iota(jnp.int32, (depth, TF), 0) + place
-    )
-    total = jnp.zeros((depth, 2 * D), F32)
+    lane_t = lax.broadcasted_iota(jnp.int32, (depth, TF), 1)
+    row_t = lax.broadcasted_iota(jnp.int32, (depth, TF), 0)
+    mine = jnp.zeros((depth, 2 * D), F32)
+    theirs = jnp.zeros((depth, 2 * D), F32)
     for d in range(nd):
         for b in range(nb):
             row = dall[d, b : b + 1]
-            column = jnp.sum(jnp.where(hit, row[:, 2 * D :], 0.0), axis=1, keepdims=True)
-            total = total + column * row[:, : 2 * D]
-    s_time[...] = total
+            for which, other in ((0, s), (1, s2)):
+                hit = lane_t == row_t + (4 * g + other) * depth
+                column = jnp.sum(jnp.where(hit, row[:, 2 * D :], 0.0), axis=1, keepdims=True)
+                if which:
+                    theirs = theirs + column * row[:, : 2 * D]
+                else:
+                    mine = mine + column * row[:, : 2 * D]
+    tx[0] = theirs
+    swap = remote(tx.at[0], tx.at[1], ss, rs, 12, (g, s2))
+    swap.start()
+    s_qkv[...] = jnp.concatenate([ring.result() for ring in qkv_rings], axis=1)
+    swap.wait_recv()
+    s_time[...] = mine + tx[1]
     for b in range(nb):
         back[b].wait_send()
         far_copy(b).wait_send()
         for phase in range(2):
             near_copy(b, phase).wait_send()
-    for cp in cross + small + wide + [over]:
+    for cp in cross + small + [over, swap]:
         cp.wait_send()
-    for ring in (down_ring, up_ring, out_ring, qkv_ring):
+    for ring in out_rings + qkv_rings + [up_ring, time_ring]:
         ring.drain()
 
 
 def run_k3(
-    nd, qkv, lse, own, d_heads, w, h_one, tokens, modul, cs, sn, d_mid, base, osend,
-    g_down, g_up, g_out, dsc_two, feats,
+    nd, qkv, lse, attn_heads, d_heads, w, normed, tokens, modul, cs, sn, d_mid, base, osend,
+    g_up, g_out, dsc_two, feats,
 ):
     nb, tl, width = tokens.shape
-    rows, cols = own.shape[1], own.shape[2]
+    rows, cols = attn_heads.shape[1], attn_heads.shape[2]
     hidden = g_up.shape[1]
     pc = width // nd
     vm = pl.BlockSpec(memory_space=pltpu.VMEM)
@@ -1154,11 +1441,10 @@
             sds((pc, 3 * cols), F32),
             sds((cols, pc), F32),
             sds((pc, hidden), F32),
-            sds((hidden, pc), F32),
             sds((TF // (4 * nd), 2 * width), F32),
         ),
-        in_specs=[vm] * 12 + [hb, hb, hb, hb, vm, vm],
-        out_specs=(vm,) * 7,
+        in_specs=[hb, vm, hb, hb, hb, hb, hb, vm, hb, hb, hb, hb, hb, hb, hb, vm, vm],
+        out_specs=(vm,) * 6,
         scratch_shapes=[
             v((nb, tl, width), BF),
             v((cols, rows), F32),
@@ -1169,38 +1455,78 @@
             v((nb, tl, width), BF),
             v((nb, tl, width), F32),
             v((rows, cols), BF),
-            v((hidden, width), BF),
             v((width, hidden), BF),
-            v((cols, width), BF),
+            v((2, cols, width), BF),
             v((width, 3 * cols), BF),
             v((4, cols, width), BF),
             v((2, cols, width), BF),
-            v((cols, width), BF),
-            v((cols, width), BF),
-            v((2, hidden // 2, pc), BF),
-            v((6, hidden, pc), BF),
+            v((cols, pc), BF),
+            v((cols, pc), BF),
             v((2, pc // 2, hidden), BF),
             v((6, pc, hidden), BF),
-            v((2, cols // 2, pc), BF),
-            v((6, cols, pc), BF),
-            v((2, pc // 2, 3 * cols), BF),
-            v((6, pc, 3 * cols), BF),
-            v((4, nb, 2 * width), F32),
+            v((2, 2, cols // 2, pc), BF),
+            v((2, 6, cols, pc), BF),
+            v((2, 2, pc // 2, 3 * cols // 2), BF),
+            v((2, 6, pc, 3 * cols // 2), BF),
+            v((2, nb, 2 * width), F32),
+            v((2, TF // (4 * nd), 2 * width), F32),
             v((nd, nb, 2 * width + TF), F32),
-            dma((3,)),
-            dma((21,)),
-            dma((21,)),
-            dma((32,)),
-            dma((32,)),
+            v(qkv.shape, BF),
+            v((nb, rows, cols), BF),
+            v(d_heads.shape, BF),
+            v(w.shape, BF),
+            v(normed.shape, BF),
+            v(tokens.shape, BF),
+            v(cs.shape, F32),
+            v(sn.shape, F32),
+            v(d_mid.shape, F32),
+            v(base.shape, F32),
+            dma((10,)),
+            dma((2,)),
+            dma((13,)),
+            dma((13,)),
+            dma((48,)),
+            dma((48,)),
         ],
         compiler_params=pltpu.CompilerParams(
             collective_id=2, has_side_effects=True, vmem_limit_bytes=VMEM_LIMIT
         ),
         name="attention_backward",
     )(
-        qkv, lse, own, d_heads, w, h_one, tokens, modul, cs, sn, d_mid, base, osend,
-        g_down, g_up, g_out, dsc_two, feats,
-    )
+        qkv, lse, attn_heads, d_heads, w, normed, tokens, modul, cs, sn, d_mid, base, osend,
+        g_up, g_out, dsc_two, feats,
+    )
+
+
+def k4_body(*refs):
+    count = len(refs) // 2
+    for i in range(count):
+        if i != 2:
+            refs[count + i][...] = refs[i][...]
+    w = refs[2][...]
+    heads = w.shape[1] // (3 * HD)
+    half, size = HD // 2, heads * HD
+    pieces = []
+    for h in range(heads):
+        for part in (0, 1):
+            for side in (0, 1):
+                at = part * size + side * (size // 2) + h * half
+                pieces.append(w[:, at : at + half])
+        at = 2 * size + h * HD
+        pieces.append(w[:, at : at + HD])
+    refs[count + 2][...] = jnp.concatenate(pieces, axis=1)
+
+
+def run_k4(arrays):
+    vm = pl.BlockSpec(memory_space=pltpu.VMEM)
+    return pl.pallas_call(
+        k4_body,
+        out_shape=tuple(jax.ShapeDtypeStruct(a.shape, a.dtype) for a in arrays),
+        in_specs=[vm] * len(arrays),
+        out_specs=(vm,) * len(arrays),
+        compiler_params=pltpu.CompilerParams(vmem_limit_bytes=VMEM_LIMIT),
+        name="results",
+    )(*arrays)
 
 
 def order_columns(w):
@@ -1210,15 +1536,6 @@
     turned = w[:, :, 0:2].reshape(rows, heads, 2, 2, HD // 2)
     turned = jnp.transpose(turned, (0, 2, 3, 1, 4)).reshape(rows, 2 * heads * HD)
     return jnp.concatenate([turned, w[:, :, 2].reshape(rows, heads * HD)], axis=1)
-
-
-def restore_columns(w):
-    rows = w.shape[0]
-    heads = w.shape[1] // (3 * HD)
-    turned = w[:, : 2 * heads * HD].reshape(rows, 2, 2, heads, HD // 2)
-    turned = jnp.transpose(turned, (0, 3, 1, 2, 4)).reshape(rows, heads, 2, HD)
-    values = w[:, 2 * heads * HD :].reshape(rows, heads, 1, HD)
-    return jnp.concatenate([turned, values], axis=2).reshape(rows, heads * 3 * HD)
 
 
 def fast_shards(nd, tokens, bins, plan, w_qkv, w_out, w_up, w_down, w_time, cotangent):
@@ -1235,20 +1552,20 @@
     cs = jnp.tile(jnp.cos(angle), (1, 128 // half))
     sn = jnp.tile(jnp.sin(angle), (1, 128 // half))
     (
-        tok_all, modul, full_qkv, full_out, full_up, full_down,
-        h_one, qkv, lse, own, attn_all, cot_all,
+        modul, full_qkv, full_out, full_up, full_down, normed, qkv, lse, attn_heads, attn_rows,
+        cot_all, act, slope, htwo, mid,
     ) = run_k1(
         nd, tokens, w_time, fs, order_columns(w_qkv), w_out, w_up, w_down, cs, sn, cotangent
     )
-    grad_down, grad_up, grad_out, d_mid, base, osend, d_heads, dsc_two = run_k2(
-        tok_all, attn_all, cot_all, modul, full_out, full_up, full_down
-    )
-    output, grad_tokens, sum_qkv, sum_out, sum_up, sum_down, grad_time = run_k3(
-        nd, qkv, lse, own, d_heads, full_qkv, h_one, tokens, modul, cs, sn, d_mid, base, osend,
-        grad_down, grad_up, grad_out, dsc_two, feats,
-    )
-    return (
-        output, grad_tokens, restore_columns(sum_qkv), sum_out, sum_up, sum_down, grad_time
+    grad_up, grad_out, d_mid, base, osend, d_heads, dsc_two, sum_down = run_k2(
+        nd, act, slope, htwo, mid, attn_rows, cot_all, modul, full_out, full_up, full_down
+    )
+    output, grad_tokens, sum_qkv, sum_out, sum_up, grad_time = run_k3(
+        nd, qkv, lse, attn_heads, d_heads, full_qkv, normed, tokens, modul, cs, sn, d_mid, base,
+        osend, grad_up, grad_out, dsc_two, feats,
+    )
+    return tuple(
+        run_k4((output, grad_tokens, sum_qkv, sum_out, sum_up, sum_down, grad_time))
     )
 
 

time: 246 us -> 234 us (0.951)
  local copies, waits for them, and re-layouts: 11.3 us -> 3.29 us
  Pallas kernels: 230 us -> 227 us
    pallas_call x1, Pallas kernels: 87.1 us -> 74.4 us  [run_k3(): pl.pallas_call(k3_body, out_shape=(sds((nb, tl, width), BF), sds((nb, tl,...]
    pallas_call x2 -> x3, Pallas kernels: 143 us -> 152 us  [the longest x1 93.9 us: run_k1(): pl.pallas_call(k1_body, out_shape=(sds((nb, 2 * width), F32), sds((width,...]
    unnamed x22 -> x3, local copies, waits for them, and re-layouts: 5.91 us -> 0.16 us
where the time goes in v2:
time: 234 us
  Pallas kernels  227 us (97%)
  local copies, waits for them, and re-layouts  3.29 us (1%)
  other arithmetic  3.09 us (1%)
    pallas_call x1, Pallas kernels, run_k1(): pl.pallas_call(k1_body, out_shape=(sds((nb, 2 * width), F32), sds((width,...  93.9 us
    pallas_call x1, Pallas kernels, run_k3(): pl.pallas_call(k3_body, out_shape=(sds((nb, tl, width), BF), sds((nb, tl,...  74.4 us
    pallas_call x1, Pallas kernels, run_k2(): pl.pallas_call(k2_body, out_shape=(sds((width, hidden), BF), sds((4, cols...  54.3 us

profile of v2, /device:TPU:0, one launch (start us, length us, event | category | flops | bytes accessed | tf_op | source)
XLA Modules:
  0.0 233.8 jit_solution(9006155279610755291)
XLA Ops:
  0.6 0.0 copy-start
  0.6 0.9 fusion.7
  1.6 0.2 fusion.3
  1.8 0.8 copy.31.fs
  2.6 0.5 fusion
  3.2 1.0 copy.32.cs.cs_h
  4.3 1.0 copy.33.sn.sn_h
  5.3 0.0 copy-done
  5.3 0.2 copy.27
  5.5 0.1 copy.29
  5.6 0.1 copy.30
  5.7 0.7 pad_maximum_fusion.w_qkv
  6.4 93.9 %attention_forward.1 = (f32[2,2048]{1,0:T(2,128)}, bf16[1024,768]{1,0:T(8,128)(2,1)}, bf16[1024,1024]{1,0:T(8,128)(2,1)}, bf16[1024,1024]{1,0:T(8,128)(2,1)}, bf...) custom-call(bf16[2,256,1024]{2,1,0:T(8,128)(2,1)} %tok_h.1, ...), custom_call_target="tpu_custom_call" | custom-call | tf_op jit(solution)/shard_map/attention_forward/pallas_call | solution.py:787
  100.3 54.3 %feed_forward.1 = (bf16[1024,1024]{1,0:T(8,128)(2,1)}, bf16[4,256,1024]{2,1,0:T(8,128)(2,1)}, f32[2,256,1024]{2,1,0:T(8,128)}, f32[2,256,1024]{2,1,0:T(8,128)}, ...) custom-call(bf16[8,256,1024]{2,1,0:T(8,128)(2,1)} %get-tuple-element., ...), custom_call_target="tpu_custom_call" | custom-call | tf_op jit(solution)/shard_map/feed_forward/pallas_call | solution.py:1063
  154.6 0.1 fusion.5
  154.7 0.6 maximum_convert_fusion.feats
  155.3 74.4 %attention_backward.1 = (bf16[2,256,1024]{2,1,0:T(8,128)(2,1)}, bf16[2,256,1024]{2,1,0:T(8,128)(2,1)}, f32[128,768]{1,0:T(8,128)}, f32[256,128]{1,0:T(8,128)}, f32[128,1024]{1,0:T(8,128)}, /*index=5*/f32[8,2048]{1,0:T(8,128)}) custom-call(bf16[2,3,1024,256]{3,2,1,0:T(8,128)(2,1)} %get-tuple-element.36.fields_h, f32[2,8,1024]{2,1,0:T(8,128)} %get-tuple-element.37.lse, ...), custom_call_target="tpu_custom_call" | custom-call | tf_op jit(solution)/shard_map/attention_backward/pallas_call | solution.py:1436
  229.7 4.1 %results.1 = (bf16[2,256,1024]{2,1,0:T(8,128)(2,1)}, bf16[2,256,1024]{2,1,0:T(8,128)(2,1)}, f32[128,768]{1,0:T(8,128)}, f32[256,128]{1,0:T(8,128)}, f32[128,1024...) custom-call(bf16[2,256,1024]{2,1,0:T(8,128)(2,1)} %get-tuple-element.58.refs_0_, ...), custom_call_target="tpu_custom_call" | custom-call | tf_op jit(solution)/shard_map/results/pallas_call | solution.py:1522
  (10 shorter events, 0.2 us)
Async XLA Ops:
  0.6 4.6 %copy-start = (bf16[128,768]{1,0:T(8,128)(2,1)S(1)}, bf16[128,768]{1,0:T(8,128)(2,1)}, u32[]{:S(2)}) copy-start(bf16[128,768]{1,0:T(8,128)(2,1)} %param.12) | copy-start | bytes 589828

commit v3 on v2

--- a/solution.py
+++ b/solution.py
@@ -3,6 +3,7 @@
 
 import jax
 import jax.numpy as jnp
+import numpy as np
 from jax import lax
 from jax.experimental import pallas as pl
 from jax.experimental.pallas import tpu as pltpu
@@ -421,9 +422,21 @@
     return ref if half is None else ref.at[half * (size // 2) : (half + 1) * (size // 2)]
 
 
+def ordering(heads):
+    half, size = HD // 2, heads * HD
+    to = lax.broadcasted_iota(jnp.int32, (1, 3 * size), 1)
+    part, at = to // size, lax.rem(to, size)
+    side, rest = at // (size // 2), lax.rem(at, size // 2)
+    turned = (rest // half) * (3 * HD) + part * HD + side * half + lax.rem(rest, half)
+    plain = (at // HD) * (3 * HD) + 2 * HD + lax.rem(at, HD)
+    source = jnp.where(part == 2, plain, turned)
+    rows = lax.broadcasted_iota(jnp.int32, (3 * size, 3 * size), 0)
+    return jnp.where(rows == source, 1.0, 0.0).astype(BF)
+
+
 def k1_body(
-    tok, wt, fs, w_qkv, w_out, w_up, w_down, cs, sn, cot,
-    modul, wq_out, out_all, up_all, down_all, n_out, qkv_out, lse, attn_heads, attn_rows, cot_all,
+    tok, wt, feats, w_qkv, w_out, w_up, w_down, cs, sn, cot,
+    modul, feats_out, wq_out, out_all, up_all, down_all, n_out, qkv_out, lse, attn_heads, attn_rows, cot_all,
     act_out, slope_out, htwo_out, mid_out,
     tokv, wtime, pbuf, vt, cotv, wq, nv, qkv, attn, outv, upv, act, slope, htwo, mids, csv, snv,
     ks, ls, ss, rs, gs, gr, fs_, fr_, os_,
@@ -476,7 +489,7 @@
     time_ring = Gather(wt, view_time, gs, gr, 0)
     part = w_qkv.shape[0] // 2
     qkv_rings = [
-        Gather(w_qkv.at[i * part : (i + 1) * part], view_qkv(i), gs, gr, 8 + 40 * i)
+        Gather(view_qkv(i)(g, None), view_qkv(i), gs, gr, 8 + 40 * i)
         for i in range(2)
     ]
     up_ring = Gather(w_up, view_rows(upv, w_up.shape[0]), gs, gr, 16)
@@ -486,24 +499,24 @@
 
     local = [
         pltpu.make_async_copy(tok, tokv.at[:, s], ls.at[0]),
-        pltpu.make_async_copy(w_qkv, view_rows(wq, w_qkv.shape[0])(g, None), ls.at[1]),
+        pltpu.make_async_copy(cot, cotv, ls.at[5]),
         pltpu.make_async_copy(w_up, view_rows(upv, w_up.shape[0])(g, None), ls.at[2]),
         pltpu.make_async_copy(w_down, view_down(g, None), ls.at[3]),
         pltpu.make_async_copy(w_out, here, ls.at[4]),
-        pltpu.make_async_copy(cot, cotv, ls.at[5]),
         pltpu.make_async_copy(cs, csv, ls.at[6]),
         pltpu.make_async_copy(sn, snv, ls.at[7]),
     ]
     greet([(g, s1), (g, s2), (g, s3), (ring_index(p + 1), s), (ring_index(p - 1), s)])
     time_ring.start()
-    for ring in qkv_rings:
-        ring.start()
-    out_ring.start()
     pair_out = remote(w_out, here, ss, rs, 0, (g, s2))
     pair_out.start()
     far = [remote(tok.at[b], tokv.at[b, s], ss, rs, 1 + b, (g, s2)) for b in range(nb)]
+    far[0].start()
+    ordered = mm(w_qkv[...], ordering(heads)).astype(BF)
+    wq[pl.ds(pl.multiple_of(g * w_qkv.shape[0], w_qkv.shape[0]), w_qkv.shape[0])] = ordered
+    for ring in qkv_rings:
+        ring.start()
     near = []
-    far[0].start()
     for b in range(nb):
         cp = remote(tok.at[b], tokv.at[b, s], ss, rs, 3 + b, (g, s1))
         cp.start()
@@ -511,31 +524,38 @@
     for cp in local:
         cp.start()
     wtime[g] = wt[...]
-    half_rows = tl // 2
+    pieces = [(0, 0, tl // 4), (0, tl // 4, tl)] + [(b, 0, tl) for b in range(1, nb)]
 
     def cot_piece(k):
-        r = slice((k % 2) * half_rows, (k % 2 + 1) * half_rows)
+        b, lo, hi = pieces[k]
         return remote(
-            cotv.at[k // 2, r], cot_all.at[k // 2, s, r], ss, rs, 18 + k, (g, s2)
+            cotv.at[b, lo:hi], cot_all.at[b, s, lo:hi], ss, rs, 18 + k, (g, s2)
         )
 
-    local[5].wait()
-    cot_far = [cot_piece(k) for k in range(2 * nb)]
+    local[1].wait()
+    cot_far = [cot_piece(k) for k in range(len(pieces))]
     cot_far[0].start()
     for k in (2, 3, 4):
         time_ring.forward(k)
         for ring in qkv_rings:
             ring.forward(k)
-        out_ring.forward(k)
+    up_ring.start()
+    out_ring.start()
     pair_out.wait_recv()
     far_ring.start()
-    up_ring.start()
     time_ring.arrive()
-    weights = wtime[...].astype(F32)
-    parts = [
-        jnp.sum(jnp.sum(weights * fs[b], axis=0), axis=0, keepdims=True) for b in range(nb)
-    ]
-    pbuf[0] = jnp.concatenate(parts, axis=0)
+    depth = wt.shape[0]
+    feats_out[...] = feats[...]
+    lane_t = lax.broadcasted_iota(jnp.int32, (depth, TF), 1)
+    row_t = lax.broadcasted_iota(jnp.int32, (depth, TF), 0)
+    sums = [jnp.zeros((depth, 2 * D), F32) for _ in range(nb)]
+    for d in range(wtime.shape[0]):
+        hit = lane_t == row_t + (4 * d + s) * depth
+        weights = wtime[d].astype(F32)
+        for b in range(nb):
+            column = jnp.sum(jnp.where(hit, feats[b : b + 1], 0.0), axis=1, keepdims=True)
+            sums[b] = sums[b] + weights * column
+    pbuf[0] = jnp.concatenate([jnp.sum(v, axis=0, keepdims=True) for v in sums], axis=0)
     small = []
     for e, other in ((1, s1), (2, s2), (3, s3)):
         cp = remote(pbuf.at[0], pbuf.at[e], ss, rs, 4 + e, (g, other))
@@ -557,7 +577,7 @@
     modul[...] = (pbuf[0] + pbuf[1]) + (pbuf[2] + pbuf[3])
     for ring in qkv_rings:
         ring.arrive()
-    for i in (0, 1, 6, 7):
+    for i in (0, 5, 6):
         local[i].wait()
     keep_w = pltpu.make_async_copy(wq, wq_out, ls.at[8])
     keep_w.start()
@@ -628,6 +648,20 @@
             def _(i=i):
                 tokens_of(i)
 
+        def at(events):
+            for when, action in events:
+
+                @pl.when(it == when)
+                def _(action=action):
+                    action()
+
+        def up_out(k):
+            up_ring.forward(k)
+            out_ring.forward(k)
+            far_ring.forward(k)
+
+        at(((4, lambda: up_out(4)), (4, down_ring.start)))
+
         @pl.when(q == 0)
         def _():
             project(b)
@@ -635,22 +669,15 @@
             for cp in keep_fields(b):
                 cp.start()
 
-        for when, action in (
-            (1, lambda: up_ring.forward(2)),
-            (1, lambda: far_ring.forward(2)),
-            (2, second_tokens),
-            (3, lambda: up_ring.forward(3)),
-            (3, lambda: far_ring.forward(3)),
-            (4, lambda: up_ring.forward(4)),
-            (4, down_ring.start),
-            (5, lambda: far_ring.forward(4)),
-            (6, lambda: pass_attn(0, nq)),
-        ):
-
-            @pl.when(it == when)
-            def _(action=action):
-                action()
-
+        at(
+            (
+                (0, lambda: up_out(2)),
+                (2, lambda: up_out(3)),
+                (2, second_tokens),
+                (6, lambda: pass_attn(0, nq)),
+                (7, lambda: down_ring.forward(2)),
+            )
+        )
         r = pl.ds(pl.multiple_of(q * blk, blk), blk)
         query, keys = qkv[b, 0, r], qkv[b, 1]
         outs, stats = [], []
@@ -702,11 +729,10 @@
     def feed(i, _):
         b, owner = i // 4, lax.rem(i, 4)
         for when, action in (
-            (1, lambda: down_ring.forward(2)),
+            (1, lambda: down_ring.forward(3)),
             (3, lambda: pass_attn(nq, 2 * nq)),
-            (3, lambda: down_ring.forward(3)),
             (4, lambda: arrive_attn(nq, 2 * nq)),
-            (6, lambda: down_ring.forward(4)),
+            (4, lambda: down_ring.forward(4)),
         ):
 
             @pl.when(i == when)
@@ -740,8 +766,9 @@
     keep_rows = pltpu.make_async_copy(attn.at[:, :, own_rows], attn_rows, ls.at[14])
     keep_rows.start()
     for b in range(nb):
-        cot_far[2 * b].wait_recv()
-        cot_far[2 * b + 1].wait_recv()
+        for k, piece in enumerate(pieces):
+            if piece[0] == b:
+                cot_far[k].wait_recv()
         cot_pass[b].start()
 
     def finish(it, _):
@@ -773,7 +800,7 @@
             cp.wait()
 
 
-def run_k1(nd, tokens, w_time, fs, w_qkv, w_out, w_up, w_down, cs, sn, cot):
+def run_k1(nd, tokens, w_time, feats, w_qkv, w_out, w_up, w_down, cs, sn, cot):
     nb, tl, width = tokens.shape
     rows = 4 * tl
     cols = w_qkv.shape[1] // 3
@@ -788,6 +815,7 @@
         k1_body,
         out_shape=(
             sds((nb, 2 * width), F32),
+            sds((nb, TF), F32),
             sds((width, 3 * cols), BF),
             sds((width, width), BF),
             sds((width, hidden), BF),
@@ -803,8 +831,8 @@
             sds((4 * nb, tl, width), BF),
             sds((nb, tl, width), F32),
         ),
-        in_specs=[hb, vm, vm, hb, vm, vm, vm, hb, hb, hb],
-        out_specs=(vm, hb, hb, hb, hb, hb, hb, vm) + (hb,) * 7,
+        in_specs=[hb, vm, vm, vm, vm, vm, vm, hb, hb, hb],
+        out_specs=(vm, vm, hb, hb, hb, hb, hb, hb, vm) + (hb,) * 7,
         scratch_shapes=[
             v((nb, 4, tl, width), BF),
             v((nd,) + w_time.shape, BF),
@@ -837,7 +865,7 @@
             collective_id=0, has_side_effects=True, vmem_limit_bytes=VMEM_LIMIT
         ),
         name="attention_forward",
-    )(tokens, w_time, fs, w_qkv, w_out, w_up, w_down, cs, sn, cot)
+    )(tokens, w_time, feats, w_qkv, w_out, w_up, w_down, cs, sn, cot)
 
 
 def k2_body(
@@ -894,18 +922,18 @@
 
     down_ring = Scatter(view_down, down_h, down_w, gs, gr, 0)
 
-    def block(b, owner):
+    def back_part(b, owner):
         i = b * 4 + owner
         d_act = mm_nt(cot[b, owner], w_down[...])
         d_up = (d_act * dup[i].astype(F32)).astype(BF)
         dup[i] = d_up
-        return mm_nt(d_up, w_up[...]), mm(act[i], w_down[...])
-
-    def pair_copies(jp):
-        return (
-            remote(pa.at[jp], ra.at[jp], ss, rs, jp, (g, s1)),
-            remote(pb_.at[jp], rb.at[jp], ss, rs, 4 + jp, (g, s1)),
-        )
+        return mm_nt(d_up, w_up[...])
+
+    def back_copy(jp):
+        return remote(pa.at[jp], ra.at[jp], ss, rs, jp, (g, s1))
+
+    def out_copy(jp):
+        return remote(pb_.at[jp], rb.at[jp], ss, rs, 4 + jp, (g, s1))
 
     def far_copy(b):
         return remote(xs.at[b], xr.at[b], ss, rs, 8 + b, (g, s2))
@@ -922,11 +950,8 @@
             for cp in pull(jp, 0):
                 cp.wait()
 
-        dh, out = block(b, 2 * where + 1 - core)
-        pa[jp] = dh.astype(BF)
-        pb_[jp] = out.astype(BF)
-        for cp in pair_copies(jp):
-            cp.start()
+        pa[jp] = back_part(b, 2 * where + 1 - core).astype(BF)
+        back_copy(jp).start()
         return 0
 
     def take(jp, _):
@@ -937,21 +962,39 @@
             for cp in pull(jp, 1):
                 cp.wait()
 
-        dh, out = block(b, 2 * where + core)
-        for cp in pair_copies(jp):
-            cp.wait_recv()
+        dh = back_part(b, 2 * where + core)
+        back_copy(jp).wait_recv()
         dh = dh + ra[jp].astype(F32)
-        out = out + rb[jp].astype(F32)
 
         @pl.when(phase == 0)
         def _():
             xs[b] = dh.astype(BF)
-            osend[b] = out.astype(BF)
             far_copy(b).start()
 
         @pl.when(phase == 1)
         def _():
             d_mid[b] = dh
+
+        return 0
+
+    def give_out(jp, _):
+        _phase, b, where = place(jp)
+        pb_[jp] = mm(act[b * 4 + 2 * where + 1 - core], w_down[...]).astype(BF)
+        out_copy(jp).start()
+        return 0
+
+    def take_out(jp, _):
+        phase, b, where = place(jp)
+        out = mm(act[b * 4 + 2 * where + core], w_down[...])
+        out_copy(jp).wait_recv()
+        out = out + rb[jp].astype(F32)
+
+        @pl.when(phase == 0)
+        def _():
+            osend[b] = out.astype(BF)
+
+        @pl.when(phase == 1)
+        def _():
             base[b] = out + mids[b]
 
         return 0
@@ -1000,6 +1043,8 @@
     half = D // 512
     lax.fori_loop(0, nb, give, 0)
     lax.fori_loop(0, nb, take, 0)
+    lax.fori_loop(0, nb, give_out, 0)
+    lax.fori_loop(0, nb, take_out, 0)
     for jp in range(nb, 2 * nb):
         for which in (0, 1):
             for cp in pull(jp, which):
@@ -1012,8 +1057,10 @@
     lax.fori_loop(nb, 2 * nb, take, 0)
     down_ring.forward(2)
     lax.fori_loop(0, nb - 1, tail, 0)
+    lax.fori_loop(nb, 2 * nb, give_out, 0)
+    lax.fori_loop(nb, 2 * nb, take_out, 0)
+    down_ring.forward(3)
     lax.fori_loop(0, half, up_grads, 0)
-    down_ring.forward(3)
     lax.fori_loop(nb - 1, nb, tail, 0)
     lax.fori_loop(half, 2 * half, up_grads, 0)
     keep_all = []
@@ -1032,9 +1079,8 @@
         pltpu.make_async_copy(stage.at[j], grad_out.at[j], os_.at[j]).start()
 
     def done(jp, _):
-        ca, cb = pair_copies(jp)
-        ca.wait_send()
-        cb.wait_send()
+        back_copy(jp).wait_send()
+        out_copy(jp).wait_send()
         return 0
 
     lax.fori_loop(0, 2 * nb, done, 0)
@@ -1117,11 +1163,11 @@
 
 def k3_body(
     fields_h, lse, attn_h, d_heads_h, w_h, normed_h, tok_h, modul, cs_h, sn_h, d_mid_h, base_h, osend,
-    g_up, g_out, dsc_two, feats,
+    g_up, g_out, dsc_h, feats,
     output, grad_tok, s_qkv, s_out, s_up, s_time,
     orecv, dqt, draw, pa, ra, xs, xr, sumh, dhb,
     vu, vo, vq, oa, ob, ox, osum, up_h, up_w, out_h, out_w, qkv_h, qkv_w,
-    dpart, tx, dall, qkv, own, d_heads, w, normed_one, tok, cs, sn, d_mid, base,
+    dpart, tx, dall, qkv, own, d_heads, w, normed_one, tok, cs, sn, d_mid, base, dsc_two,
     ins, ls, ss, rs, gs, gr,
 ):
     g, s, core, s1, s2, s3 = peers()
@@ -1137,6 +1183,7 @@
         (
             (fields_h, qkv), (attn_h, own), (d_heads_h, d_heads), (cs_h, cs), (sn_h, sn),
             (w_h, w), (normed_h, normed_one), (tok_h, tok), (d_mid_h, d_mid), (base_h, base),
+            (dsc_h, dsc_two),
         )
     ):
         pulls.append(pltpu.make_async_copy(src, dst, ins.at[i]))
@@ -1146,7 +1193,8 @@
         cp.start()
     for cp in pulls[3:]:
         cp.start()
-    greet([(g, s1), (g, s2), (ring_index(p + 1), s), (ring_index(p - 1), s)])
+    others = [(lax.rem(g + d, nd), s) for d in range(1, nd)]
+    greet([(g, s1), (g, s2)] + others)
     nb, tl = tok.shape[0], tok.shape[1]
     rows, cols = own.shape[1], own.shape[2]
     heads = cols // HD
@@ -1172,16 +1220,10 @@
         return view
 
     up_ring = Scatter(view_rows(vu), up_h, up_w, gs, gr, 16)
-    def view_time(j, half):
-        wide = (2 * D + TF) // 2
-        ref = dall.at[j]
-        return ref if half is None else ref.at[:, half * wide : (half + 1) * wide]
-
     out_rings = [
         Scatter(view_cols(vo.at[i], vo.shape[1]), out_h.at[i], out_w.at[i], gs, gr, 8 * i)
         for i in range(2)
     ]
-    time_ring = Gather(dall.at[g], view_time, gs, gr, 32)
     def view_qkv(side):
         wide = vq.shape[1] // 2
 
@@ -1274,12 +1316,12 @@
         def keys_block(i, _):
             it = b * nk + i
             for when, act in (
-                (1, lambda: up_ring.forward(2)),
-                (2, lambda: out_forward(2)),
-                (3, lambda: up_ring.forward(3)),
-                (4, lambda: out_forward(3)),
-                (5, lambda: up_ring.forward(4)),
-                (6, lambda: out_forward(4)),
+                (2, lambda: up_ring.forward(2)),
+                (3, lambda: out_forward(2)),
+                (4, lambda: up_ring.forward(3)),
+                (5, lambda: out_forward(3)),
+                (6, lambda: up_ring.forward(4)),
+                (7, lambda: out_forward(4)),
             ):
 
                 @pl.when(it == when)
@@ -1327,25 +1369,23 @@
             )
             return res
 
+        for phase in range(2):
+            where = chip if phase else 1 - chip
+            pa[2 * b + phase] = part(2 * where + 1 - core).astype(BF)
+            near_copy(b, phase).start()
+        kept = part(2 * (1 - chip) + core)
+        near_copy(b, 0).wait_recv()
+        xs[b] = (kept + ra[2 * b].astype(F32)).astype(BF)
+        far_copy(b).start()
+
         @pl.when(b == nb - 1)
         def _():
             grads(0)
             grads(1)
 
-        for phase in range(2):
-            where = chip if phase else 1 - chip
-            pa[2 * b + phase] = part(2 * where + 1 - core).astype(BF)
-            near_copy(b, phase).start()
-        for phase in range(2):
-            where = chip if phase else 1 - chip
-            kept = part(2 * where + core)
-            near_copy(b, phase).wait_recv()
-            kept = kept + ra[2 * b + phase].astype(F32)
-            if phase == 0:
-                xs[b] = kept.astype(BF)
-                far_copy(b).start()
-            else:
-                sumh[b] = kept
+        kept = part(2 * chip + core)
+        near_copy(b, 1).wait_recv()
+        sumh[b] = kept + ra[2 * b + 1].astype(F32)
         return 0
 
     lax.fori_loop(0, nb, sequence, 0)
@@ -1358,15 +1398,16 @@
     over.start()
     qkv_forward(2)
     small[0].wait_recv()
-    dall[g, :, : 2 * D] = dpart[0] + dpart[1]
-    dall[g, :, 2 * D :] = feats[...]
-    time_ring.start()
+    dall[0, :, : 2 * D] = dpart[0] + dpart[1]
+    dall[0, :, 2 * D :] = feats[...]
+    wide = [remote(dall.at[0], dall.at[d], ss, rs, 12 + d, others[d - 1]) for d in range(1, nd)]
+    for cp in wide:
+        cp.start()
     for b in range(nb):
         back[b].wait_recv()
         output[b] = (base[b] + orecv[b].astype(F32)).astype(BF)
     s_up[...] = up_ring.result()
     qkv_forward(3)
-    time_ring.forward(2)
 
     def tail(b, _):
         scale = 1.0 + modul[pl.ds(b, 1), :D]
@@ -1382,12 +1423,11 @@
 
     lax.fori_loop(0, nb - 1, tail, 0)
     qkv_forward(4)
-    time_ring.forward(3)
-    time_ring.forward(4)
     lax.fori_loop(nb - 1, nb, tail, 0)
     over.wait_recv()
     s_out[...] = own_out + ox[...].astype(F32)
-    time_ring.arrive()
+    for cp in wide:
+        cp.wait_recv()
     depth = s_time.shape[0]
     lane_t = lax.broadcasted_iota(jnp.int32, (depth, TF), 1)
     row_t = lax.broadcasted_iota(jnp.int32, (depth, TF), 0)
@@ -1414,9 +1454,9 @@
         far_copy(b).wait_send()
         for phase in range(2):
             near_copy(b, phase).wait_send()
-    for cp in cross + small + [over, swap]:
+    for cp in cross + small + wide + [over, swap]:
         cp.wait_send()
-    for ring in out_rings + qkv_rings + [up_ring, time_ring]:
+    for ring in out_rings + qkv_rings + [up_ring]:
         ring.drain()
 
 
@@ -1443,7 +1483,7 @@
             sds((pc, hidden), F32),
             sds((TF // (4 * nd), 2 * width), F32),
         ),
-        in_specs=[hb, vm, hb, hb, hb, hb, hb, vm, hb, hb, hb, hb, hb, hb, hb, vm, vm],
+        in_specs=[hb, vm, hb, hb, hb, hb, hb, vm, hb, hb, hb, hb, hb, hb, hb, pl.BlockSpec(memory_space=pltpu.HBM), vm],
         out_specs=(vm,) * 6,
         scratch_shapes=[
             v((nb, tl, width), BF),
@@ -1481,15 +1521,16 @@
             v(sn.shape, F32),
             v(d_mid.shape, F32),
             v(base.shape, F32),
-            dma((10,)),
+            v(dsc_two.shape, F32),
+            dma((11,)),
             dma((2,)),
-            dma((13,)),
-            dma((13,)),
+            dma((20,)),
+            dma((20,)),
             dma((48,)),
             dma((48,)),
         ],
         compiler_params=pltpu.CompilerParams(
-            collective_id=2, has_side_effects=True, vmem_limit_bytes=VMEM_LIMIT
+            collective_id=2, has_side_effects=True, vmem_limit_bytes=52 * 1024 * 1024
         ),
         name="attention_backward",
     )(
@@ -1499,10 +1540,14 @@
 
 
 def k4_body(*refs):
+    *refs, sems = refs
     count = len(refs) // 2
-    for i in range(count):
-        if i != 2:
-            refs[count + i][...] = refs[i][...]
+    moves = []
+    for i in range(2):
+        moves.append(pltpu.make_async_copy(refs[i], refs[count + i], sems.at[i]))
+        moves[i].start()
+    for i in range(3, count):
+        refs[count + i][...] = refs[i][...]
     w = refs[2][...]
     heads = w.shape[1] // (3 * HD)
     half, size = HD // 2, heads * HD
@@ -1515,47 +1560,39 @@
         at = 2 * size + h * HD
         pieces.append(w[:, at : at + HD])
     refs[count + 2][...] = jnp.concatenate(pieces, axis=1)
+    for cp in moves:
+        cp.wait()
 
 
 def run_k4(arrays):
     vm = pl.BlockSpec(memory_space=pltpu.VMEM)
+    hb = pl.BlockSpec(memory_space=pltpu.HBM)
+    specs = [hb, hb] + [vm] * (len(arrays) - 2)
     return pl.pallas_call(
         k4_body,
         out_shape=tuple(jax.ShapeDtypeStruct(a.shape, a.dtype) for a in arrays),
-        in_specs=[vm] * len(arrays),
-        out_specs=(vm,) * len(arrays),
-        compiler_params=pltpu.CompilerParams(vmem_limit_bytes=VMEM_LIMIT),
+        in_specs=specs,
+        out_specs=tuple(specs),
+        scratch_shapes=[pltpu.SemaphoreType.DMA((2,))],
+        compiler_params=pltpu.CompilerParams(vmem_limit_bytes=16 * 1024 * 1024),
         name="results",
     )(*arrays)
 
 
-def order_columns(w):
-    rows = w.shape[0]
-    heads = w.shape[1] // (3 * HD)
-    w = w.reshape(rows, heads, 3, HD)
-    turned = w[:, :, 0:2].reshape(rows, heads, 2, 2, HD // 2)
-    turned = jnp.transpose(turned, (0, 2, 3, 1, 4)).reshape(rows, 2 * heads * HD)
-    return jnp.concatenate([turned, w[:, :, 2].reshape(rows, heads * HD)], axis=1)
-
-
 def fast_shards(nd, tokens, bins, plan, w_qkv, w_out, w_up, w_down, w_time, cotangent):
-    s = lax.axis_index("seq")
     nb, tl, width = tokens.shape
     rows = 4 * tl
     feats = time_features(plan, bins).astype(BF).astype(F32)
-    depth = w_time.shape[0]
-    table = feats.reshape(nb, nd, 4, depth)
-    fs = lax.dynamic_index_in_dim(table, s, axis=2, keepdims=False)[:, :, :, None]
     half = HD // 2
-    inverse = jnp.exp(jnp.arange(half, dtype=F32) * (-math.log(10000.0) / half))
-    angle = jnp.arange(rows, dtype=F32)[:, None] * inverse[None, :]
-    cs = jnp.tile(jnp.cos(angle), (1, 128 // half))
-    sn = jnp.tile(jnp.sin(angle), (1, 128 // half))
+    inverse = np.exp(np.arange(half, dtype=np.float32) * np.float32(-math.log(10000.0) / half))
+    angle = np.arange(rows, dtype=np.float32)[:, None] * inverse.astype(np.float32)[None, :]
+    cs = np.tile(np.cos(angle.astype(np.float64)).astype(np.float32), (1, 128 // half))
+    sn = np.tile(np.sin(angle.astype(np.float64)).astype(np.float32), (1, 128 // half))
     (
-        modul, full_qkv, full_out, full_up, full_down, normed, qkv, lse, attn_heads, attn_rows,
+        modul, feats, full_qkv, full_out, full_up, full_down, normed, qkv, lse, attn_heads, attn_rows,
         cot_all, act, slope, htwo, mid,
     ) = run_k1(
-        nd, tokens, w_time, fs, order_columns(w_qkv), w_out, w_up, w_down, cs, sn, cotangent
+        nd, tokens, w_time, feats, w_qkv, w_out, w_up, w_down, cs, sn, cotangent
     )
     grad_up, grad_out, d_mid, base, osend, d_heads, dsc_two, sum_down = run_k2(
         nd, act, slope, htwo, mid, attn_rows, cot_all, modul, full_out, full_up, full_down

time: 234 us -> 220 us (0.940)
  Pallas kernels: 227 us -> 214 us
    pallas_call x1, Pallas kernels: 74.4 us -> 67.5 us  [run_k3(): pl.pallas_call(k3_body, out_shape=(sds((nb, tl, width), BF), sds((nb, tl,...]
    unnamed x3 -> x16, local copies, waits for them, and re-layouts: 0.16 us -> 3.16 us
where the time goes in v3:
time: 220 us
  Pallas kernels  214 us (97%)
  local copies, waits for them, and re-layouts  3.16 us (1%)
    pallas_call x1, Pallas kernels, run_k1(): pl.pallas_call(k1_body, out_shape=(sds((nb, 2 * width), F32), sds((nb, TF...  91.8 us
    pallas_call x1, Pallas kernels, run_k3(): pl.pallas_call(k3_body, out_shape=(sds((nb, tl, width), BF), sds((nb, tl,...  67.5 us
    pallas_call x1, Pallas kernels, run_k2(): pl.pallas_call(k2_body, out_shape=(sds((width, hidden), BF), sds((4, cols...  52.4 us

profile of v3, /device:TPU:0, one launch (start us, length us, event | category | flops | bytes accessed | tf_op | source)
XLA Modules:
  0.0 219.8 jit_solution(18419349893051253842)
XLA Ops:
  0.6 0.9 fusion.2
  1.5 0.1 fusion
  1.6 0.6 maximum_convert_fusion.feats
  2.2 91.8 %attention_forward.1 = (f32[2,2048]{1,0:T(2,128)}, f32[2,256]{1,0:T(2,128)}, bf16[1024,768]{1,0:T(8,128)(2,1)}, bf16[1024,1024]{1,0:T(8,128)(2,1)}, bf16[1024,10...) custom-call(bf16[2,256,1024]{2,1,0:T(8,128)(2,1)} %tok_h.1, ...), custom_call_target="tpu_custom_call" | custom-call | tf_op jit(solution)/shard_map/attention_forward/pallas_call | solution.py:814
  94.0 0.0 copy-start
  94.0 0.0 copy-start.4
  94.0 0.0 copy-start.5
  94.0 0.0 copy-start.7
  94.0 52.4 %feed_forward.1 = (bf16[1024,1024]{1,0:T(8,128)(2,1)}, bf16[4,256,1024]{2,1,0:T(8,128)(2,1)}, f32[2,256,1024]{2,1,0:T(8,128)}, f32[2,256,1024]{2,1,0:T(8,128)}, ...) custom-call(bf16[8,256,1024]{2,1,0:T(8,128)(2,1)} %get-tuple-element., ...), custom_call_target="tpu_custom_call" | custom-call | tf_op jit(solution)/shard_map/feed_forward/pallas_call | solution.py:1109
  146.4 0.0 copy-done
  146.4 0.0 copy-done.4
  146.4 0.0 copy-done.5
  146.4 0.0 copy-done.7
  146.4 0.0 copy-start.6
  146.5 0.7 copy-done.6
  147.1 0.0 copy-start.3
  147.1 67.5 %attention_backward.1 = (bf16[2,256,1024]{2,1,0:T(8,128)(2,1)}, bf16[2,256,1024]{2,1,0:T(8,128)(2,1)}, f32[128,768]{1,0:T(8,128)S(1)}, f32[256,128]{1,0:T(8,128)...) custom-call(bf16[2,3,1024,256]{3,2,1,0:T(8,128)(2,1)} %get-tuple-element.37.fields_h, f32[2,8,1024]{2,1,0:T(8,128)S(1)} %copy-done.4, ...), custom_call_target="tpu_custom_call" | custom-call | tf_op jit(solution)/shard_map/attention_backward/pallas_call | solution.py:1476
  214.6 0.0 copy-done.3
  214.6 0.0 copy-start.1
  214.6 1.2 copy-done.1
  215.9 0.0 copy-start.2
  215.9 1.2 copy-done.2
  217.1 2.5 %results.1 = (bf16[2,256,1024]{2,1,0:T(8,128)(2,1)}, bf16[2,256,1024]{2,1,0:T(8,128)(2,1)}, f32[128,768]{1,0:T(8,128)}, f32[256,128]{1,0:T(8,128)}, f32[128,1024...) custom-call(bf16[2,256,1024]{2,1,0:T(8,128)(2,1)S(1)} %copy-done.1, bf16[2,256,1024]{2,1,0:T(8,128)(2,1)S(1)} %copy-done.2, ...), custom_call_target="tpu_custom_call" | custom-call | tf_op jit(solution)/shard_map/results/pallas_call | solution.py:1571
  (2 shorter events, 0.0 us)
Async XLA Ops:
  94.0 52.4 %copy-start = (f32[1024,128]{1,0:T(8,128)S(1)}, f32[1024,128]{1,0:T(8,128)}, u32[]{:S(2)}) copy-start(f32[1024,128]{1,0:T(8,128)} %constant.10.clone.cs.cs_h) | copy-start | bytes 1572868
  94.0 52.4 %copy-start.4 = (f32[2,8,1024]{2,1,0:T(8,128)S(1)}, f32[2,8,1024]{2,1,0:T(8,128)}, u32[]{:S(2)}) copy-start(f32[2,8,1024]{2,1,0:T(8,128)} %get-tuple-element.38.lse) | copy-start | bytes 196612
  94.0 52.4 %copy-start.5 = (f32[2,2048]{1,0:T(2,128)S(1)}, f32[2,2048]{1,0:T(2,128)}, u32[]{:S(2)}) copy-start(f32[2,2048]{1,0:T(2,128)} %get-tuple-element.46.modul) | copy-start | bytes 49156
  94.0 52.4 %copy-start.7 = (f32[2,256]{1,0:T(2,128)S(1)}, f32[2,256]{1,0:T(2,128)}, u32[]{:S(2)}) copy-start(f32[2,256]{1,0:T(2,128)} %get-tuple-element.59.feats) | copy-start | bytes 6148
  146.4 0.7 copy-start.6
  147.1 67.5 %copy-start.3 = (f32[1024,128]{1,0:T(8,128)S(1)}, f32[1024,128]{1,0:T(8,128)}, u32[]{:S(2)}) copy-start(f32[1024,128]{1,0:T(8,128)} %get-tuple-element.65.refs_5_) | copy-start | bytes 1572868
  214.6 1.2 copy-start.1
  215.9 1.2 copy-start.2

commit v4 on v3

--- a/solution.py
+++ b/solution.py
@@ -681,14 +681,23 @@
         r = pl.ds(pl.multiple_of(q * blk, blk), blk)
         query, keys = qkv[b, 0, r], qkv[b, 1]
         outs, stats = [], []
+        masked = jnp.concatenate(
+            [
+                jnp.where(lax.rem(lane, 128) // 32 == h, query, jnp.zeros_like(query))
+                for h in range(heads)
+            ],
+            axis=0,
+        )
+        both = mm_nt(keys, masked)
+        tops = jnp.max(both, axis=0, keepdims=True)
+        expo = jnp.exp2(both - tops)
+        totals = jnp.sum(expo, axis=0, keepdims=True)
+        expo = expo.astype(BF)
+        shares = 1.0 / totals
         for h in range(heads):
-            mask = lax.rem(lane, 128) // 32 == h
-            scores = mm_nt(keys, jnp.where(mask, query, jnp.zeros_like(query)))
-            top = jnp.max(scores, axis=0, keepdims=True)
-            expo = jnp.exp2(scores - top)
-            total = jnp.sum(expo, axis=0, keepdims=True)
-            outs.append(mm(vt[h * HD : (h + 1) * HD], expo.astype(BF)) * (1.0 / total))
-            stats.append(top + jnp.log2(total))
+            c = slice(h * blk, (h + 1) * blk)
+            outs.append(mm(vt[h * HD : (h + 1) * HD], expo[:, c]) * shares[:, c])
+            stats.append(tops[:, c] + jnp.log2(totals[:, c]))
         attn[b, s, r] = jnp.concatenate(outs, axis=0).T.astype(BF)
         lse[b, :, r] = jnp.concatenate(stats + [jnp.zeros((8 - heads, blk), F32)], axis=0)
         attn_copy(0, it).start()

time: 220 us -> 217 us (0.986)
  Pallas kernels: 214 us -> 211 us
    pallas_call x1, Pallas kernels: 91.8 us -> 89.5 us  [run_k1(): pl.pallas_call(k1_body, out_shape=(sds((nb, 2 * width), F32), sds((nb, TF...]
where the time goes in v4:
time: 217 us
  Pallas kernels  211 us (97%)
  local copies, waits for them, and re-layouts  3.16 us (1%)
    pallas_call x1, Pallas kernels, run_k1(): pl.pallas_call(k1_body, out_shape=(sds((nb, 2 * width), F32), sds((nb, TF...  89.5 us
    pallas_call x1, Pallas kernels, run_k3(): pl.pallas_call(k3_body, out_shape=(sds((nb, tl, width), BF), sds((nb, tl,...  67.5 us
    pallas_call x1, Pallas kernels, run_k2(): pl.pallas_call(k2_body, out_shape=(sds((width, hidden), BF), sds((4, cols...  51.7 us

profile of v4, /device:TPU:0, one launch (start us, length us, event | category | flops | bytes accessed | tf_op | source)
XLA Modules:
  0.0 216.9 jit_solution(10450745147449388388)
XLA Ops:
  0.6 0.9 fusion.2
  1.5 0.1 fusion
  1.6 0.6 maximum_convert_fusion.feats
  2.2 89.5 %attention_forward.1 = (f32[2,2048]{1,0:T(2,128)}, f32[2,256]{1,0:T(2,128)}, bf16[1024,768]{1,0:T(8,128)(2,1)}, bf16[1024,1024]{1,0:T(8,128)(2,1)}, bf16[1024,10...) custom-call(bf16[2,256,1024]{2,1,0:T(8,128)(2,1)} %tok_h.1, ...), custom_call_target="tpu_custom_call" | custom-call | tf_op jit(solution)/shard_map/attention_forward/pallas_call | solution.py:823
  91.7 0.0 copy-start
  91.7 0.0 copy-start.4
  91.7 0.0 copy-start.5
  91.7 0.0 copy-start.7
  91.7 51.7 %feed_forward.1 = (bf16[1024,1024]{1,0:T(8,128)(2,1)}, bf16[4,256,1024]{2,1,0:T(8,128)(2,1)}, f32[2,256,1024]{2,1,0:T(8,128)}, f32[2,256,1024]{2,1,0:T(8,128)}, ...) custom-call(bf16[8,256,1024]{2,1,0:T(8,128)(2,1)} %get-tuple-element., ...), custom_call_target="tpu_custom_call" | custom-call | tf_op jit(solution)/shard_map/feed_forward/pallas_call | solution.py:1118
  143.5 0.0 copy-done
  143.5 0.0 copy-done.4
  143.5 0.0 copy-done.5
  143.5 0.0 copy-done.7
  143.5 0.0 copy-start.6
  143.5 0.7 copy-done.6
  144.2 0.0 copy-start.3
  144.2 67.5 %attention_backward.1 = (bf16[2,256,1024]{2,1,0:T(8,128)(2,1)}, bf16[2,256,1024]{2,1,0:T(8,128)(2,1)}, f32[128,768]{1,0:T(8,128)S(1)}, f32[256,128]{1,0:T(8,128)...) custom-call(bf16[2,3,1024,256]{3,2,1,0:T(8,128)(2,1)} %get-tuple-element.37.fields_h, f32[2,8,1024]{2,1,0:T(8,128)S(1)} %copy-done.4, ...), custom_call_target="tpu_custom_call" | custom-call | tf_op jit(solution)/shard_map/attention_backward/pallas_call | solution.py:1485
  211.7 0.0 copy-done.3
  211.8 0.0 copy-start.1
  211.8 1.2 copy-done.1
  213.0 0.0 copy-start.2
  213.0 1.2 copy-done.2
  214.2 2.5 %results.1 = (bf16[2,256,1024]{2,1,0:T(8,128)(2,1)}, bf16[2,256,1024]{2,1,0:T(8,128)(2,1)}, f32[128,768]{1,0:T(8,128)}, f32[256,128]{1,0:T(8,128)}, f32[128,1024...) custom-call(bf16[2,256,1024]{2,1,0:T(8,128)(2,1)S(1)} %copy-done.1, bf16[2,256,1024]{2,1,0:T(8,128)(2,1)S(1)} %copy-done.2, ...), custom_call_target="tpu_custom_call" | custom-call | tf_op jit(solution)/shard_map/results/pallas_call | solution.py:1580
  (2 shorter events, 0.0 us)
Async XLA Ops:
  91.7 51.8 %copy-start = (f32[1024,128]{1,0:T(8,128)S(1)}, f32[1024,128]{1,0:T(8,128)}, u32[]{:S(2)}) copy-start(f32[1024,128]{1,0:T(8,128)} %constant.10.clone.cs.cs_h) | copy-start | bytes 1572868
  91.7 51.8 %copy-start.4 = (f32[2,8,1024]{2,1,0:T(8,128)S(1)}, f32[2,8,1024]{2,1,0:T(8,128)}, u32[]{:S(2)}) copy-start(f32[2,8,1024]{2,1,0:T(8,128)} %get-tuple-element.38.lse) | copy-start | bytes 196612
  91.7 51.8 %copy-start.5 = (f32[2,2048]{1,0:T(2,128)S(1)}, f32[2,2048]{1,0:T(2,128)}, u32[]{:S(2)}) copy-start(f32[2,2048]{1,0:T(2,128)} %get-tuple-element.46.modul) | copy-start | bytes 49156
  91.7 51.8 %copy-start.7 = (f32[2,256]{1,0:T(2,128)S(1)}, f32[2,256]{1,0:T(2,128)}, u32[]{:S(2)}) copy-start(f32[2,256]{1,0:T(2,128)} %get-tuple-element.59.feats) | copy-start | bytes 6148
  143.5 0.7 copy-start.6
  144.2 67.5 %copy-start.3 = (f32[1024,128]{1,0:T(8,128)S(1)}, f32[1024,128]{1,0:T(8,128)}, u32[]{:S(2)}) copy-start(f32[1024,128]{1,0:T(8,128)} %get-tuple-element.65.refs_5_) | copy-start | bytes 1572868
  211.8 1.2 copy-start.1
  213.0 1.2 copy-start.2

commit v5 on v4

--- a/solution.py
+++ b/solution.py
@@ -914,13 +914,6 @@
     for cp in first:
         cp.start()
     loads[1].start()
-    for jp in range(2 * nb):
-        for which in (0, 1):
-            if jp + which:
-                for cp in pull(jp, which):
-                    cp.start()
-    for cp in loads[2:]:
-        cp.start()
     greet([(g, s1), (g, s2), (g, s3), (ring_index(p + 1), s), (ring_index(p - 1), s)])
     hidden = act.shape[2]
     pc = s_down.shape[1]
@@ -1047,10 +1040,21 @@
             spread(e, other, b).start()
         return 0
 
+    for which in (0, 1):
+        for jp in range(nb):
+            if jp + which:
+                for cp in pull(jp, which):
+                    cp.start()
     for cp in loads[:2]:
         cp.wait()
     half = D // 512
     lax.fori_loop(0, nb, give, 0)
+    for jp in range(nb, 2 * nb):
+        for which in (0, 1):
+            for cp in pull(jp, which):
+                cp.start()
+    for cp in loads[2:]:
+        cp.start()
     lax.fori_loop(0, nb, take, 0)
     lax.fori_loop(0, nb, give_out, 0)
     lax.fori_loop(0, nb, take_out, 0)

time: 217 us -> 214 us (0.986)
  Pallas kernels: 211 us -> 208 us
    pallas_call x1, Pallas kernels: 51.7 us -> 49 us  [run_k2(): pl.pallas_call(k2_body, out_shape=(sds((width, hidden), BF), sds((4, cols...]
where the time goes in v5:
time: 214 us
  Pallas kernels  208 us (97%)
  local copies, waits for them, and re-layouts  3.16 us (1%)
    pallas_call x1, Pallas kernels, run_k1(): pl.pallas_call(k1_body, out_shape=(sds((nb, 2 * width), F32), sds((nb, TF...  89.5 us
    pallas_call x1, Pallas kernels, run_k3(): pl.pallas_call(k3_body, out_shape=(sds((nb, tl, width), BF), sds((nb, tl,...  67.5 us
    pallas_call x1, Pallas kernels, run_k2(): pl.pallas_call(k2_body, out_shape=(sds((width, hidden), BF), sds((4, cols...  49 us

profile of v5, /device:TPU:0, one launch (start us, length us, event | category | flops | bytes accessed | tf_op | source)
XLA Modules:
  0.0 214.1 jit_solution(5769489196367988370)
XLA Ops:
  0.6 0.9 fusion.2
  1.5 0.1 fusion
  1.6 0.6 maximum_convert_fusion.feats
  2.2 89.5 %attention_forward.1 = (f32[2,2048]{1,0:T(2,128)}, f32[2,256]{1,0:T(2,128)}, bf16[1024,768]{1,0:T(8,128)(2,1)}, bf16[1024,1024]{1,0:T(8,128)(2,1)}, bf16[1024,10...) custom-call(bf16[2,256,1024]{2,1,0:T(8,128)(2,1)} %tok_h.1, ...), custom_call_target="tpu_custom_call" | custom-call | tf_op jit(solution)/shard_map/attention_forward/pallas_call | solution.py:823
  91.7 0.0 copy-start
  91.7 0.0 copy-start.4
  91.7 0.0 copy-start.5
  91.7 0.0 copy-start.7
  91.7 49.0 %feed_forward.1 = (bf16[1024,1024]{1,0:T(8,128)(2,1)}, bf16[4,256,1024]{2,1,0:T(8,128)(2,1)}, f32[2,256,1024]{2,1,0:T(8,128)}, f32[2,256,1024]{2,1,0:T(8,128)}, ...) custom-call(bf16[8,256,1024]{2,1,0:T(8,128)(2,1)} %get-tuple-element., ...), custom_call_target="tpu_custom_call" | custom-call | tf_op jit(solution)/shard_map/feed_forward/pallas_call | solution.py:1122
  140.7 0.0 copy-done
  140.7 0.0 copy-done.4
  140.7 0.0 copy-done.5
  140.8 0.0 copy-done.7
  140.8 0.0 copy-start.6
  140.8 0.7 copy-done.6
  141.5 0.0 copy-start.3
  141.5 67.5 %attention_backward.1 = (bf16[2,256,1024]{2,1,0:T(8,128)(2,1)}, bf16[2,256,1024]{2,1,0:T(8,128)(2,1)}, f32[128,768]{1,0:T(8,128)S(1)}, f32[256,128]{1,0:T(8,128)...) custom-call(bf16[2,3,1024,256]{3,2,1,0:T(8,128)(2,1)} %get-tuple-element.37.fields_h, f32[2,8,1024]{2,1,0:T(8,128)S(1)} %copy-done.4, ...), custom_call_target="tpu_custom_call" | custom-call | tf_op jit(solution)/shard_map/attention_backward/pallas_call | solution.py:1489
  209.0 0.0 copy-done.3
  209.0 0.0 copy-start.1
  209.0 1.2 copy-done.1
  210.2 0.0 copy-start.2
  210.2 1.2 copy-done.2
  211.4 2.5 %results.1 = (bf16[2,256,1024]{2,1,0:T(8,128)(2,1)}, bf16[2,256,1024]{2,1,0:T(8,128)(2,1)}, f32[128,768]{1,0:T(8,128)}, f32[256,128]{1,0:T(8,128)}, f32[128,1024...) custom-call(bf16[2,256,1024]{2,1,0:T(8,128)(2,1)S(1)} %copy-done.1, bf16[2,256,1024]{2,1,0:T(8,128)(2,1)S(1)} %copy-done.2, ...), custom_call_target="tpu_custom_call" | custom-call | tf_op jit(solution)/shard_map/results/pallas_call | solution.py:1584
  (2 shorter events, 0.0 us)
Async XLA Ops:
  91.7 49.0 %copy-start = (f32[1024,128]{1,0:T(8,128)S(1)}, f32[1024,128]{1,0:T(8,128)}, u32[]{:S(2)}) copy-start(f32[1024,128]{1,0:T(8,128)} %constant.10.clone.cs.cs_h) | copy-start | bytes 1572868
  91.7 49.0 %copy-start.4 = (f32[2,8,1024]{2,1,0:T(8,128)S(1)}, f32[2,8,1024]{2,1,0:T(8,128)}, u32[]{:S(2)}) copy-start(f32[2,8,1024]{2,1,0:T(8,128)} %get-tuple-element.38.lse) | copy-start | bytes 196612
  91.7 49.0 %copy-start.5 = (f32[2,2048]{1,0:T(2,128)S(1)}, f32[2,2048]{1,0:T(2,128)}, u32[]{:S(2)}) copy-start(f32[2,2048]{1,0:T(2,128)} %get-tuple-element.46.modul) | copy-start | bytes 49156
  91.7 49.0 %copy-start.7 = (f32[2,256]{1,0:T(2,128)S(1)}, f32[2,256]{1,0:T(2,128)}, u32[]{:S(2)}) copy-start(f32[2,256]{1,0:T(2,128)} %get-tuple-element.59.feats) | copy-start | bytes 6148
  140.8 0.7 copy-start.6
  141.5 67.5 %copy-start.3 = (f32[1024,128]{1,0:T(8,128)S(1)}, f32[1024,128]{1,0:T(8,128)}, u32[]{:S(2)}) copy-start(f32[1024,128]{1,0:T(8,128)} %get-tuple-element.65.refs_5_) | copy-start | bytes 1572868
  209.0 1.2 copy-start.1
  210.2 1.2 copy-start.2

commit v6 on v5

--- a/solution.py
+++ b/solution.py
@@ -1194,17 +1194,18 @@
     pulls = []
     for i, (src, dst) in enumerate(
         (
-            (fields_h, qkv), (attn_h, own), (d_heads_h, d_heads), (cs_h, cs), (sn_h, sn),
+            (fields_h.at[0], qkv.at[0]), (d_heads_h.at[:, 0], d_heads.at[:, 0]),
+            (attn_h.at[0], own.at[0]), (cs_h, cs), (sn_h, sn),
+            (fields_h.at[1], qkv.at[1]), (d_heads_h.at[:, 1], d_heads.at[:, 1]),
+            (attn_h.at[1], own.at[1]),
             (w_h, w), (normed_h, normed_one), (tok_h, tok), (d_mid_h, d_mid), (base_h, base),
             (dsc_h, dsc_two),
         )
     ):
         pulls.append(pltpu.make_async_copy(src, dst, ins.at[i]))
-    for cp in pulls[:3]:
+    for cp in pulls[:5]:
         cp.start()
     for cp in loads:
-        cp.start()
-    for cp in pulls[3:]:
         cp.start()
     others = [(lax.rem(g + d, nd), s) for d in range(1, nd)]
     greet([(g, s1), (g, s2)] + others)
@@ -1292,7 +1293,8 @@
 
     for cp in pulls[:5]:
         cp.wait()
-    out_pair()
+    for cp in pulls[5:]:
+        cp.start()
 
     def grads(side):
         wide = vq.shape[1] // 2
@@ -1314,6 +1316,11 @@
         qkv_rings[side].start()
 
     def sequence(b, _):
+        @pl.when(b == 1)
+        def _():
+            for cp in pulls[5:8]:
+                cp.wait()
+
         for j in range(4):
             dhb[j * tl : (j + 1) * tl] = d_heads[j, b]
         query = qkv[b, 0]
@@ -1329,6 +1336,7 @@
         def keys_block(i, _):
             it = b * nk + i
             for when, act in (
+                (1, out_pair),
                 (2, lambda: up_ring.forward(2)),
                 (3, lambda: out_forward(2)),
                 (4, lambda: up_ring.forward(3)),
@@ -1370,7 +1378,7 @@
 
         @pl.when(b == 0)
         def _():
-            for cp in pulls[5:]:
+            for cp in pulls[8:]:
                 cp.wait()
             dpart[0, :, :D] = jnp.zeros((nb, D), F32)
 
@@ -1535,7 +1543,7 @@
             v(d_mid.shape, F32),
             v(base.shape, F32),
             v(dsc_two.shape, F32),
-            dma((11,)),
+            dma((14,)),
             dma((2,)),
             dma((20,)),
             dma((20,)),

time: 214 us -> 212 us (level)
    pallas_call x1, Pallas kernels: 67.5 us -> 64.8 us  [run_k3(): pl.pallas_call(k3_body, out_shape=(sds((nb, tl, width), BF), sds((nb, tl,...]
where the time goes in v6:
time: 212 us; the launch traced here: 211 us
  Pallas kernels  206 us (97%)
  local copies, waits for them, and re-layouts  3.16 us (1%)
    pallas_call x1, Pallas kernels, run_k1(): pl.pallas_call(k1_body, out_shape=(sds((nb, 2 * width), F32), sds((nb, TF...  89.5 us
    pallas_call x1, Pallas kernels, run_k3(): pl.pallas_call(k3_body, out_shape=(sds((nb, tl, width), BF), sds((nb, tl,...  64.8 us
    pallas_call x1, Pallas kernels, run_k2(): pl.pallas_call(k2_body, out_shape=(sds((width, hidden), BF), sds((4, cols...  49 us

profile of v6, /device:TPU:0, one launch (start us, length us, event | category | flops | bytes accessed | tf_op | source)
XLA Modules:
  0.0 211.4 jit_solution(14858748217515929313)
XLA Ops:
  0.6 0.9 fusion.2
  1.5 0.1 fusion
  1.6 0.6 maximum_convert_fusion.feats
  2.2 89.5 %attention_forward.1 = (f32[2,2048]{1,0:T(2,128)}, f32[2,256]{1,0:T(2,128)}, bf16[1024,768]{1,0:T(8,128)(2,1)}, bf16[1024,1024]{1,0:T(8,128)(2,1)}, bf16[1024,10...) custom-call(bf16[2,256,1024]{2,1,0:T(8,128)(2,1)} %tok_h.1, ...), custom_call_target="tpu_custom_call" | custom-call | tf_op jit(solution)/shard_map/attention_forward/pallas_call | solution.py:823
  91.7 0.0 copy-start
  91.7 0.0 copy-start.4
  91.7 0.0 copy-start.5
  91.7 0.0 copy-start.7
  91.7 49.0 %feed_forward.1 = (bf16[1024,1024]{1,0:T(8,128)(2,1)}, bf16[4,256,1024]{2,1,0:T(8,128)(2,1)}, f32[2,256,1024]{2,1,0:T(8,128)}, f32[2,256,1024]{2,1,0:T(8,128)}, ...) custom-call(bf16[8,256,1024]{2,1,0:T(8,128)(2,1)} %get-tuple-element., ...), custom_call_target="tpu_custom_call" | custom-call | tf_op jit(solution)/shard_map/feed_forward/pallas_call | solution.py:1122
  140.7 0.0 copy-done
  140.7 0.0 copy-done.4
  140.7 0.0 copy-done.5
  140.8 0.0 copy-done.7
  140.8 0.0 copy-start.6
  140.8 0.7 copy-done.6
  141.5 0.0 copy-start.3
  141.5 64.8 %attention_backward.1 = (bf16[2,256,1024]{2,1,0:T(8,128)(2,1)}, bf16[2,256,1024]{2,1,0:T(8,128)(2,1)}, f32[128,768]{1,0:T(8,128)S(1)}, f32[256,128]{1,0:T(8,128)...) custom-call(bf16[2,3,1024,256]{3,2,1,0:T(8,128)(2,1)} %get-tuple-element.37.fields_h, f32[2,8,1024]{2,1,0:T(8,128)S(1)} %copy-done.4, ...), custom_call_target="tpu_custom_call" | custom-call | tf_op jit(solution)/shard_map/attention_backward/pallas_call | solution.py:1497
  206.2 0.0 copy-done.3
  206.2 0.0 copy-start.1
  206.2 1.2 copy-done.1
  207.5 0.0 copy-start.2
  207.5 1.2 copy-done.2
  208.7 2.5 %results.1 = (bf16[2,256,1024]{2,1,0:T(8,128)(2,1)}, bf16[2,256,1024]{2,1,0:T(8,128)(2,1)}, f32[128,768]{1,0:T(8,128)}, f32[256,128]{1,0:T(8,128)}, f32[128,1024...) custom-call(bf16[2,256,1024]{2,1,0:T(8,128)(2,1)S(1)} %copy-done.1, bf16[2,256,1024]{2,1,0:T(8,128)(2,1)S(1)} %copy-done.2, ...), custom_call_target="tpu_custom_call" | custom-call | tf_op jit(solution)/shard_map/results/pallas_call | solution.py:1592
  (2 shorter events, 0.0 us)
Async XLA Ops:
  91.7 49.0 %copy-start = (f32[1024,128]{1,0:T(8,128)S(1)}, f32[1024,128]{1,0:T(8,128)}, u32[]{:S(2)}) copy-start(f32[1024,128]{1,0:T(8,128)} %constant.10.clone.cs.cs_h) | copy-start | bytes 1572868
  91.7 49.0 %copy-start.4 = (f32[2,8,1024]{2,1,0:T(8,128)S(1)}, f32[2,8,1024]{2,1,0:T(8,128)}, u32[]{:S(2)}) copy-start(f32[2,8,1024]{2,1,0:T(8,128)} %get-tuple-element.38.lse) | copy-start | bytes 196612
  91.7 49.0 %copy-start.5 = (f32[2,2048]{1,0:T(2,128)S(1)}, f32[2,2048]{1,0:T(2,128)}, u32[]{:S(2)}) copy-start(f32[2,2048]{1,0:T(2,128)} %get-tuple-element.46.modul) | copy-start | bytes 49156
  91.7 49.0 %copy-start.7 = (f32[2,256]{1,0:T(2,128)S(1)}, f32[2,256]{1,0:T(2,128)}, u32[]{:S(2)}) copy-start(f32[2,256]{1,0:T(2,128)} %get-tuple-element.59.feats) | copy-start | bytes 6148
  140.8 0.7 copy-start.6
  141.5 64.8 %copy-start.3 = (f32[1024,128]{1,0:T(8,128)S(1)}, f32[1024,128]{1,0:T(8,128)}, u32[]{:S(2)}) copy-start(f32[1024,128]{1,0:T(8,128)} %get-tuple-element.65.refs_5_) | copy-start | bytes 1572868
  206.2 1.2 copy-start.1
  207.5 1.2 copy-start.2
